TPU v7x, 32 devices: a whole 2x2x4 slice. The times are simulated.
32 devices in a mesh: groups: 2 (over x), gx: 16 (over z, y, core).
Axes of the slice: x: 2, y: 2, z: 4, core: 2. Of those that a mesh axis runs over, the one named last changes fastest.
Arguments:
- input_tiles: bfloat16 [16, 512, 1024], P('gx', 'groups'), parts along dimension 1, may hold values from -6 to 6
- grad_tiles: bfloat16 [16, 512, 1024], P('gx', 'groups'), parts along dimension 1, may hold values from -0.59765625 to 0.59765625
- context_tiles: bfloat16 [16, 128, 4096], P('gx', 'groups'), parts along dimension 1, may hold values from -6 to 6
- up_tiles: bfloat16 [16, 1024, 8192], P('gx'), may hold values from -0.0625 to 0.0625
- down_tiles: bfloat16 [16, 8192, 1024], P('gx'), may hold values from -0.046875 to 0.046875
- output_tiles: bfloat16 [16, 4096, 1024], P('gx'), may hold values from -0.0625 to 0.0625
Outputs:
- d_input: bfloat16 [16, 512, 1024], P('gx', 'groups'), parts along dimension 1
- d_context: bfloat16 [16, 128, 4096], P('gx', 'groups'), parts along dimension 1
- d_up: bfloat16 [16, 2048, 8192], P('gx', 'groups'), parts along dimension 1
- d_down: bfloat16 [16, 16384, 1024], P('gx', 'groups'), parts along dimension 1
- d_output: bfloat16 [16, 8192, 1024], P('gx', 'groups'), parts along dimension 1
There are 2 independent parts, one for each index of `groups`. A program takes and returns all parts, laid end to end along the dimension named above; an argument that names none is the same for every part. Nothing has to cross between parts.
All inputs are finite; a program needn't handle non-finite values.
Results may differ from a plain program's by a relative error of at most 0.0052.
Values may be sent and summed in bfloat16 or wider, within the bound.
No kernel may reach another device: no remote copies, remote signals or barrier semaphores. Data moves between devices by JAX's collectives and lax.ppermute only.
A program may use at most 256 MiB of HBM per device.

v0:
```python
import jax
import jax.numpy as jnp
from jax import lax
from jax.sharding import PartitionSpec as P

PBITS = 3


def swapped(block, axis, stride):
    count = lax.axis_size(axis)
    route = []
    for low in range(count):
        high = low | 1 << stride
        if high != low and high < count:
            route += [(low, high), (high, low)]
    return lax.ppermute(block, axis, route)


def gelu_tanh(value):
    return jax.nn.gelu(value, approximate=True)


def contract(left, right, left_dim, right_dim):
    return lax.dot_general(
        left, right, (((left_dim,), (right_dim,)), ((), ())), preferred_element_type=jnp.float32
    )


def bit_clear(grid_index, bit):
    return jnp.bitwise_and(jnp.right_shift(grid_index, bit), 1) == 0


def group_gather(value, dim, bits, trade, grid_index):
    for bit in bits:
        other = trade(value, bit)
        lower = bit_clear(grid_index, bit)
        first = jnp.where(lower, value, other)
        second = jnp.where(lower, other, value)
        value = jnp.concatenate([first, second], axis=dim)
    return value


def group_scatter(value, dim, bits, trade, grid_index):
    for bit in reversed(bits):
        half = value.shape[dim] // 2
        first = lax.slice_in_dim(value, 0, half, axis=dim)
        second = lax.slice_in_dim(value, half, 2 * half, axis=dim)
        lower = bit_clear(grid_index, bit)
        keep = jnp.where(lower, first, second)
        sent = jnp.where(lower, second, first)
        value = keep + trade(sent, bit)
    return value


def body(input_tiles, grad_tiles, context_tiles, up_tiles, down_tiles, output_tiles):
    grid_index = lax.axis_index("gx")
    total_bits = lax.axis_size("gx").bit_length() - 1
    row_bits = list(range(PBITS))
    col_bits = list(range(PBITS, total_bits))
    inputs = input_tiles[0]
    grads = grad_tiles[0]
    up_block = up_tiles[0]
    down_block = down_tiles[0]
    proj_block = output_tiles[0]
    paired = jnp.stack([inputs, grads])
    paired_rows = group_gather(
        paired, 1, col_bits, lambda value, bit: swapped(value, "gx", bit), grid_index
    )
    input_rows = paired_rows[0]
    grad_rows = paired_rows[1]
    pre_part = jnp.dot(input_rows, up_block, preferred_element_type=jnp.float32)
    hidden_part = contract(grad_rows, down_block, 1, 1)
    stacked = jnp.stack([pre_part, hidden_part])
    shares = group_scatter(
        stacked, 1, row_bits, lambda value, bit: swapped(value, "gx", bit), grid_index
    )
    act_share, gelu_back = jax.vjp(gelu_tanh, shares[0])
    dpre_share = gelu_back(shares[1])[0].astype(jnp.bfloat16)
    both = jnp.stack([act_share.astype(jnp.bfloat16), dpre_share])
    both_rows = group_gather(
        both, 1, row_bits, lambda value, bit: swapped(value, "gx", bit), grid_index
    )
    act_rows = both_rows[0]
    dpre_rows = both_rows[1]
    d_down = contract(act_rows, grad_rows, 0, 0).astype(jnp.bfloat16)
    d_up = contract(input_rows, dpre_rows, 0, 0).astype(jnp.bfloat16)
    input_part = contract(dpre_rows, up_block, 1, 1)
    input_share = group_scatter(
        input_part, 0, col_bits, lambda value, bit: swapped(value, "gx", bit), grid_index
    )
    d_input = (grads.astype(jnp.float32) + input_share).astype(jnp.bfloat16)
    dinput_rows = group_gather(
        d_input, 0, col_bits, lambda value, bit: swapped(value, "gx", bit), grid_index
    )
    context_rows = group_gather(
        context_tiles[0], 0, row_bits, lambda value, bit: swapped(value, "gx", bit), grid_index
    )
    d_output = contract(context_rows, dinput_rows, 0, 0).astype(jnp.bfloat16)
    context_part = contract(dinput_rows, proj_block, 1, 1)
    d_context = group_scatter(
        context_part, 0, row_bits, lambda value, bit: swapped(value, "gx", bit), grid_index
    ).astype(jnp.bfloat16)
    return (d_input[None], d_context[None], d_up[None], d_down[None], d_output[None])


def solution(mesh):
    return jax.shard_map(
        body,
        mesh=mesh,
        in_specs=(
            P("gx", "groups", None),
            P("gx", "groups", None),
            P("gx", "groups", None),
            P("gx", None, None),
            P("gx", None, None),
            P("gx", None, None),
        ),
        out_specs=(
            P("gx", "groups", None),
            P("gx", "groups", None),
            P("gx", "groups", None),
            P("gx", "groups", None),
            P("gx", "groups", None),
        ),
        check_vma=False,
    )
```

profile of v0, /device:TPU:0, one launch (start us, length us, event | category | flops | bytes accessed | tf_op | source)
XLA Modules:
  0.0 1285.0 jit_solution(16303507232616403271)
XLA Ops:
  2.8 4.1 collective-permute-start
  6.9 45.7 %collective-permute-done = bf16[2,256,1024]{2,1,0:T(8,128)(2,1)} collective-permute-done((bf16[2,256,1024]{2,1,0:T(8,128)(2,1)S(1)}, bf16[2,256,1024]{2,1,0:T(8,128)(2,1)}, u32[]{:S(2)}, u32[]{:S(2)}) %collective-permute-start) | collective-permute-done | bytes 1048608 | tf_op jit(solution)/shard_map/ppermute | solution.py:16
  54.0 16.6 %fusion.7 = f32[1,512,8192]{2,1,0:T(8,128)} fusion(bf16[1,1024,8192]{2,1,0:T(8,128)(2,1)} %param.9, bf16[2,256,1024]{2,1,0:T(8,128)(2,1)S(1)} %get-tuple-element.17, bf16[2,256,1024]{2,1,0:T(8,128)(2,1)S(1)} %get-tuple-element.18), kind=kOutput, calls=%fused_computation.15 | convolution fusion | flops 8592031744 | bytes 35651584 | tf_op jit(solution)/shard_map/dot_general | solution.py:71
  70.6 15.9 %fusion.10 = f32[1,512,8192]{2,1,0:T(8,128)} fusion(bf16[1,8192,1024]{2,1,0:T(8,128)(2,1)} %param.10, bf16[2,256,1024]{2,1,0:T(8,128)(2,1)S(1)} %get-tuple-element.18, bf16[2,256,1024]{2,1,0:T(8,128)(2,1)S(1)} %get-tuple-element.17), kind=kOutput, calls=%fused_computation.16 | convolution fusion | flops 8592031744 | bytes 35651584 | tf_op jit(solution)/shard_map/dot_general | solution.py:24
  86.5 17.9 %broadcast_select_fusion.2 = f32[2,256,8192]{2,1,0:T(8,128)} fusion(pred[]{:T(512)S(6)} %eq.9, f32[1,512,8192]{2,1,0:T(8,128)} %fusion.10, f32[1,512,8192]{2,1,0:T(8,128)} %fusion.7), kind=kLoop, calls=%fused_computation.29 | loop fusion | flops 12582912 | bytes 50331648 | tf_op jit(solution)/shard_map/jit(_where)/select_n | solution.py:50
  104.9 361.1 %collective-permute-done.1 = f32[2,256,8192]{2,1,0:T(8,128)} collective-permute-done((f32[2,256,8192]{2,1,0:T(8,128)}, f32[2,256,8192]{2,1,0:T(8,128)}, u32[]{:S(2)}, u32[]{:S(2)}) %collective-permute-start.1) | collective-permute-done | bytes 16777248 | tf_op jit(solution)/shard_map/ppermute | solution.py:16
  466.1 22.8 %select_add_fusion = f32[2,256,8192]{2,1,0:T(8,128)} fusion(f32[2,256,8192]{2,1,0:T(8,128)} %collective-permute-done.1, pred[]{:T(512)S(6)} %eq.9, f32[1,512,8192]{2,1,0:T(8,128)} %fusion.10, f32[1,512,8192]{2,1,0:T(8,128)} %fusion.7), kind=kLoop, calls=%fused_computation.14 | loop fusion | flops 16777216 | bytes 67108864 | tf_op jit(solution)/shard_map/add | solution.py:51
  488.8 10.5 slice_select_fusion
  500.6 179.8 %collective-permute-done.2 = f32[2,128,8192]{2,1,0:T(8,128)} collective-permute-done((f32[2,128,8192]{2,1,0:T(8,128)}, f32[2,128,8192]{2,1,0:T(8,128)}, u32[]{:S(2)}, u32[]{:S(2)}) %collective-permute-start.2) | collective-permute-done | bytes 8388640 | tf_op jit(solution)/shard_map/ppermute | solution.py:16
  680.3 9.0 select_add_fusion.1
  690.0 7.1 collective-permute-done.3
  699.7 4.0 collective-permute-done.4
  705.7 91.4 %collective-permute-done.5 = bf16[2,128,8192]{2,1,0:T(8,128)(2,1)S(1)} collective-permute-done((bf16[2,128,8192]{2,1,0:T(8,128)(2,1)S(1)}, bf16[2,128,8192]{2,1,0:T(8,128)(2,1)S(1)}, u32[]{:S(2)}, u32[]{:S(2)}) %collective-permute-start.5) | collective-permute-done | bytes 4194336 | tf_op jit(solution)/shard_map/ppermute | solution.py:16
  797.1 4.2 broadcast_select_fusion.4
  801.3 7.9 pad_maximum_fusion.2
  809.1 2.2 collective-permute-start.6
  811.3 180.1 %collective-permute-done.6 = bf16[2,256,8192]{2,1,0:T(8,128)(2,1)S(1)} collective-permute-done((bf16[2,256,8192]{2,1,0:T(8,128)(2,1)}, bf16[2,256,8192]{2,1,0:T(8,128)(2,1)S(1)}, u32[]{:S(2)}, u32[]{:S(2)}) %collective-permute-start.6) | collective-permute-done | bytes 8388640 | tf_op jit(solution)/shard_map/ppermute | solution.py:16
  991.4 6.3 broadcast_select_fusion
  997.7 16.6 %fusion.3 = f32[512,1024]{1,0:T(8,128)S(1)} fusion(bf16[1,1024,8192]{2,1,0:T(8,128)(2,1)} %param.9, bf16[2,256,8192]{2,1,0:T(8,128)(2,1)S(1)} %get-tuple-element.6, bf16[2,256,8192]{2,1,0:T(8,128)(2,1)S(1)} %get-tuple-element.5), kind=kOutput, calls=%fused_computation.8 | convolution fusion | flops 8606711808 | bytes 35651584 | tf_op jit(solution)/shard_map/dot_general | solution.py:24
  1014.5 3.9 collective-permute-start.7
  1018.4 44.2 %collective-permute-done.7 = f32[256,1024]{1,0:T(8,128)S(1)} collective-permute-done((f32[256,1024]{1,0:T(8,128)S(1)}, f32[256,1024]{1,0:T(8,128)S(1)}, u32[]{:S(2)}, u32[]{:S(2)}) %collective-permute-start.7) | collective-permute-done | bytes 1048608 | tf_op jit(solution)/shard_map/ppermute | solution.py:16
  1064.2 24.9 %collective-permute-done.8 = bf16[256,1024]{1,0:T(8,128)(2,1)S(1)} collective-permute-done((bf16[256,1024]{1,0:T(8,128)(2,1)S(1)}, bf16[256,1024]{1,0:T(8,128)(2,1)S(1)}, u32[]{:S(2)}, u32[]{:S(2)}) %collective-permute-start.8) | collective-permute-done | bytes 524320 | tf_op jit(solution)/shard_map/ppermute | solution.py:16
  1089.2 7.5 fusion.18
  1099.2 21.7 %collective-permute-done.13 = bf16[128,4096]{1,0:T(8,128)(2,1)S(1)} collective-permute-done((bf16[128,4096]{1,0:T(8,128)(2,1)S(1)}, bf16[128,4096]{1,0:T(8,128)(2,1)S(1)}, u32[]{:S(2)}, u32[]{:S(2)}) %collective-permute-start.13) | collective-permute-done | bytes 1048608 | tf_op jit(solution)/shard_map/ppermute | solution.py:16
  1124.6 66.3 %collective-permute-done.9 = f32[256,4096]{1,0:T(8,128)S(1)} collective-permute-done((f32[256,4096]{1,0:T(8,128)S(1)}, f32[256,4096]{1,0:T(8,128)S(1)}, u32[]{:S(2)}, u32[]{:S(2)}) %collective-permute-start.9) | collective-permute-done | bytes 4194336 | tf_op jit(solution)/shard_map/ppermute | solution.py:16
  1196.1 37.1 %collective-permute-done.14 = bf16[256,4096]{1,0:T(8,128)(2,1)} collective-permute-done((bf16[256,4096]{1,0:T(8,128)(2,1)}, bf16[256,4096]{1,0:T(8,128)(2,1)}, u32[]{:S(2)}, u32[]{:S(2)}) %collective-permute-start.14) | collective-permute-done | bytes 2097184 | tf_op jit(solution)/shard_map/ppermute | solution.py:16
  1233.1 4.6 broadcast_select_fusion.6
  1237.7 14.9 %convert_bitcast_fusion = bf16[1,8192,1024]{2,1,0:T(8,128)(2,1)} fusion(bf16[2,256,8192]{2,1,0:T(8,128)(2,1)} %copy-done.1, bf16[2,256,8192]{2,1,0:T(8,128)(2,1)} %copy-done.2, bf16[2,256,1024]{2,1,0:T(8,128)(2,1)} %copy-done.6, bf16[2,256,1024]{2,1,0:T(8,128)(2,1)S(1)} %copy-done.5), kind=kOutput, calls=%fused_computation.12 | convolution fusion | flops 8617197568 | bytes 35651584 | tf_op jit(solution)/shard_map/dot_general | solution.py:24
  1252.6 3.2 select_add_fusion.4
  1256.9 15.1 %convert_bitcast_fusion.1 = bf16[1,1024,8192]{2,1,0:T(8,128)(2,1)} fusion(bf16[2,256,1024]{2,1,0:T(8,128)(2,1)S(1)} %copy-done.5, bf16[2,256,1024]{2,1,0:T(8,128)(2,1)} %copy-done.6, bf16[2,256,8192]{2,1,0:T(8,128)(2,1)} %copy-done.2, bf16[2,256,8192]{2,1,0:T(8,128)(2,1)} %copy-done.1), kind=kOutput, calls=%fused_computation.13 | convolution fusion | flops 8617197568 | bytes 35651584 | tf_op jit(solution)/shard_map/dot_general | solution.py:24
  1272.0 10.4 convert_bitcast_fusion.2
  1282.4 2.2 fusion.34
  (55 shorter events, 24.5 us)
Async XLA Ops:
  2.8 49.8 %collective-permute-start = (bf16[2,256,1024]{2,1,0:T(8,128)(2,1)S(1)}, bf16[2,256,1024]{2,1,0:T(8,128)(2,1)}, u32[]{:S(2)}, u32[]{:S(2)}) collective-permute-start(bf16[2,256,1024]{2,1,0:T(8,128)(2,1)S(1)} %constant_dynamic-update-slice_fusion), channel_id=1, source_target_pairs={{0,8},{8,0},{1,9},{9,1},{2,10},{10,2},{3,11},{11,3},{4,12},{12,4},... | collective-permute-start | bytes 3145736 | tf_op jit(solution)/shard_map/ppermute | solution.py:16
  54.0 16.6 %copy-start.4 = (bf16[2,256,1024]{2,1,0:T(8,128)(2,1)}, bf16[2,256,1024]{2,1,0:T(8,128)(2,1)S(1)}, u32[]{:S(2)}) copy-start(bf16[2,256,1024]{2,1,0:T(8,128)(2,1)S(1)} %get-tuple-element.17) | copy-start | bytes 3145732
  54.0 16.6 %copy-start.6 = (bf16[2,256,1024]{2,1,0:T(8,128)(2,1)}, bf16[2,256,1024]{2,1,0:T(8,128)(2,1)S(1)}, u32[]{:S(2)}) copy-start(bf16[2,256,1024]{2,1,0:T(8,128)(2,1)S(1)} %get-tuple-element.18) | copy-start | bytes 3145732
  104.3 361.7 %collective-permute-start.1 = (f32[2,256,8192]{2,1,0:T(8,128)}, f32[2,256,8192]{2,1,0:T(8,128)}, u32[]{:S(2)}, u32[]{:S(2)}) collective-permute-start(f32[2,256,8192]{2,1,0:T(8,128)} %broadcast_select_fusion.2), channel_id=1, source_target_pairs={{0,4},{4,0},{1,5},{5,1},{2,6},{6,2},{3,7},{7,3},{8,12},{12,8},{9,1... | collective-permute-start | bytes 50331656 | tf_op jit(solution)/shard_map/ppermute | solution.py:16
  499.3 181.0 %collective-permute-start.2 = (f32[2,128,8192]{2,1,0:T(8,128)}, f32[2,128,8192]{2,1,0:T(8,128)}, u32[]{:S(2)}, u32[]{:S(2)}) collective-permute-start(f32[2,128,8192]{2,1,0:T(8,128)} %slice_select_fusion), channel_id=1, source_target_pairs={{0,2},{2,0},{1,3},{3,1},{4,6},{6,4},{5,7},{7,5},{8,10},{10,8},{9,1... | collective-permute-start | bytes 25165832 | tf_op jit(solution)/shard_map/ppermute | solution.py:16
  689.9 7.2 collective-permute-start.3
  699.5 4.2 collective-permute-start.4
  704.4 92.7 %collective-permute-start.5 = (bf16[2,128,8192]{2,1,0:T(8,128)(2,1)S(1)}, bf16[2,128,8192]{2,1,0:T(8,128)(2,1)S(1)}, u32[]{:S(2)}, u32[]{:S(2)}) collective-permute-start(bf16[2,128,8192]{2,1,0:T(8,128)(2,1)S(1)} %pad_maximum_fusion.3), channel_id=1, source_target_pairs={{0,2},{2,0},{1,3},{3,1},{4,6},{6,4},{5,7},{7,5},{8,10},{10,8},{9,1... | collective-permute-start | bytes 12582920 | tf_op jit(solution)/shard_map/ppermute | solution.py:16
  809.1 182.3 %collective-permute-start.6 = (bf16[2,256,8192]{2,1,0:T(8,128)(2,1)}, bf16[2,256,8192]{2,1,0:T(8,128)(2,1)S(1)}, u32[]{:S(2)}, u32[]{:S(2)}) collective-permute-start(bf16[2,256,8192]{2,1,0:T(8,128)(2,1)} %pad_maximum_fusion.2), channel_id=1, source_target_pairs={{0,4},{4,0},{1,5},{5,1},{2,6},{6,2},{3,7},{7,3},{8,12},{12,8},{9,1... | collective-permute-start | bytes 25165832 | tf_op jit(solution)/shard_map/ppermute | solution.py:16
  997.7 16.6 %copy-start.1 = (bf16[2,256,8192]{2,1,0:T(8,128)(2,1)}, bf16[2,256,8192]{2,1,0:T(8,128)(2,1)S(1)}, u32[]{:S(2)}) copy-start(bf16[2,256,8192]{2,1,0:T(8,128)(2,1)S(1)} %get-tuple-element.5) | copy-start | bytes 25165828
  997.7 16.6 %copy-start.2 = (bf16[2,256,8192]{2,1,0:T(8,128)(2,1)}, bf16[2,256,8192]{2,1,0:T(8,128)(2,1)S(1)}, u32[]{:S(2)}) copy-start(bf16[2,256,8192]{2,1,0:T(8,128)(2,1)S(1)} %get-tuple-element.6) | copy-start | bytes 25165828
  1014.4 49.8 %copy-start.7 = (bf16[1,64,4096]{2,1,0:T(8,128)(2,1)S(1)}, bf16[1,64,4096]{2,1,0:T(8,128)(2,1)}, u32[]{:S(2)}) copy-start(bf16[1,64,4096]{2,1,0:T(8,128)(2,1)} %param.8) | copy-start | bytes 1572868
  1014.5 48.0 %collective-permute-start.7 = (f32[256,1024]{1,0:T(8,128)S(1)}, f32[256,1024]{1,0:T(8,128)S(1)}, u32[]{:S(2)}, u32[]{:S(2)}) collective-permute-start(f32[256,1024]{1,0:T(8,128)S(1)} %slice_select_fusion.5), channel_id=1, source_target_pairs={{0,8},{8,0},{1,9},{9,1},{2,10},{10,2},{3,11},{11,3},{4,12},{12,4},... | collective-permute-start | bytes 3145736 | tf_op jit(solution)/shard_map/ppermute | solution.py:16
  1064.0 32.8 %copy-start.3 = (bf16[256,1024]{1,0:T(8,128)(2,1)}, bf16[256,1024]{1,0:T(8,128)(2,1)S(1)}, u32[]{:S(2)}) copy-start(bf16[256,1024]{1,0:T(8,128)(2,1)S(1)} %fusion.33) | copy-start | bytes 1572868
  1064.0 25.1 %collective-permute-start.8 = (bf16[256,1024]{1,0:T(8,128)(2,1)S(1)}, bf16[256,1024]{1,0:T(8,128)(2,1)S(1)}, u32[]{:S(2)}, u32[]{:S(2)}) collective-permute-start(bf16[256,1024]{1,0:T(8,128)(2,1)S(1)} %fusion.33), channel_id=1, source_target_pairs={{0,8},{8,0},{1,9},{9,1},{2,10},{10,2},{3,11},{11,3},{4,12},{12,4},... | collective-permute-start | bytes 1572872 | tf_op jit(solution)/shard_map/ppermute | solution.py:16
  1064.1 33.3 %collective-permute-start.12 = (bf16[64,4096]{1,0:T(8,128)(2,1)S(1)}, bf16[64,4096]{1,0:T(8,128)(2,1)S(1)}, u32[]{:S(2)}, u32[]{:S(2)}) collective-permute-start(bf16[64,4096]{1,0:T(8,128)(2,1)S(1)} %bitcast.50), channel_id=1, source_target_pairs={{0,1},{1,0},{2,3},{3,2},{4,5},{5,4},{6,7},{7,6},{8,9},{9,8},{10,11... | collective-permute-start | bytes 1572872 | tf_op jit(solution)/shard_map/ppermute | solution.py:16
  1089.2 7.6 copy-start.8
  1089.2 7.6 copy-start.9
  1097.3 93.6 %collective-permute-start.9 = (f32[256,4096]{1,0:T(8,128)S(1)}, f32[256,4096]{1,0:T(8,128)S(1)}, u32[]{:S(2)}, u32[]{:S(2)}) collective-permute-start(f32[256,4096]{1,0:T(8,128)S(1)} %slice_select_fusion.1), channel_id=1, source_target_pairs={{0,4},{4,0},{1,5},{5,1},{2,6},{6,2},{3,7},{7,3},{8,12},{12,8},{9,1... | collective-permute-start | bytes 12582920 | tf_op jit(solution)/shard_map/ppermute | solution.py:16
  1097.6 23.3 %collective-permute-start.13 = (bf16[128,4096]{1,0:T(8,128)(2,1)S(1)}, bf16[128,4096]{1,0:T(8,128)(2,1)S(1)}, u32[]{:S(2)}, u32[]{:S(2)}) collective-permute-start(bf16[128,4096]{1,0:T(8,128)(2,1)S(1)} %pad_maximum_fusion.8), channel_id=1, source_target_pairs={{0,2},{2,0},{1,3},{3,1},{4,6},{6,4},{5,7},{7,5},{8,10},{10,8},{9,1... | collective-permute-start | bytes 3145736 | tf_op jit(solution)/shard_map/ppermute | solution.py:16
  1122.9 110.2 %collective-permute-start.14 = (bf16[256,4096]{1,0:T(8,128)(2,1)}, bf16[256,4096]{1,0:T(8,128)(2,1)}, u32[]{:S(2)}, u32[]{:S(2)}) collective-permute-start(bf16[256,4096]{1,0:T(8,128)(2,1)} %pad_maximum_fusion.5), channel_id=1, source_target_pairs={{0,4},{4,0},{1,5},{5,1},{2,6},{6,2},{3,7},{7,3},{8,12},{12,8},{9,1... | collective-permute-start | bytes 6291464 | tf_op jit(solution)/shard_map/ppermute | solution.py:16
  1192.2 2.0 copy-start
  1194.5 43.3 %copy-start.5 = (bf16[2,256,1024]{2,1,0:T(8,128)(2,1)S(1)}, bf16[2,256,1024]{2,1,0:T(8,128)(2,1)}, u32[]{:S(2)}) copy-start(bf16[2,256,1024]{2,1,0:T(8,128)(2,1)} %copy-done.4) | copy-start | bytes 3145732
  1194.5 58.1 %collective-permute-start.10 = (f32[128,4096]{1,0:T(8,128)S(1)}, f32[128,4096]{1,0:T(8,128)}, u32[]{:S(2)}, u32[]{:S(2)}) collective-permute-start(f32[128,4096]{1,0:T(8,128)S(1)} %slice_select_fusion.3), channel_id=1, source_target_pairs={{0,2},{2,0},{1,3},{3,1},{4,6},{6,4},{5,7},{7,5},{8,10},{10,8},{9,1... | collective-permute-start | bytes 6291464 | tf_op jit(solution)/shard_map/ppermute | solution.py:16
  1256.9 25.6 %collective-permute-start.11 = (f32[64,4096]{1,0:T(8,128)}, f32[64,4096]{1,0:T(8,128)}, u32[]{:S(2)}, u32[]{:S(2)}) collective-permute-start(f32[64,4096]{1,0:T(8,128)} %slice_select_fusion.4), channel_id=1, source_target_pairs={{0,1},{1,0},{2,3},{3,2},{4,5},{5,4},{6,7},{7,6},{8,9},{9,8},{10,11... | collective-permute-start | bytes 3145736 | tf_op jit(solution)/shard_map/ppermute | solution.py:16
where the time goes:
time: 1290 us
  waiting for transfers between devices  1060 us (82%)
  other arithmetic  100 us (8%)
  matrix products  97 us (8%)
  starting transfers between devices  18.7 us (1%)
    ppermute x15, waiting for transfers between devices, swapped(): return lax.ppermute(block, axis, route)  1060 us
    dot_general x6, matrix products, contract(): lax.dot_general(left, right, (((left_dim,), (right_dim,)), ((), ())), pre...  80.4 us
    add x5, other arithmetic, group_scatter(): value = keep + trade(sent, bit)  36.8 us
    select_n x7, other arithmetic, group_scatter(): sent = jnp.where(lower, second, first)  30.9 us
  transfers between devices with their start and end apart: 15, of which 12 were waited for; matrix products, arithmetic and copies ran while one was open for 4% of the time, Pallas kernels for 0%

commit v1 on v0

v1 whole, which is shorter than its diff:
```python
import jax
import jax.numpy as jnp
from jax import lax
from jax.sharding import PartitionSpec as P

CORE, NEAR, FAR = 1, 2, 4
SHARES = 8
GROUP = 16


def swap(value, mask):
    count = lax.axis_size("gx")
    return lax.ppermute(value, "gx", [(at, at ^ mask) for at in range(count)])


def gelu_tanh(value):
    return jax.nn.gelu(value, approximate=True)


def contract(left, right, left_dim, right_dim):
    return lax.dot_general(
        left, right, (((left_dim,), (right_dim,)), ((), ())), preferred_element_type=jnp.float32
    )


def gather(value, masks):
    for mask in masks:
        value = jnp.concatenate([value, swap(value, mask)], axis=0)
    return value


def scatter(value, masks):
    for mask in masks:
        half = value.shape[0] // 2
        sent = value[half:].astype(jnp.bfloat16)
        value = value[:half].astype(jnp.float32) + swap(sent, mask).astype(jnp.float32)
    return value


NEAR_FAR = (CORE, NEAR, FAR)
FAR_NEAR = (CORE, FAR, NEAR)


def offset_of(place, order):
    total = jnp.zeros_like(place)
    for at, mask in enumerate(order):
        total = total + mask * ((place >> (2 - at)) & 1)
    return total


def place_of(offset, order):
    total = jnp.zeros_like(offset)
    for at, mask in enumerate(order):
        total = total + jnp.where((offset & mask) != 0, 1 << (2 - at), 0)
    return total


def picked(source, value):
    columns = lax.broadcasted_iota(jnp.int32, (source.shape[0], value.shape[0]), 1)
    chooser = (source[:, None] == columns).astype(jnp.bfloat16)
    return contract(chooser, value, 1, 0).astype(jnp.bfloat16)


def body(input_tiles, grad_tiles, context_tiles, up_tiles, down_tiles, output_tiles):
    grid_index = lax.axis_index("gx")
    total_bits = lax.axis_size("gx").bit_length() - 1
    q_masks = [1 << bit for bit in range(3, total_bits)]
    own_p = grid_index & (SHARES - 1)
    own_q = grid_index >> 3
    inputs = input_tiles[0]
    grads = grad_tiles[0]
    context = context_tiles[0]
    up_block = up_tiles[0]
    down_block = down_tiles[0]
    proj_block = output_tiles[0]
    rows = inputs.shape[0]
    half_rows = rows // 2
    share_rows = half_rows // SHARES
    block_rows = context.shape[0]
    half_block = block_rows // 2
    q_count = 1 << len(q_masks)

    def half_source(order):
        at = jnp.arange(rows, dtype=jnp.int32)
        half, at = at // half_rows, at % half_rows
        share = own_p ^ offset_of(at // share_rows, order)
        inside = share * share_rows + at % share_rows
        return (inside // GROUP) * 2 * GROUP + half * GROUP + inside % GROUP

    def token_source(half, order):
        at = jnp.arange(SHARES * half_block, dtype=jnp.int32)
        block = own_p ^ offset_of(at // half_block, order)
        at = at % half_block
        token = block * block_rows + (at // GROUP) * 2 * GROUP + half * GROUP + at % GROUP
        local = token % rows
        inside = (local // (2 * GROUP)) * GROUP + local % GROUP
        place = place_of(own_p ^ (inside // share_rows), NEAR_FAR)
        return ((token // rows) ^ own_q) * half_rows + place * share_rows + inside % share_rows

    source_nf = half_source(NEAR_FAR)
    inputs_nf = picked(source_nf, inputs)
    grads_nf = picked(source_nf, grads)
    grads_fn = picked(half_source(FAR_NEAR), grads)

    def q_gather(value):
        value = value[None]
        for mask in q_masks:
            value = jnp.concatenate([value, swap(value, mask)], axis=0)
        return value

    chunks = {}
    for half in range(2):
        at = slice(half * half_rows, (half + 1) * half_rows)
        pair = q_gather(jnp.stack([inputs_nf[at], grads_fn[at]]))
        chunks["own", half] = pair[0, 0], pair[0, 1]
        chunks["other", half] = tuple(
            pair[1:, which].reshape((q_count - 1) * half_rows, -1) for which in range(2)
        )

    halves = context.reshape(block_rows // (2 * GROUP), 2, GROUP, -1)
    halves = [halves[:, half].reshape(half_block, -1) for half in range(2)]
    context_orders = (FAR_NEAR, NEAR_FAR)
    context_rows = [gather(halves[half], context_orders[half][::-1]) for half in range(2)]

    act_rows, dpre_rows, input_parts = {}, {}, {}

    def forward(name):
        chunk_in, chunk_grad = chunks[name]
        count = chunk_in.shape[0]
        pre_part = contract(chunk_in, up_block, 1, 0)
        hidden_part = contract(chunk_grad, down_block, 1, 1)
        pre_share = scatter(pre_part, NEAR_FAR)
        hidden_share = scatter(hidden_part, FAR_NEAR)
        act_share, gelu_back = jax.vjp(gelu_tanh, pre_share)
        dpre_share = gelu_back(hidden_share)[0].astype(jnp.bfloat16)
        act_rows[name] = gather(act_share.astype(jnp.bfloat16), FAR_NEAR[::-1])
        dpre_rows[name] = gather(dpre_share, NEAR_FAR[::-1])
        input_parts[name] = contract(dpre_rows[name], up_block, 1, 1)

    d_input_own, d_input_rows, d_context_halves = [], [], []

    def finish(half):
        own = input_parts["own", half][None]
        other = input_parts["other", half].reshape(q_count - 1, half_rows, -1)
        parts = jnp.concatenate([own, other], axis=0) if q_count > 2 else None
        if q_count == 2:
            share = own[0] + swap(other[0].astype(jnp.bfloat16), q_masks[0]).astype(jnp.float32)
        else:
            share = scatter(parts, q_masks[::-1])[0]
        at = slice(half * half_rows, (half + 1) * half_rows)
        d_input = (grads_nf[at].astype(jnp.float32) + share).astype(jnp.bfloat16)
        d_input_own.append(d_input)
        gathered = q_gather(d_input).reshape(q_count * half_rows, -1)
        by_order = {
            order: picked(token_source(half, order), gathered) for order in (NEAR_FAR, FAR_NEAR)
        }
        d_input_rows.append(by_order[context_orders[half]])
        columns = proj_block.shape[0] // 2
        first = contract(by_order[NEAR_FAR], proj_block[:columns], 1, 1)
        second = contract(by_order[FAR_NEAR], proj_block[columns:], 1, 1)
        first = scatter(first, NEAR_FAR)
        second = scatter(second, FAR_NEAR)
        d_context_halves.append(
            jnp.concatenate([first, second], axis=1).astype(jnp.bfloat16)
        )

    order = [("own", 0), ("other", 0), ("other", 1), ("own", 1)]
    for name in order[:2]:
        forward(name)
    finish(0)
    for name in order[2:]:
        forward(name)
    finish(1)

    act_all = jnp.concatenate([act_rows[name] for name in order], axis=0)
    dpre_all = jnp.concatenate([dpre_rows[name] for name in order], axis=0)
    in_all = jnp.concatenate([chunks[name][0] for name in order], axis=0)
    grad_all = jnp.concatenate([chunks[name][1] for name in order], axis=0)
    d_down = contract(act_all, grad_all, 0, 0).astype(jnp.bfloat16)
    d_up = contract(in_all, dpre_all, 0, 0).astype(jnp.bfloat16)

    own_all = jnp.concatenate(d_input_own, axis=0)
    columns = lax.broadcasted_iota(jnp.int32, (rows, rows), 1)
    chooser = (source_nf[:, None] == columns).astype(jnp.bfloat16)
    d_input = contract(chooser, own_all, 0, 0).astype(jnp.bfloat16)

    context_all = jnp.concatenate(context_rows, axis=0)
    d_input_all = jnp.concatenate(d_input_rows, axis=0)
    d_output = contract(context_all, d_input_all, 0, 0).astype(jnp.bfloat16)

    split = [
        part.reshape(block_rows // (2 * GROUP), 1, GROUP, -1) for part in d_context_halves
    ]
    d_context = jnp.concatenate(split, axis=1).reshape(block_rows, -1)
    return (d_input[None], d_context[None], d_up[None], d_down[None], d_output[None])


def solution(mesh):
    return jax.shard_map(
        body,
        mesh=mesh,
        in_specs=(
            P("gx", "groups", None),
            P("gx", "groups", None),
            P("gx", "groups", None),
            P("gx", None, None),
            P("gx", None, None),
            P("gx", None, None),
        ),
        out_specs=(
            P("gx", "groups", None),
            P("gx", "groups", None),
            P("gx", "groups", None),
            P("gx", "groups", None),
            P("gx", "groups", None),
        ),
        check_vma=False,
    )
```

time: 1290 us -> 529 us (0.41)
  waiting for transfers between devices: 1060 us -> 175 us
  matrix products: 97 us -> 201 us
  other arithmetic: 100 us -> 27.9 us
  local copies, waits for them, and re-layouts: 4.21 us -> 57.3 us
  starting transfers between devices: 18.7 us -> 56 us
    ppermute x15 -> x72, waiting for transfers between devices: 1060 us -> 175 us  [swap(): return lax.ppermute(value, 'gx', [(at, at ^ mask) for at in range(count)])]
    dot_general x6 -> x25, matrix products: 80.4 us -> 201 us  [contract(): lax.dot_general(left, right, (((left_dim,), (right_dim,)), ((), ())), pre...]
    select_n x15 -> x0, other arithmetic: 48.2 us -> none  [the longest x7 30.9 us: group_scatter(): sent = jnp.where(lower, second, first)]
    ppermute x15 -> x72, starting transfers between devices: 18.7 us -> 56 us  [swap(): return lax.ppermute(value, 'gx', [(at, at ^ mask) for at in range(count)])]
    unnamed x21 -> x111, local copies, waits for them, and re-layouts: 3.13 us -> 30.8 us
    add x5 -> x29, other arithmetic: 36.8 us -> 9.95 us  [the longest x24 9.76 us: scatter(): value[:half].astype(jnp.float32) + swap(sent, mask).astype(jnp.float32)]
    slice x0 -> x37, local copies, waits for them, and re-layouts: none -> 18.9 us  [the longest x36 17.8 us: scatter(): sent = value[half:].astype(jnp.bfloat16)]
    dot_general x1 -> x0, matrix products: 16.6 us -> none  [body(): pre_part = jnp.dot(input_rows, up_block, preferred_element_type=jnp.float32)]
  transfers between devices with their start and end apart: 15 -> 72, of which waited for: 12 -> 32; matrix products, arithmetic and copies ran while one was open for 4% -> 51% of each run, Pallas kernels for 0% -> 0%
where the time goes in v1:
time: 529 us; the launch traced here: 520 us
  matrix products  201 us (38%)
  waiting for transfers between devices  175 us (33%)
  local copies, waits for them, and re-layouts  57.3 us (11%)
  starting transfers between devices  56 us (11%)
  other arithmetic  27.9 us (5%)
    dot_general x25, matrix products, contract(): lax.dot_general(left, right, (((left_dim,), (right_dim,)), ((), ())), pre...  201 us
    ppermute x72, waiting for transfers between devices, swap(): return lax.ppermute(value, 'gx', [(at, at ^ mask) for at in range(count)])  175 us
    ppermute x72, starting transfers between devices, swap(): return lax.ppermute(value, 'gx', [(at, at ^ mask) for at in range(count)])  56 us
    unnamed x111, local copies, waits for them, and re-layouts  30.8 us
    slice x36, local copies, waits for them, and re-layouts, scatter(): sent = value[half:].astype(jnp.bfloat16)  17.8 us
  transfers between devices with their start and end apart: 72, of which 32 were waited for; matrix products, arithmetic and copies ran while one was open for 51% of the time, Pallas kernels for 0%

profile of v1, /device:TPU:0, one launch (start us, length us, event | category | flops | bytes accessed | tf_op | source)
XLA Modules:
  0.0 519.7 jit_solution(10891011445355200243)
XLA Ops:
  7.7 8.1 %fusion.14 = f32[128,8192]{1,0:T(8,128)S(1)} fusion(bf16[1,1024,8192]{2,1,0:T(8,128)(2,1)} %param.9, bf16[1,2,128,1024]{3,2,1,0:T(8,128)(2,1)S(1)} %maximum_bitcast_fusion), kind=kOutput, calls=%fused_computation.14 | convolution fusion | flops 2147483648 | bytes 21233664 | tf_op jit(solution)/shard_map/dot_general | solution.py:21
  18.9 13.3 %fusion.22 = f32[128,8192]{1,0:T(8,128)} fusion(bf16[1,8192,1024]{2,1,0:T(8,128)(2,1)} %param.10, bf16[1,2,128,1024]{3,2,1,0:T(8,128)(2,1)S(1)} %maximum_bitcast_fusion), kind=kOutput, calls=%fused_computation.22 | convolution fusion | flops 2147483648 | bytes 21233664 | tf_op jit(solution)/shard_map/dot_general | solution.py:21
  38.6 10.1 %fusion.6 = f32[128,8192]{1,0:T(8,128)} fusion(bf16[1,1024,8192]{2,1,0:T(8,128)(2,1)} %param.9, bf16[1,2,128,1024]{3,2,1,0:T(8,128)(2,1)S(1)} %maximum_bitcast_fusion.1), kind=kOutput, calls=%fused_computation.6 | convolution fusion | flops 2147483648 | bytes 21233664 | tf_op jit(solution)/shard_map/dot_general | solution.py:21
  48.7 13.7 %fusion.18 = f32[128,8192]{1,0:T(8,128)} fusion(bf16[1,8192,1024]{2,1,0:T(8,128)(2,1)} %param.10, bf16[1,2,128,1024]{3,2,1,0:T(8,128)(2,1)S(1)} %maximum_bitcast_fusion.1), kind=kOutput, calls=%fused_computation.18 | convolution fusion | flops 2147483648 | bytes 21233664 | tf_op jit(solution)/shard_map/dot_general | solution.py:21
  81.2 13.3 %fusion.20 = f32[128,8192]{1,0:T(8,128)} fusion(bf16[1,8192,1024]{2,1,0:T(8,128)(2,1)} %param.10, bf16[1,2,128,1024]{3,2,1,0:T(8,128)(2,1)S(1)} %collective-permute-done.9), kind=kOutput, calls=%fused_computation.20 | convolution fusion | flops 2147483648 | bytes 21233664 | tf_op jit(solution)/shard_map/dot_general | solution.py:21
  94.5 10.1 %fusion.10 = f32[128,8192]{1,0:T(8,128)} fusion(bf16[1,1024,8192]{2,1,0:T(8,128)(2,1)} %param.9, bf16[1,2,128,1024]{3,2,1,0:T(8,128)(2,1)S(1)} %collective-permute-done.9), kind=kOutput, calls=%fused_computation.10 | convolution fusion | flops 2147483648 | bytes 21233664 | tf_op jit(solution)/shard_map/dot_general | solution.py:21
  106.2 13.4 %fusion.16 = f32[128,8192]{1,0:T(8,128)} fusion(bf16[1,8192,1024]{2,1,0:T(8,128)(2,1)} %param.10, bf16[1,2,128,1024]{3,2,1,0:T(8,128)(2,1)S(1)} %collective-permute-done.29), kind=kOutput, calls=%fused_computation.16 | convolution fusion | flops 2147483648 | bytes 21233664 | tf_op jit(solution)/shard_map/dot_general | solution.py:21
  119.6 8.3 %fusion.2 = f32[128,8192]{1,0:T(8,128)S(1)} fusion(bf16[1,1024,8192]{2,1,0:T(8,128)(2,1)} %param.9, bf16[1,2,128,1024]{3,2,1,0:T(8,128)(2,1)S(1)} %collective-permute-done.29), kind=kOutput, calls=%fused_computation.2 | convolution fusion | flops 2147483648 | bytes 21233664 | tf_op jit(solution)/shard_map/dot_general | solution.py:21
  134.1 12.1 %collective-permute-done.70 = bf16[64,4096]{1,0:T(8,128)(2,1)S(1)} collective-permute-done((bf16[64,4096]{1,0:T(8,128)(2,1)S(1)}, bf16[64,4096]{1,0:T(8,128)(2,1)S(1)}, u32[]{:S(2)}, u32[]{:S(2)}) %collective-permute-start.70) | collective-permute-done | bytes 524320 | tf_op jit(solution)/shard_map/ppermute | solution.py:13
  160.0 11.4 %collective-permute-done.4 = bf16[32,8192]{1,0:T(8,128)(2,1)S(1)} collective-permute-done((bf16[32,8192]{1,0:T(8,128)(2,1)S(1)}, bf16[32,8192]{1,0:T(8,128)(2,1)S(1)}, u32[]{:S(2)}, u32[]{:S(2)}) %collective-permute-start.4) | collective-permute-done | bytes 524320 | tf_op jit(solution)/shard_map/ppermute | solution.py:13
  173.8 7.9 %collective-permute-done.24 = bf16[32,8192]{1,0:T(8,128)(2,1)S(1)} collective-permute-done((bf16[32,8192]{1,0:T(8,128)(2,1)S(1)}, bf16[32,8192]{1,0:T(8,128)(2,1)S(1)}, u32[]{:S(2)}, u32[]{:S(2)}) %collective-permute-start.24) | collective-permute-done | bytes 524320 | tf_op jit(solution)/shard_map/ppermute | solution.py:13
  195.0 22.2 %collective-permute-done.54 = bf16[16,8192]{1,0:T(8,128)(2,1)S(1)} collective-permute-done((bf16[16,8192]{1,0:T(8,128)(2,1)S(1)}, bf16[16,8192]{1,0:T(8,128)(2,1)S(1)}, u32[]{:S(2)}, u32[]{:S(2)}) %collective-permute-start.54) | collective-permute-done | bytes 262176 | tf_op jit(solution)/shard_map/ppermute | solution.py:13
  218.4 5.2 %collective-permute-done.6 = bf16[16,8192]{1,0:T(8,128)(2,1)S(1)} collective-permute-done((bf16[16,8192]{1,0:T(8,128)(2,1)S(1)}, bf16[16,8192]{1,0:T(8,128)(2,1)S(1)}, u32[]{:S(2)}, u32[]{:S(2)}) %collective-permute-start.6) | collective-permute-done | bytes 262176 | tf_op jit(solution)/shard_map/ppermute | solution.py:13
  228.4 12.2 %collective-permute-done.55 = bf16[32,8192]{1,0:T(8,128)(2,1)S(1)} collective-permute-done((bf16[32,8192]{1,0:T(8,128)(2,1)S(1)}, bf16[32,8192]{1,0:T(8,128)(2,1)S(1)}, u32[]{:S(2)}, u32[]{:S(2)}) %collective-permute-start.55) | collective-permute-done | bytes 524320 | tf_op jit(solution)/shard_map/ppermute | solution.py:13
  245.5 6.3 %collective-permute-done.15 = bf16[16,8192]{1,0:T(8,128)(2,1)S(1)} collective-permute-done((bf16[16,8192]{1,0:T(8,128)(2,1)S(1)}, bf16[16,8192]{1,0:T(8,128)(2,1)S(1)}, u32[]{:S(2)}, u32[]{:S(2)}) %collective-permute-start.15) | collective-permute-done | bytes 262176 | tf_op jit(solution)/shard_map/ppermute | solution.py:13
  256.4 5.5 %collective-permute-done.57 = bf16[16,8192]{1,0:T(8,128)(2,1)S(1)} collective-permute-done((bf16[16,8192]{1,0:T(8,128)(2,1)S(1)}, bf16[16,8192]{1,0:T(8,128)(2,1)S(1)}, u32[]{:S(2)}, u32[]{:S(2)}) %collective-permute-start.57) | collective-permute-done | bytes 262176 | tf_op jit(solution)/shard_map/ppermute | solution.py:13
  267.7 8.4 %collective-permute-done.58 = bf16[32,8192]{1,0:T(8,128)(2,1)S(1)} collective-permute-done((bf16[32,8192]{1,0:T(8,128)(2,1)S(1)}, bf16[32,8192]{1,0:T(8,128)(2,1)S(1)}, u32[]{:S(2)}, u32[]{:S(2)}) %collective-permute-start.58) | collective-permute-done | bytes 524320 | tf_op jit(solution)/shard_map/ppermute | solution.py:13
  280.6 6.7 %collective-permute-done.32 = bf16[16,8192]{1,0:T(8,128)(2,1)S(1)} collective-permute-done((bf16[16,8192]{1,0:T(8,128)(2,1)S(1)}, bf16[16,8192]{1,0:T(8,128)(2,1)S(1)}, u32[]{:S(2)}, u32[]{:S(2)}) %collective-permute-start.32) | collective-permute-done | bytes 262176 | tf_op jit(solution)/shard_map/ppermute | solution.py:13
  292.6 12.7 %fusion.95 = bf16[128,1024]{1,0:T(8,128)(2,1)} fusion(bf16[1,1024,8192]{2,1,0:T(8,128)(2,1)} %param.9, bf16[64,8192]{1,0:T(8,128)(2,1)} %copy-done.21, bf16[32,8192]{1,0:T(8,128)(2,1)} %copy-done.15, bf16[16,8192]{1,0:T(8,128)(2,1)} %copy-done.10, bf16[16,8192]{1,0:T(8,128)(2,1)S(1)} %get-tuple-element.26), kind=kOutput, calls=%fused_computation.98 | convolution fusion | flops 2156003328 | bytes 19136512 | tf_op jit(solution)/shard_map/dot_general | solution.py:21
  313.4 6.1 %collective-permute-done.19 = bf16[128,1024]{1,0:T(8,128)(2,1)} collective-permute-done((bf16[128,1024]{1,0:T(8,128)(2,1)}, bf16[128,1024]{1,0:T(8,128)(2,1)}, u32[]{:S(2)}, u32[]{:S(2)}) %collective-permute-start.19) | collective-permute-done | bytes 262176 | tf_op jit(solution)/shard_map/ppermute | solution.py:13
  319.5 12.0 %fusion.90 = bf16[128,1024]{1,0:T(8,128)(2,1)S(1)} fusion(bf16[1,1024,8192]{2,1,0:T(8,128)(2,1)} %param.9, bf16[64,8192]{1,0:T(8,128)(2,1)} %copy-done.19, bf16[32,8192]{1,0:T(8,128)(2,1)} %copy-done.14, bf16[16,8192]{1,0:T(8,128)(2,1)S(1)} %collective-permute-done.6, bf16[16,8192]{1,0:T(8,128)(2,1)S(1)} %get-tuple-element.28, ...), kind=kOutput, calls=%fused_computation.97 | convolution fusion | flops 2156527616 | bytes 19660800 | tf_op jit(solution)/shard_map/dot_general | solution.py:21
  335.0 10.4 %collective-permute-done.40 = bf16[1,128,1024]{2,1,0:T(8,128)(2,1)S(1)} collective-permute-done((bf16[1,128,1024]{2,1,0:T(8,128)(2,1)S(1)}, bf16[1,128,1024]{2,1,0:T(8,128)(2,1)S(1)}, u32[]{:S(2)}, u32[]{:S(2)}) %collective-permute-start.40) | collective-permute-done | bytes 262176 | tf_op jit(solution)/shard_map/ppermute | solution.py:13
  352.6 5.1 fusion.30
  368.0 8.0 %collective-permute-done.45 = bf16[64,2048]{1,0:T(8,128)(2,1)S(1)} collective-permute-done((bf16[64,2048]{1,0:T(8,128)(2,1)S(1)}, bf16[64,2048]{1,0:T(8,128)(2,1)S(1)}, u32[]{:S(2)}, u32[]{:S(2)}) %collective-permute-start.45) | collective-permute-done | bytes 262176 | tf_op jit(solution)/shard_map/ppermute | solution.py:13
  377.9 5.9 %collective-permute-done.42 = bf16[64,2048]{1,0:T(8,128)(2,1)S(1)} collective-permute-done((bf16[64,2048]{1,0:T(8,128)(2,1)S(1)}, bf16[64,2048]{1,0:T(8,128)(2,1)S(1)}, u32[]{:S(2)}, u32[]{:S(2)}) %collective-permute-start.42) | collective-permute-done | bytes 262176 | tf_op jit(solution)/shard_map/ppermute | solution.py:13
  399.5 12.7 %fusion.100 = bf16[128,1024]{1,0:T(8,128)(2,1)} fusion(bf16[1,1024,8192]{2,1,0:T(8,128)(2,1)} %param.9, bf16[64,8192]{1,0:T(8,128)(2,1)} %copy-done.20, bf16[32,8192]{1,0:T(8,128)(2,1)} %collective-permute-done.37, bf16[16,8192]{1,0:T(8,128)(2,1)} %collective-permute-done.36, bf16[16,8192]{1,0:T(8,128)(2,1)S(1)} %get-tuple-element.24), kind=kOutput, calls=%fused_computation.99 | convolution fusion | flops 2156003328 | bytes 19136512 | tf_op jit(solution)/shard_map/dot_general | solution.py:21
  415.8 7.1 %collective-permute-done.63 = bf16[16,8192]{1,0:T(8,128)(2,1)S(1)} collective-permute-done((bf16[16,8192]{1,0:T(8,128)(2,1)S(1)}, bf16[16,8192]{1,0:T(8,128)(2,1)S(1)}, u32[]{:S(2)}, u32[]{:S(2)}) %collective-permute-start.63) | collective-permute-done | bytes 262176 | tf_op jit(solution)/shard_map/ppermute | solution.py:13
  435.0 12.2 %fusion.85 = bf16[128,1024]{1,0:T(8,128)(2,1)} fusion(bf16[1,1024,8192]{2,1,0:T(8,128)(2,1)} %param.9, bf16[64,8192]{1,0:T(8,128)(2,1)S(1)} %collective-permute-done.28, bf16[32,8192]{1,0:T(8,128)(2,1)S(1)} %collective-permute-done.27, bf16[16,8192]{1,0:T(8,128)(2,1)S(1)} %collective-permute-done.26, bf16[16,8192]{1,0:T(8,128)(2,1)S(1)} %get-tuple-element.22, ...), kind=kOutput, calls=%fused_computation.96 | convolution fusion | flops 2156527616 | bytes 19660800 | tf_op jit(solution)/shard_map/dot_general | solution.py:21
  450.9 16.4 %convert_bitcast_fusion = bf16[1,8192,1024]{2,1,0:T(8,128)(2,1)} fusion(bf16[512,8192]{1,0:T(8,128)(2,1)} %constant_dynamic-update-slice_fusion.16, bf16[128,1024]{1,0:T(8,128)(2,1)S(1)} %copy-done.31, bf16[128,1024]{1,0:T(8,128)(2,1)} %get-tuple-element.35, bf16[128,1024]{1,0:T(8,128)(2,1)} %get-tuple-element.33, bf16[128,1024]{1,0:T(8,128)(2,1)S(1)} %copy-done.32), kind=kOutput, calls=%fused_computation.24 | convolution fusion | flops 8602517504 | bytes 26214400 | tf_op jit(solution)/shard_map/dot_general | solution.py:21
  468.3 16.2 %convert_bitcast_fusion.1 = bf16[1,1024,8192]{2,1,0:T(8,128)(2,1)} fusion(bf16[512,8192]{1,0:T(8,128)(2,1)} %constant_dynamic-update-slice_fusion, bf16[128,1024]{1,0:T(8,128)(2,1)S(1)} %copy-done.29, bf16[128,1024]{1,0:T(8,128)(2,1)S(1)} %copy-done.33, bf16[128,1024]{1,0:T(8,128)(2,1)S(1)} %copy-done.34, bf16[128,1024]{1,0:T(8,128)(2,1)S(1)} %copy-done.30), kind=kOutput, calls=%fused_computation.25 | convolution fusion | flops 8602517504 | bytes 26214400 | tf_op jit(solution)/shard_map/dot_general | solution.py:21
  496.1 7.0 %convert_bitcast_fusion.2 = bf16[1,4096,1024]{2,1,0:T(8,128)(2,1)} fusion(bf16[512,4096]{1,0:T(8,128)(2,1)S(1)} %copy-done.39, bf16[256,1024]{1,0:T(8,128)(2,1)S(1)} %convolution_convert_fusion.1, bf16[256,1024]{1,0:T(8,128)(2,1)S(1)} %copy-done.24), kind=kOutput, calls=%fused_computation.26 | convolution fusion | flops 4301258752 | bytes 13631488 | tf_op jit(solution)/shard_map/dot_general | solution.py:21
  506.4 5.4 %collective-permute-done.52 = bf16[64,2048]{1,0:T(8,128)(2,1)S(1)} collective-permute-done((bf16[64,2048]{1,0:T(8,128)(2,1)S(1)}, bf16[64,2048]{1,0:T(8,128)(2,1)S(1)}, u32[]{:S(2)}, u32[]{:S(2)}) %collective-permute-start.52) | collective-permute-done | bytes 262176 | tf_op jit(solution)/shard_map/ppermute | solution.py:13
  (356 shorter events, 192.2 us)
Async XLA Ops:
  3.6 77.1 %collective-permute-start.9 = (bf16[1,2,128,1024]{3,2,1,0:T(8,128)(2,1)S(1)}, bf16[1,2,128,1024]{3,2,1,0:T(8,128)(2,1)S(1)}, u32[]{:S(2)}, u32[]{:S(2)}) collective-permute-start(bf16[1,2,128,1024]{3,2,1,0:T(8,128)(2,1)S(1)} %maximum_bitcast_fusion), channel_id=1, source_target_pairs={{0,8},{1,9},{2,10},{3,11},{4,12},{5,13},{6,14},{7,15},{8,0},{9,1},... | collective-permute-start | bytes 1572872 | tf_op jit(solution)/shard_map/ppermute | solution.py:13
  18.9 127.4 %collective-permute-start.3 = (bf16[64,8192]{1,0:T(8,128)(2,1)}, bf16[64,8192]{1,0:T(8,128)(2,1)}, u32[]{:S(2)}, u32[]{:S(2)}) collective-permute-start(bf16[64,8192]{1,0:T(8,128)(2,1)} %slice.642), channel_id=1, source_target_pairs={{0,1},{1,0},{2,3},{3,2},{4,5},{5,4},{6,7},{7,6},{8,9},{9,8},{10,11... | collective-permute-start | bytes 3145736 | tf_op jit(solution)/shard_map/ppermute | solution.py:13
  35.0 113.4 %collective-permute-start = (bf16[64,8192]{1,0:T(8,128)(2,1)}, bf16[64,8192]{1,0:T(8,128)(2,1)}, u32[]{:S(2)}, u32[]{:S(2)}) collective-permute-start(bf16[64,8192]{1,0:T(8,128)(2,1)} %slice.643), channel_id=1, source_target_pairs={{0,1},{1,0},{2,3},{3,2},{4,5},{5,4},{6,7},{7,6},{8,9},{9,8},{10,11... | collective-permute-start | bytes 3145736 | tf_op jit(solution)/shard_map/ppermute | solution.py:13
  35.5 69.1 %collective-permute-start.29 = (bf16[1,2,128,1024]{3,2,1,0:T(8,128)(2,1)S(1)}, bf16[1,2,128,1024]{3,2,1,0:T(8,128)(2,1)S(1)}, u32[]{:S(2)}, u32[]{:S(2)}) collective-permute-start(bf16[1,2,128,1024]{3,2,1,0:T(8,128)(2,1)S(1)} %maximum_bitcast_fusion.1), channel_id=1, source_target_pairs={{0,8},{1,9},{2,10},{3,11},{4,12},{5,13},{6,14},{7,15},{8,0},{9,1},... | collective-permute-start | bytes 1572872 | tf_op jit(solution)/shard_map/ppermute | solution.py:13
  36.7 34.7 %collective-permute-start.66 = (bf16[32,4096]{1,0:T(8,128)(2,1)S(1)}, bf16[32,4096]{1,0:T(8,128)(2,1)S(1)}, u32[]{:S(2)}, u32[]{:S(2)}) collective-permute-start(bf16[32,4096]{1,0:T(8,128)(2,1)S(1)} %bitcast.129), channel_id=1, source_target_pairs={{0,2},{1,3},{2,0},{3,1},{4,6},{5,7},{6,4},{7,5},{8,10},{9,11},{10,... | collective-permute-start | bytes 786440 | tf_op jit(solution)/shard_map/ppermute | solution.py:13
  79.8 70.4 %collective-permute-start.23 = (bf16[64,8192]{1,0:T(8,128)(2,1)}, bf16[64,8192]{1,0:T(8,128)(2,1)}, u32[]{:S(2)}, u32[]{:S(2)}) collective-permute-start(bf16[64,8192]{1,0:T(8,128)(2,1)} %slice.638), channel_id=1, source_target_pairs={{0,1},{1,0},{2,3},{3,2},{4,5},{5,4},{6,7},{7,6},{8,9},{9,8},{10,11... | collective-permute-start | bytes 3145736 | tf_op jit(solution)/shard_map/ppermute | solution.py:13
  80.7 72.9 %collective-permute-start.20 = (bf16[64,8192]{1,0:T(8,128)(2,1)}, bf16[64,8192]{1,0:T(8,128)(2,1)}, u32[]{:S(2)}, u32[]{:S(2)}) collective-permute-start(bf16[64,8192]{1,0:T(8,128)(2,1)} %slice.639), channel_id=1, source_target_pairs={{0,1},{1,0},{2,3},{3,2},{4,5},{5,4},{6,7},{7,6},{8,9},{9,8},{10,11... | collective-permute-start | bytes 3145736 | tf_op jit(solution)/shard_map/ppermute | solution.py:13
  104.6 28.0 %collective-permute-start.67 = (bf16[64,4096]{1,0:T(8,128)(2,1)}, bf16[64,4096]{1,0:T(8,128)(2,1)S(1)}, u32[]{:S(2)}, u32[]{:S(2)}) collective-permute-start(bf16[64,4096]{1,0:T(8,128)(2,1)} %pad_maximum_fusion.20), channel_id=1, source_target_pairs={{0,4},{1,5},{2,6},{3,7},{4,0},{5,1},{6,2},{7,3},{8,12},{9,13},{10,... | collective-permute-start | bytes 1572872 | tf_op jit(solution)/shard_map/ppermute | solution.py:13
  153.6 39.1 %collective-permute-start.68 = (bf16[128,4096]{1,0:T(8,128)(2,1)S(1)}, bf16[128,4096]{1,0:T(8,128)(2,1)S(1)}, u32[]{:S(2)}, u32[]{:S(2)}) collective-permute-start(bf16[128,4096]{1,0:T(8,128)(2,1)S(1)} %pad_maximum_fusion.8), channel_id=1, source_target_pairs={{0,1},{1,0},{2,3},{3,2},{4,5},{5,4},{6,7},{7,6},{8,9},{9,8},{10,11... | collective-permute-start | bytes 3145736 | tf_op jit(solution)/shard_map/ppermute | solution.py:13
  155.9 37.6 %collective-permute-start.71 = (bf16[128,4096]{1,0:T(8,128)(2,1)S(1)}, bf16[128,4096]{1,0:T(8,128)(2,1)S(1)}, u32[]{:S(2)}, u32[]{:S(2)}) collective-permute-start(bf16[128,4096]{1,0:T(8,128)(2,1)S(1)} %pad_maximum_fusion.9), channel_id=1, source_target_pairs={{0,1},{1,0},{2,3},{3,2},{4,5},{5,4},{6,7},{7,6},{8,9},{9,8},{10,11... | collective-permute-start | bytes 3145736 | tf_op jit(solution)/shard_map/ppermute | solution.py:13
  156.6 14.9 %collective-permute-start.4 = (bf16[32,8192]{1,0:T(8,128)(2,1)S(1)}, bf16[32,8192]{1,0:T(8,128)(2,1)S(1)}, u32[]{:S(2)}, u32[]{:S(2)}) collective-permute-start(bf16[32,8192]{1,0:T(8,128)(2,1)S(1)} %slice.654), channel_id=1, source_target_pairs={{0,2},{1,3},{2,0},{3,1},{4,6},{5,7},{6,4},{7,5},{8,10},{9,11},{10,... | collective-permute-start | bytes 1572872 | tf_op jit(solution)/shard_map/ppermute | solution.py:13
  158.2 23.6 %collective-permute-start.24 = (bf16[32,8192]{1,0:T(8,128)(2,1)S(1)}, bf16[32,8192]{1,0:T(8,128)(2,1)S(1)}, u32[]{:S(2)}, u32[]{:S(2)}) collective-permute-start(bf16[32,8192]{1,0:T(8,128)(2,1)S(1)} %copy-done.25), channel_id=1, source_target_pairs={{0,2},{1,3},{2,0},{3,1},{4,6},{5,7},{6,4},{7,5},{8,10},{9,11},{10,... | collective-permute-start | bytes 1572872 | tf_op jit(solution)/shard_map/ppermute | solution.py:13
  172.1 17.1 %collective-permute-start.5 = (bf16[16,8192]{1,0:T(8,128)(2,1)S(1)}, bf16[16,8192]{1,0:T(8,128)(2,1)S(1)}, u32[]{:S(2)}, u32[]{:S(2)}) collective-permute-start(bf16[16,8192]{1,0:T(8,128)(2,1)S(1)} %slice.666), channel_id=1, source_target_pairs={{0,4},{1,5},{2,6},{3,7},{4,0},{5,1},{6,2},{7,3},{8,12},{9,13},{10,... | collective-permute-start | bytes 786440 | tf_op jit(solution)/shard_map/ppermute | solution.py:13
  186.3 37.9 %collective-permute-start.14 = (bf16[32,8192]{1,0:T(8,128)(2,1)S(1)}, bf16[32,8192]{1,0:T(8,128)(2,1)S(1)}, u32[]{:S(2)}, u32[]{:S(2)}) collective-permute-start(bf16[32,8192]{1,0:T(8,128)(2,1)S(1)} %slice.652), channel_id=1, source_target_pairs={{0,2},{1,3},{2,0},{3,1},{4,6},{5,7},{6,4},{7,5},{8,10},{9,11},{10,... | collective-permute-start | bytes 1572872 | tf_op jit(solution)/shard_map/ppermute | solution.py:13
  189.2 35.7 %collective-permute-start.11 = (bf16[32,8192]{1,0:T(8,128)(2,1)S(1)}, bf16[32,8192]{1,0:T(8,128)(2,1)S(1)}, u32[]{:S(2)}, u32[]{:S(2)}) collective-permute-start(bf16[32,8192]{1,0:T(8,128)(2,1)S(1)} %slice.653), channel_id=1, source_target_pairs={{0,4},{1,5},{2,6},{3,7},{4,0},{5,1},{6,2},{7,3},{8,12},{9,13},{10,... | collective-permute-start | bytes 1572872 | tf_op jit(solution)/shard_map/ppermute | solution.py:13
  191.0 35.7 %collective-permute-start.34 = (bf16[32,8192]{1,0:T(8,128)(2,1)S(1)}, bf16[32,8192]{1,0:T(8,128)(2,1)S(1)}, u32[]{:S(2)}, u32[]{:S(2)}) collective-permute-start(bf16[32,8192]{1,0:T(8,128)(2,1)S(1)} %slice.648), channel_id=1, source_target_pairs={{0,2},{1,3},{2,0},{3,1},{4,6},{5,7},{6,4},{7,5},{8,10},{9,11},{10,... | collective-permute-start | bytes 1572872 | tf_op jit(solution)/shard_map/ppermute | solution.py:13
  192.6 62.3 %collective-permute-start.31 = (bf16[32,8192]{1,0:T(8,128)(2,1)S(1)}, bf16[32,8192]{1,0:T(8,128)(2,1)S(1)}, u32[]{:S(2)}, u32[]{:S(2)}) collective-permute-start(bf16[32,8192]{1,0:T(8,128)(2,1)S(1)} %slice.649), channel_id=1, source_target_pairs={{0,4},{1,5},{2,6},{3,7},{4,0},{5,1},{6,2},{7,3},{8,12},{9,13},{10,... | collective-permute-start | bytes 1572872 | tf_op jit(solution)/shard_map/ppermute | solution.py:13
  193.5 23.7 %collective-permute-start.54 = (bf16[16,8192]{1,0:T(8,128)(2,1)S(1)}, bf16[16,8192]{1,0:T(8,128)(2,1)S(1)}, u32[]{:S(2)}, u32[]{:S(2)}) collective-permute-start(bf16[16,8192]{1,0:T(8,128)(2,1)S(1)} %get-tuple-element.12), channel_id=1, source_target_pairs={{0,2},{1,3},{2,0},{3,1},{4,6},{5,7},{6,4},{7,5},{8,10},{9,11},{10,... | collective-permute-start | bytes 786440 | tf_op jit(solution)/shard_map/ppermute | solution.py:13
  223.6 172.9 %collective-permute-start.25 = (bf16[16,8192]{1,0:T(8,128)(2,1)}, bf16[16,8192]{1,0:T(8,128)(2,1)}, u32[]{:S(2)}, u32[]{:S(2)}) collective-permute-start(bf16[16,8192]{1,0:T(8,128)(2,1)} %slice.662), channel_id=1, source_target_pairs={{0,4},{1,5},{2,6},{3,7},{4,0},{5,1},{6,2},{7,3},{8,12},{9,13},{10,... | collective-permute-start | bytes 786440 | tf_op jit(solution)/shard_map/ppermute | solution.py:13
  224.2 172.4 %collective-permute-start.22 = (bf16[16,8192]{1,0:T(8,128)(2,1)}, bf16[16,8192]{1,0:T(8,128)(2,1)}, u32[]{:S(2)}, u32[]{:S(2)}) collective-permute-start(bf16[16,8192]{1,0:T(8,128)(2,1)} %slice.663), channel_id=1, source_target_pairs={{0,2},{1,3},{2,0},{3,1},{4,6},{5,7},{6,4},{7,5},{8,10},{9,11},{10,... | collective-permute-start | bytes 786440 | tf_op jit(solution)/shard_map/ppermute | solution.py:13
  224.8 15.8 %collective-permute-start.55 = (bf16[32,8192]{1,0:T(8,128)(2,1)S(1)}, bf16[32,8192]{1,0:T(8,128)(2,1)S(1)}, u32[]{:S(2)}, u32[]{:S(2)}) collective-permute-start(bf16[32,8192]{1,0:T(8,128)(2,1)S(1)} %pad_maximum_fusion.16), channel_id=1, source_target_pairs={{0,4},{1,5},{2,6},{3,7},{4,0},{5,1},{6,2},{7,3},{8,12},{9,13},{10,... | collective-permute-start | bytes 1572872 | tf_op jit(solution)/shard_map/ppermute | solution.py:13
  251.7 28.8 %collective-permute-start.35 = (bf16[16,8192]{1,0:T(8,128)(2,1)S(1)}, bf16[16,8192]{1,0:T(8,128)(2,1)S(1)}, u32[]{:S(2)}, u32[]{:S(2)}) collective-permute-start(bf16[16,8192]{1,0:T(8,128)(2,1)S(1)} %slice.660), channel_id=1, source_target_pairs={{0,4},{1,5},{2,6},{3,7},{4,0},{5,1},{6,2},{7,3},{8,12},{9,13},{10,... | collective-permute-start | bytes 786440 | tf_op jit(solution)/shard_map/ppermute | solution.py:13
  288.4 19.5 %collective-permute-start.60 = (bf16[16,8192]{1,0:T(8,128)(2,1)S(1)}, bf16[16,8192]{1,0:T(8,128)(2,1)}, u32[]{:S(2)}, u32[]{:S(2)}) collective-permute-start(bf16[16,8192]{1,0:T(8,128)(2,1)S(1)} %get-tuple-element.8), channel_id=1, source_target_pairs={{0,2},{1,3},{2,0},{3,1},{4,6},{5,7},{6,4},{7,5},{8,10},{9,11},{10,... | collective-permute-start | bytes 786440 | tf_op jit(solution)/shard_map/ppermute | solution.py:13
  291.8 19.3 %collective-permute-start.36 = (bf16[16,8192]{1,0:T(8,128)(2,1)S(1)}, bf16[16,8192]{1,0:T(8,128)(2,1)}, u32[]{:S(2)}, u32[]{:S(2)}) collective-permute-start(bf16[16,8192]{1,0:T(8,128)(2,1)S(1)} %get-tuple-element.24), channel_id=1, source_target_pairs={{0,4},{1,5},{2,6},{3,7},{4,0},{5,1},{6,2},{7,3},{8,12},{9,13},{10,... | collective-permute-start | bytes 786440 | tf_op jit(solution)/shard_map/ppermute | solution.py:13
  309.7 49.4 %collective-permute-start.61 = (bf16[32,8192]{1,0:T(8,128)(2,1)}, bf16[32,8192]{1,0:T(8,128)(2,1)}, u32[]{:S(2)}, u32[]{:S(2)}) collective-permute-start(bf16[32,8192]{1,0:T(8,128)(2,1)} %pad_maximum_fusion.18), channel_id=1, source_target_pairs={{0,4},{1,5},{2,6},{3,7},{4,0},{5,1},{6,2},{7,3},{8,12},{9,13},{10,... | collective-permute-start | bytes 1572872 | tf_op jit(solution)/shard_map/ppermute | solution.py:13
  312.9 50.0 %collective-permute-start.37 = (bf16[32,8192]{1,0:T(8,128)(2,1)}, bf16[32,8192]{1,0:T(8,128)(2,1)}, u32[]{:S(2)}, u32[]{:S(2)}) collective-permute-start(bf16[32,8192]{1,0:T(8,128)(2,1)} %pad_maximum_fusion.13), channel_id=1, source_target_pairs={{0,2},{1,3},{2,0},{3,1},{4,6},{5,7},{6,4},{7,5},{8,10},{9,11},{10,... | collective-permute-start | bytes 1572872 | tf_op jit(solution)/shard_map/ppermute | solution.py:13
  362.9 31.5 %collective-permute-start.62 = (bf16[64,8192]{1,0:T(8,128)(2,1)S(1)}, bf16[64,8192]{1,0:T(8,128)(2,1)S(1)}, u32[]{:S(2)}, u32[]{:S(2)}) collective-permute-start(bf16[64,8192]{1,0:T(8,128)(2,1)S(1)} %pad_maximum_fusion.6), channel_id=1, source_target_pairs={{0,1},{1,0},{2,3},{3,2},{4,5},{5,4},{6,7},{7,6},{8,9},{9,8},{10,11... | collective-permute-start | bytes 3145736 | tf_op jit(solution)/shard_map/ppermute | solution.py:13
  366.0 29.4 %collective-permute-start.38 = (bf16[64,8192]{1,0:T(8,128)(2,1)S(1)}, bf16[64,8192]{1,0:T(8,128)(2,1)S(1)}, u32[]{:S(2)}, u32[]{:S(2)}) collective-permute-start(bf16[64,8192]{1,0:T(8,128)(2,1)S(1)} %pad_maximum_fusion.3), channel_id=1, source_target_pairs={{0,1},{1,0},{2,3},{3,2},{4,5},{5,4},{6,7},{7,6},{8,9},{9,8},{10,11... | collective-permute-start | bytes 3145736 | tf_op jit(solution)/shard_map/ppermute | solution.py:13
  398.9 16.5 %collective-permute-start.26 = (bf16[16,8192]{1,0:T(8,128)(2,1)S(1)}, bf16[16,8192]{1,0:T(8,128)(2,1)S(1)}, u32[]{:S(2)}, u32[]{:S(2)}) collective-permute-start(bf16[16,8192]{1,0:T(8,128)(2,1)S(1)} %get-tuple-element.22), channel_id=1, source_target_pairs={{0,4},{1,5},{2,6},{3,7},{4,0},{5,1},{6,2},{7,3},{8,12},{9,13},{10,... | collective-permute-start | bytes 786440 | tf_op jit(solution)/shard_map/ppermute | solution.py:13
  412.2 22.7 %collective-permute-start.39 = (bf16[128,1024]{1,0:T(8,128)(2,1)}, bf16[128,1024]{1,0:T(8,128)(2,1)}, u32[]{:S(2)}, u32[]{:S(2)}) collective-permute-start(bf16[128,1024]{1,0:T(8,128)(2,1)} %fusion.100), channel_id=1, source_target_pairs={{0,8},{1,9},{2,10},{3,11},{4,12},{5,13},{6,14},{7,15},{8,0},{9,1},... | collective-permute-start | bytes 786440 | tf_op jit(solution)/shard_map/ppermute | solution.py:13
  433.2 15.4 %collective-permute-start.65 = (bf16[64,8192]{1,0:T(8,128)(2,1)}, bf16[64,8192]{1,0:T(8,128)(2,1)}, u32[]{:S(2)}, u32[]{:S(2)}) collective-permute-start(bf16[64,8192]{1,0:T(8,128)(2,1)} %pad_maximum_fusion.7), channel_id=1, source_target_pairs={{0,1},{1,0},{2,3},{3,2},{4,5},{5,4},{6,7},{7,6},{8,9},{9,8},{10,11... | collective-permute-start | bytes 3145736 | tf_op jit(solution)/shard_map/ppermute | solution.py:13
  447.1 39.6 %collective-permute-start.47 = (bf16[1,128,1024]{2,1,0:T(8,128)(2,1)}, bf16[1,128,1024]{2,1,0:T(8,128)(2,1)S(1)}, u32[]{:S(2)}, u32[]{:S(2)}) collective-permute-start(bf16[1,128,1024]{2,1,0:T(8,128)(2,1)} %bitcast.25), channel_id=1, source_target_pairs={{0,8},{1,9},{2,10},{3,11},{4,12},{5,13},{6,14},{7,15},{8,0},{9,1},... | collective-permute-start | bytes 786440 | tf_op jit(solution)/shard_map/ppermute | solution.py:13
  (81 other events, 787.3 us)

commit v2 on v1

v2 whole, which is shorter than its diff:
```python
import jax
import jax.numpy as jnp
from jax import lax
from jax.experimental import pallas as pl
from jax.experimental.pallas import tpu as pltpu
from jax.sharding import PartitionSpec as P

CORE, NEAR, FAR = 1, 2, 4
SHARES = 8
GROUP = 16


def swap(value, mask):
    count = lax.axis_size("gx")
    return lax.ppermute(value, "gx", [(at, at ^ mask) for at in range(count)])


def gelu_tanh(value):
    return jax.nn.gelu(value, approximate=True)


def contract(left, right, left_dim, right_dim):
    return lax.dot_general(
        left, right, (((left_dim,), (right_dim,)), ((), ())), preferred_element_type=jnp.float32
    )


def tie(values, after):
    return lax.optimization_barrier((values, after))[0]


def gather(value, masks):
    for mask in masks:
        value = jnp.concatenate([value, swap(value, mask)], axis=0)
    return value


def scatter(value, masks):
    for mask in masks:
        half = value.shape[0] // 2
        sent = value[half:].astype(jnp.bfloat16)
        value = value[:half].astype(jnp.float32) + swap(sent, mask).astype(jnp.float32)
    return value


NEAR_FAR = (CORE, NEAR, FAR)
FAR_NEAR = (CORE, FAR, NEAR)


def offset_of(place, order):
    total = jnp.zeros_like(place)
    for at, mask in enumerate(order):
        total = total + mask * ((place >> (2 - at)) & 1)
    return total


def place_of(offset, order):
    total = jnp.zeros_like(offset)
    for at, mask in enumerate(order):
        total = total + jnp.where((offset & mask) != 0, 1 << (2 - at), 0)
    return total


def picked(source, value):
    columns = lax.broadcasted_iota(jnp.int32, (source.shape[0], value.shape[0]), 1)
    chooser = (source[:, None] == columns).astype(jnp.bfloat16)
    return contract(chooser, value, 1, 0).astype(jnp.bfloat16)


def estimate():
    return pl.CostEstimate(flops=1, bytes_accessed=1, transcendentals=0)


def params():
    return pltpu.CompilerParams(
        dimension_semantics=("arbitrary",), vmem_limit_bytes=44 * 1024 * 1024
    )


def tile_of(size, most):
    return most if size % most == 0 else size


def whole_block(part):
    return pl.BlockSpec(part.shape, lambda at: (0,) * part.ndim)


def hidden_parts(rows_in, rows_grad, up_block, down_block):
    count, depth = rows_in.shape
    width = up_block.shape[1]
    tile = tile_of(width, 1024)
    half = count // 2

    def kernel(in_ref, grad_ref, up_ref, down_ref, keep_ref, send_ref):
        pre = jnp.dot(in_ref[...], up_ref[...], preferred_element_type=jnp.float32)
        keep_ref[0] = pre[:half]
        send_ref[0] = pre[half:].astype(jnp.bfloat16)
        hidden = contract(grad_ref[...], down_ref[...], 1, 1)
        keep_ref[1] = hidden[:half]
        send_ref[1] = hidden[half:].astype(jnp.bfloat16)

    results = (
        jax.ShapeDtypeStruct((2, half, width), jnp.float32),
        jax.ShapeDtypeStruct((2, half, width), jnp.bfloat16),
    )
    operands = (rows_in, rows_grad, up_block, down_block)
    return pl.pallas_call(
        kernel,
        grid=(width // tile,),
        in_specs=[
            whole_block(rows_in),
            whole_block(rows_grad),
            pl.BlockSpec((depth, tile), lambda at: (0, at)),
            pl.BlockSpec((tile, depth), lambda at: (at, 0)),
        ],
        out_specs=[pl.BlockSpec((2, half, tile), lambda at: (0, 0, at))] * 2,
        out_shape=results,
        compiler_params=params(),
        cost_estimate=estimate(),
        name="hidden_parts",
    )(*operands)


def joined(pieces):
    if pieces[0].shape[0] % 16:
        return [jnp.concatenate(pieces, axis=0)]
    return pieces


def input_part(pieces, up_block):
    pieces = joined(pieces)
    count = sum(piece.shape[0] for piece in pieces)
    depth, width = up_block.shape
    tile = tile_of(width, 1024)

    def kernel(*refs):
        up_ref, out_ref = refs[-2:]
        rows = jnp.concatenate([ref[...] for ref in refs[:-2]], axis=0)
        part = contract(rows, up_ref[...], 1, 1)

        @pl.when(pl.program_id(0) == 0)
        def _():
            out_ref[...] = part

        @pl.when(pl.program_id(0) != 0)
        def _():
            out_ref[...] += part

    result = jax.ShapeDtypeStruct((count, depth), jnp.float32)
    operands = (*pieces, up_block)
    return pl.pallas_call(
        kernel,
        grid=(width // tile,),
        in_specs=[pl.BlockSpec((part.shape[0], tile), lambda at: (0, at)) for part in operands],
        out_specs=whole_block(result),
        out_shape=result,
        compiler_params=params(),
        cost_estimate=estimate(),
        name="input_part",
    )(*operands)


def up_gradient(turned, pieces):
    pieces = joined(pieces)
    depth, count = turned.shape
    width = pieces[0].shape[1]
    tile = tile_of(width, 512)

    def kernel(turned_ref, *refs):
        rows = jnp.concatenate([ref[...] for ref in refs[:-2]], axis=0)
        refs[-1][...] = jnp.zeros_like(refs[-1])
        refs[-2][...] = jnp.dot(
            turned_ref[...], rows, preferred_element_type=jnp.float32
        ).astype(jnp.bfloat16)

    result = jax.ShapeDtypeStruct((depth, width), jnp.bfloat16)
    mark = jax.ShapeDtypeStruct((8, 128), jnp.float32)
    operands = (turned, *pieces)
    return pl.pallas_call(
        kernel,
        grid=(width // tile,),
        in_specs=[whole_block(turned)]
        + [pl.BlockSpec((piece.shape[0], tile), lambda at: (0, at)) for piece in pieces],
        out_specs=(pl.BlockSpec((depth, tile), lambda at: (0, at)), whole_block(mark)),
        out_shape=(result, mark),
        compiler_params=params(),
        cost_estimate=estimate(),
        name="up_gradient",
    )(*operands)


def down_gradient(pieces, rows_grad):
    pieces = joined(pieces)
    count, depth = rows_grad.shape
    width = pieces[0].shape[1]
    tile = tile_of(width, 512)

    def kernel(grad_ref, *refs):
        rows = jnp.concatenate([ref[...] for ref in refs[:-2]], axis=0)
        refs[-1][...] = jnp.zeros_like(refs[-1])
        refs[-2][...] = contract(rows, grad_ref[...], 0, 0).astype(jnp.bfloat16)

    result = jax.ShapeDtypeStruct((width, depth), jnp.bfloat16)
    mark = jax.ShapeDtypeStruct((8, 128), jnp.float32)
    operands = (rows_grad, *pieces)
    return pl.pallas_call(
        kernel,
        grid=(width // tile,),
        in_specs=[whole_block(rows_grad)]
        + [pl.BlockSpec((piece.shape[0], tile), lambda at: (0, at)) for piece in pieces],
        out_specs=(pl.BlockSpec((tile, depth), lambda at: (at, 0)), whole_block(mark)),
        out_shape=(result, mark),
        compiler_params=params(),
        cost_estimate=estimate(),
        name="down_gradient",
    )(*operands)


def body(input_tiles, grad_tiles, context_tiles, up_tiles, down_tiles, output_tiles):
    grid_index = lax.axis_index("gx")
    total_bits = lax.axis_size("gx").bit_length() - 1
    q_masks = [1 << bit for bit in range(3, total_bits)]
    own_p = grid_index & (SHARES - 1)
    own_q = grid_index >> 3
    inputs = input_tiles[0]
    grads = grad_tiles[0]
    context = context_tiles[0]
    up_block = up_tiles[0]
    down_block = down_tiles[0]
    proj_block = output_tiles[0]
    rows = inputs.shape[0]
    half_rows = rows // 2
    share_rows = half_rows // SHARES
    block_rows = context.shape[0]
    half_block = block_rows // 2
    q_count = 1 << len(q_masks)

    def half_source(order):
        at = jnp.arange(rows, dtype=jnp.int32)
        half, at = at // half_rows, at % half_rows
        share = own_p ^ offset_of(at // share_rows, order)
        inside = share * share_rows + at % share_rows
        return (inside // GROUP) * 2 * GROUP + half * GROUP + inside % GROUP

    def token_source(half, order):
        at = jnp.arange(SHARES * half_block, dtype=jnp.int32)
        block = own_p ^ offset_of(at // half_block, order)
        at = at % half_block
        token = block * block_rows + (at // GROUP) * 2 * GROUP + half * GROUP + at % GROUP
        local = token % rows
        inside = (local // (2 * GROUP)) * GROUP + local % GROUP
        place = place_of(own_p ^ (inside // share_rows), NEAR_FAR)
        return ((token // rows) ^ own_q) * half_rows + place * share_rows + inside % share_rows

    source_nf = half_source(NEAR_FAR)
    inputs_nf = picked(source_nf, inputs)
    grads_nf = picked(source_nf, grads)
    grads_fn = picked(half_source(FAR_NEAR), grads)

    def q_gather(value):
        value = value[None]
        for mask in q_masks:
            value = jnp.concatenate([value, swap(value, mask)], axis=0)
        return value

    chunks = {}
    pairs = []
    for half in range(2):
        at = slice(half * half_rows, (half + 1) * half_rows)
        pairs.append(q_gather(jnp.stack([inputs_nf[at], grads_fn[at]])))
        chunks["own", half] = inputs_nf[at], grads_fn[at]

    state = {}
    late = [()]

    def held(values):
        return tie(values, late[0])

    def sums(name):
        if name[0] == "other":
            pair = held(pairs[name[1]][1:])
            chunks[name] = tuple(
                pair[:, which].reshape((q_count - 1) * half_rows, -1) for which in range(2)
            )
        chunk_in, chunk_grad = held(chunks[name])
        keep, send = hidden_parts(chunk_in, chunk_grad, up_block, down_block)
        state[name] = keep, swap(send, CORE)
        late[0] = send

    def summed(parts, which, at):
        keep, recv, *more = parts
        total = keep[which, at] + recv[which, at].astype(jnp.float32)
        for part in more:
            total = total + part[which][at].astype(jnp.float32)
        return total

    def halved(parts, which):
        count = parts[-1][which].shape[0] // 2
        return summed(parts, which, slice(count, 2 * count)).astype(jnp.bfloat16)

    def sums_core(name):
        parts = held(state[name])
        send = halved(parts, 0), halved(parts, 1)
        state[name] = *parts, (swap(send[0], NEAR), swap(send[1], FAR))
        late[0] = send

    def sums_one(name):
        parts = held(state[name])
        send = halved(parts, 0), halved(parts, 1)
        state[name] = *parts, (swap(send[0], FAR), swap(send[1], NEAR))
        late[0] = send

    def gelu(name):
        parts = held(state[name])
        at = slice(0, parts[-1][0].shape[0])
        act, gelu_back = jax.vjp(gelu_tanh, summed(parts, 0, at))
        dpre = gelu_back(summed(parts, 1, at))[0].astype(jnp.bfloat16)
        act = act.astype(jnp.bfloat16)
        state[name] = dpre, act, swap(dpre, FAR), swap(act, NEAR)
        late[0] = dpre, act

    def spread_one(name):
        dpre, act, dpre_recv, act_recv = held(state[name])
        dpre = jnp.concatenate([dpre, dpre_recv], axis=0)
        act = jnp.concatenate([act, act_recv], axis=0)
        state[name] = swap(dpre, NEAR), swap(act, FAR)
        dpre_rows[name] = [dpre, swap(dpre, CORE)]
        act_rows[name] = [act, swap(act, CORE)]
        late[0] = dpre, act

    act_rows, dpre_rows, input_parts = {}, {}, {}

    def spread_two(name):
        dpre, act = held(state[name])
        first, far = dpre_rows[name]
        dpre_rows[name] = [first, dpre, far, swap(dpre, CORE)]
        first, far = act_rows[name]
        act_rows[name] = [first, act, far, swap(act, CORE)]
        late[0] = dpre, act

    q_state, d_input_own, d_input_rows, d_context_halves = {}, {}, {}, {}

    def back(name):
        dpre_rows[name] = held(dpre_rows[name])
        part = input_part(dpre_rows[name], up_block)
        input_parts[name] = part
        late[0] = part[:8, :128]
        if name[0] == "other" and q_count == 2:
            sent = part.astype(jnp.bfloat16)
            q_state[name[1]] = swap(sent, q_masks[0])
            late[0] = sent

    def own_rows(half):
        own = input_parts["own", half]
        if q_count == 2:
            own, recv = held((own, q_state[half]))
            share = own + recv.astype(jnp.float32)
        else:
            other = input_parts["other", half].reshape(q_count - 1, half_rows, -1)
            share = scatter(jnp.concatenate([own[None], other], axis=0), q_masks[::-1])[0]
        at = slice(half * half_rows, (half + 1) * half_rows)
        d_input = (grads_nf[at].astype(jnp.float32) + share).astype(jnp.bfloat16)
        d_input_own[half] = d_input
        q_state[half] = q_gather(d_input)
        late[0] = d_input

    context_orders = (FAR_NEAR, NEAR_FAR)

    def context_sums(half):
        gathered = held(q_state[half]).reshape(q_count * half_rows, -1)
        by_order = {
            order: picked(token_source(half, order), gathered) for order in (NEAR_FAR, FAR_NEAR)
        }
        d_input_rows[half] = by_order[context_orders[half]]
        columns = proj_block.shape[0] // 2
        first = contract(by_order[NEAR_FAR], proj_block[:columns], 1, 1)
        second = contract(by_order[FAR_NEAR], proj_block[columns:], 1, 1)
        at = first.shape[0] // 2
        sent = jnp.concatenate([first[at:], second[at:]], axis=1).astype(jnp.bfloat16)
        q_state[half] = (first, second), swap(sent, CORE)
        late[0] = sent

    def context_summed(parts, which, at):
        full, recv, *more = parts
        columns = full[which].shape[1]
        here = slice(which * columns, (which + 1) * columns)
        total = full[which][at] + recv[at, here].astype(jnp.float32)
        for part in more:
            total = total + part[which][at].astype(jnp.float32)
        return total

    def context_halved(parts, which, count):
        return context_summed(parts, which, slice(count, 2 * count)).astype(jnp.bfloat16)

    def context_core(half):
        parts = held(q_state[half])
        count = parts[1].shape[0] // 2
        sent = context_halved(parts, 0, count), context_halved(parts, 1, count)
        q_state[half] = *parts, (swap(sent[0], NEAR), swap(sent[1], FAR))
        late[0] = sent

    def context_one(half):
        parts = held(q_state[half])
        count = parts[1].shape[0] // 4
        sent = context_halved(parts, 0, count), context_halved(parts, 1, count)
        q_state[half] = *parts, (swap(sent[0], FAR), swap(sent[1], NEAR))
        late[0] = sent

    def context_two(half):
        parts = held(q_state[half])
        at = slice(0, parts[1].shape[0] // 4)
        first, second = context_summed(parts, 0, at), context_summed(parts, 1, at)
        d_context_halves[half] = jnp.concatenate([first, second], axis=1).astype(jnp.bfloat16)
        late[0] = d_context_halves[half]

    saved = {}

    def saved_start():
        halves = held(context).reshape(block_rows // (2 * GROUP), 2, GROUP, -1)
        halves = [halves[:, half].reshape(half_block, -1) for half in range(2)]
        saved["rows"] = halves
        saved["recv"] = swap(halves[0], NEAR), swap(halves[1], FAR)

    def saved_next(masks):
        halves, recv = held((saved["rows"], saved["recv"]))
        halves = [
            jnp.concatenate([mine, theirs], axis=0) for mine, theirs in zip(halves, recv)
        ]
        saved["rows"] = halves
        if masks:
            saved["recv"] = [swap(rows, mask) for rows, mask in zip(halves, masks)]
        late[0] = halves

    own0, other0, other1, own1 = ("own", 0), ("other", 0), ("other", 1), ("own", 1)
    order = [own0, other0, other1, own1]
    sums(own0)
    sums_core(own0)
    sums(own1)
    sums_one(own0)
    sums_core(own1)
    saved_start()
    sums(other0)
    gelu(own0)
    sums_one(own1)
    sums_core(other0)
    saved_next((FAR, NEAR))
    sums(other1)
    in_all = held(jnp.concatenate([chunks[name][0] for name in order], axis=0))
    turned = in_all.T
    grad_all = jnp.concatenate([chunks[name][1] for name in order], axis=0)
    late[0] = late[0], turned[:8, :128], grad_all[:8, :128]
    spread_one(own0)
    sums_one(other0)
    sums_core(other1)
    saved_next((CORE, CORE))
    spread_two(own0)
    gelu(other0)
    sums_one(other1)
    back(own0)
    saved_next(())
    spread_one(other0)
    gelu(other1)
    spread_two(other0)
    spread_one(other1)
    gelu(own1)
    back(other0)
    spread_two(other1)
    spread_one(own1)
    own_rows(0)
    back(other1)
    spread_two(own1)
    context_sums(0)
    context_core(0)
    back(own1)
    own_rows(1)
    context_one(0)
    pieces = held([piece for name in order for piece in dpre_rows[name]])
    d_up, late[0] = up_gradient(turned, pieces)
    context_sums(1)
    context_two(0)
    pieces = held([piece for name in order for piece in act_rows[name]])
    d_down, late[0] = down_gradient(pieces, grad_all)
    context_core(1)
    d_input_all = held(jnp.concatenate([d_input_rows[0], d_input_rows[1]], axis=0))
    context_all = jnp.concatenate(saved["rows"], axis=0)
    d_output = contract(context_all, d_input_all, 0, 0).astype(jnp.bfloat16)
    context_one(1)
    context_two(1)

    own_all = jnp.concatenate([d_input_own[0], d_input_own[1]], axis=0)
    columns = lax.broadcasted_iota(jnp.int32, (rows, rows), 1)
    chooser = (source_nf[:, None] == columns).astype(jnp.bfloat16)
    d_input = contract(chooser, own_all, 0, 0).astype(jnp.bfloat16)

    split = [
        d_context_halves[half].reshape(block_rows // (2 * GROUP), 1, GROUP, -1)
        for half in range(2)
    ]
    d_context = jnp.concatenate(split, axis=1).reshape(block_rows, -1)
    return (d_input[None], d_context[None], d_up[None], d_down[None], d_output[None])


def solution(mesh):
    return jax.shard_map(
        body,
        mesh=mesh,
        in_specs=(
            P("gx", "groups", None),
            P("gx", "groups", None),
            P("gx", "groups", None),
            P("gx", None, None),
            P("gx", None, None),
            P("gx", None, None),
        ),
        out_specs=(
            P("gx", "groups", None),
            P("gx", "groups", None),
            P("gx", "groups", None),
            P("gx", "groups", None),
            P("gx", "groups", None),
        ),
        check_vma=False,
    )
```

time: 529 us -> 419 us (0.79)
  matrix products: 201 us -> 34.7 us
  Pallas kernels: 0 us -> 142 us
  waiting for transfers between devices: 175 us -> 130 us
  local copies, waits for them, and re-layouts: 57.3 us -> 22.2 us
    dot_general x25 -> x11, matrix products: 201 us -> 34.7 us  [contract(): lax.dot_general(left, right, (((left_dim,), (right_dim,)), ((), ())), pre...]
    pallas_call x0 -> x10, Pallas kernels: none -> 142 us  [the longest x4 61.9 us: hidden_parts(): pl.pallas_call(kernel, grid=(width // tile,), in_specs=[whole_block(rows_...]
    ppermute x72 -> x74, waiting for transfers between devices: 175 us -> 130 us  [swap(): return lax.ppermute(value, 'gx', [(at, at ^ mask) for at in range(count)])]
    unnamed x111 -> x116, local copies, waits for them, and re-layouts: 30.8 us -> 7.61 us
    convert_element_type x0 -> x20, other arithmetic: none -> 16.8 us  [the longest x8 5.52 us: halved(): return summed(parts, which, slice(count, 2 * count)).astype(jnp.bfloat16)]
    slice x37 -> x5, local copies, waits for them, and re-layouts: 18.9 us -> 3.31 us  [the longest x2 2.11 us: context_sums(): second[at:]]
    add x24 -> x0, other arithmetic: 9.76 us -> none  [scatter(): value[:half].astype(jnp.float32) + swap(sent, mask).astype(jnp.float32)]
    concatenate x20 -> x5, other arithmetic: 10.3 us -> 3.47 us  [the longest x2 1.18 us: context_sums(): jnp.concatenate([first[at:], second[at:]], axis=1).astype(jnp.bfloat16)]
  transfers between devices with their start and end apart: 72 -> 74, of which waited for: 32 -> 25; matrix products, arithmetic and copies ran while one was open for 51% -> 15% of each run, Pallas kernels for 0% -> 31%
where the time goes in v2:
time: 419 us; the launch traced here: 415 us
  Pallas kernels  142 us (34%)
  waiting for transfers between devices  130 us (31%)
  starting transfers between devices  58.4 us (14%)
  matrix products  34.7 us (8%)
  other arithmetic  25.5 us (6%)
  local copies, waits for them, and re-layouts  22.2 us (5%)
    ppermute x74, waiting for transfers between devices, swap(): return lax.ppermute(value, 'gx', [(at, at ^ mask) for at in range(count)])  130 us
    pallas_call x4, Pallas kernels, hidden_parts(): pl.pallas_call(kernel, grid=(width // tile,), in_specs=[whole_block(rows_...  61.9 us
    ppermute x74, starting transfers between devices, swap(): return lax.ppermute(value, 'gx', [(at, at ^ mask) for at in range(count)])  58.4 us
    pallas_call x4, Pallas kernels, input_part(): pl.pallas_call(kernel, grid=(width // tile,), in_specs=[pl.BlockSpec((par...  46 us
    dot_general x11, matrix products, contract(): lax.dot_general(left, right, (((left_dim,), (right_dim,)), ((), ())), pre...  34.7 us
    pallas_call x1, Pallas kernels, down_gradient(): pl.pallas_call(kernel, grid=(width // tile,), in_specs=[whole_block(rows_...  18.5 us
    pallas_call x1, Pallas kernels, up_gradient(): pl.pallas_call(kernel, grid=(width // tile,), in_specs=[whole_block(turne...  16.1 us
  transfers between devices with their start and end apart: 74, of which 25 were waited for; matrix products, arithmetic and copies ran while one was open for 15% of the time, Pallas kernels for 31%

profile of v2, /device:TPU:0, one launch (start us, length us, event | category | flops | bytes accessed | tf_op | source)
XLA Modules:
  0.0 414.8 jit_solution(14962273594512801988)
XLA Ops:
  2.7 15.5 %hidden_parts.4 = (f32[2,64,8192]{2,1,0:T(8,128)S(1)}, bf16[2,64,8192]{2,1,0:T(8,128)(2,1)S(1)}) custom-call(bf16[128,1024]{1,0:T(8,128)(2,1)S(1)} %get-tuple-element.195.in_ref, bf16[128,1024]{1,0:T(8,128)(2,1)S(1)} %get-tuple-element.196.grad_ref, bf16[1024,8192]{1,0:T(8,128)(2,1)} %bitcast.171, bf16[8192,1024]{1,0:T(8,128)(2,1)} %bitcast.179), custom_call_target="tpu_custom_call" | custom-call | flops 1 | bytes 1 | tf_op jit(solution)/shard_map/hidden_parts/pallas_call | solution.py:107
  18.8 3.8 collective-permute-done
  22.8 2.9 collective-permute-start.1
  27.3 15.4 %hidden_parts.5 = (f32[2,64,8192]{2,1,0:T(8,128)S(1)}, bf16[2,64,8192]{2,1,0:T(8,128)(2,1)S(1)}) custom-call(bf16[128,1024]{1,0:T(8,128)(2,1)S(1)} %get-tuple-element.201.in_ref, bf16[128,1024]{1,0:T(8,128)(2,1)S(1)} %get-tuple-element.202.grad_ref, bf16[1024,8192]{1,0:T(8,128)(2,1)} %bitcast.172, bf16[8192,1024]{1,0:T(8,128)(2,1)} %bitcast.180), custom_call_target="tpu_custom_call" | custom-call | flops 1 | bytes 1 | tf_op jit(solution)/shard_map/hidden_parts/pallas_call | solution.py:107
  50.5 30.0 %collective-permute-done.5 = bf16[1,2,128,1024]{3,2,1,0:T(8,128)(2,1)S(1)} collective-permute-done((bf16[1,2,128,1024]{3,2,1,0:T(8,128)(2,1)S(1)}, bf16[1,2,128,1024]{3,2,1,0:T(8,128)(2,1)S(1)}, u32[]{:S(2)}, u32[]{:S(2)}) %collective-permute-start.5) | collective-permute-done | bytes 524320 | tf_op jit(solution)/shard_map/ppermute | solution.py:15
  80.7 15.5 %hidden_parts.6 = (f32[2,64,8192]{2,1,0:T(8,128)S(1)}, bf16[2,64,8192]{2,1,0:T(8,128)(2,1)S(1)}) custom-call(bf16[128,1024]{1,0:T(8,128)(2,1)S(1)} %get-tuple-element.212.in_ref, bf16[128,1024]{1,0:T(8,128)(2,1)S(1)} %get-tuple-element.213.grad_ref, bf16[1024,8192]{1,0:T(8,128)(2,1)} %bitcast.173, bf16[8192,1024]{1,0:T(8,128)(2,1)} %bitcast.181), custom_call_target="tpu_custom_call" | custom-call | flops 1 | bytes 1 | tf_op jit(solution)/shard_map/hidden_parts/pallas_call | solution.py:107
  107.5 7.3 %collective-permute-done.11 = bf16[32,4096]{1,0:T(8,128)(2,1)S(1)} collective-permute-done((bf16[32,4096]{1,0:T(8,128)(2,1)S(1)}, bf16[32,4096]{1,0:T(8,128)(2,1)S(1)}, u32[]{:S(2)}, u32[]{:S(2)}) %collective-permute-start.11) | collective-permute-done | bytes 262176 | tf_op jit(solution)/shard_map/ppermute | solution.py:15
  118.1 15.5 %hidden_parts.7 = (f32[2,64,8192]{2,1,0:T(8,128)S(1)}, bf16[2,64,8192]{2,1,0:T(8,128)(2,1)S(1)}) custom-call(bf16[128,1024]{1,0:T(8,128)(2,1)S(1)} %get-tuple-element.234.in_ref, bf16[128,1024]{1,0:T(8,128)(2,1)S(1)} %get-tuple-element.235.grad_ref, bf16[1024,8192]{1,0:T(8,128)(2,1)} %bitcast.174, bf16[8192,1024]{1,0:T(8,128)(2,1)} %bitcast.182), custom_call_target="tpu_custom_call" | custom-call | flops 1 | bytes 1 | tf_op jit(solution)/shard_map/hidden_parts/pallas_call | solution.py:107
  145.3 3.3 collective-permute-done.18
  153.0 6.8 %collective-permute-done.15.refs_1_ = bf16[32,8192]{1,0:T(8,128)(2,1)S(1)} collective-permute-done((bf16[32,8192]{1,0:T(8,128)(2,1)S(1)}, bf16[32,8192]{1,0:T(8,128)(2,1)S(1)}, u32[]{:S(2)}, u32[]{:S(2)}) %collective-permute-start.15) | collective-permute-done | bytes 524320 | tf_op jit(solution)/shard_map/ppermute | solution.py:15
  160.0 3.5 collective-permute-done.27
  169.2 5.2 %collective-permute-done.28 = bf16[16,8192]{1,0:T(8,128)(2,1)S(1)} collective-permute-done((bf16[16,8192]{1,0:T(8,128)(2,1)S(1)}, bf16[16,8192]{1,0:T(8,128)(2,1)S(1)}, u32[]{:S(2)}, u32[]{:S(2)}) %collective-permute-start.28) | collective-permute-done | bytes 262176 | tf_op jit(solution)/shard_map/ppermute | solution.py:15
  178.4 8.8 %collective-permute-done.24 = bf16[32,8192]{1,0:T(8,128)(2,1)S(1)} collective-permute-done((bf16[32,8192]{1,0:T(8,128)(2,1)S(1)}, bf16[32,8192]{1,0:T(8,128)(2,1)S(1)}, u32[]{:S(2)}, u32[]{:S(2)}) %collective-permute-start.24) | collective-permute-done | bytes 524320 | tf_op jit(solution)/shard_map/ppermute | solution.py:15
  191.8 3.0 collective-permute-done.32
  194.8 6.0 %collective-permute-done.33 = bf16[16,8192]{1,0:T(8,128)(2,1)S(1)} collective-permute-done((bf16[16,8192]{1,0:T(8,128)(2,1)S(1)}, bf16[16,8192]{1,0:T(8,128)(2,1)S(1)}, u32[]{:S(2)}, u32[]{:S(2)}) %collective-permute-start.33) | collective-permute-done | bytes 262176 | tf_op jit(solution)/shard_map/ppermute | solution.py:15
  205.5 3.8 collective-permute-done.38
  217.6 11.4 %input_part.4 = f32[128,1024]{1,0:T(8,128)S(1)} custom-call(bf16[32,8192]{1,0:T(8,128)(2,1)S(1)} %constant_dynamic-update-slice_fusion.4.refs_0_, bf16[32,8192]{1,0:T(8,128)(2,1)S(1)} %collective-permute-done.15.refs_1_, bf16[32,8192]{1,0:T(8,128)(2,1)S(1)} %collective-permute-done.22.refs_2_, bf16[32,8192]{1,0:T(8,128)(2,1)S(1)} %collective-permute-done.23.refs_3_, ...), custom_call_target="tpu_custom_call" | custom-call | flops 1 | bytes 1 | tf_op jit(solution)/shard_map/input_part/pallas_call | solution.py:151
  229.2 11.3 %input_part.5 = f32[128,1024]{1,0:T(8,128)S(1)} custom-call(bf16[32,8192]{1,0:T(8,128)(2,1)S(1)} %constant_dynamic-update-slice_fusion.12.refs_0_.refs_4_, bf16[32,8192]{1,0:T(8,128)(2,1)S(1)} %collective-permute-done.30.refs_1_.refs_5_, bf16[32,8192]{1,0:T(8,128)(2,1)S(1)} %collective-permute-done.34.refs_2_.refs_6_, ...), custom_call_target="tpu_custom_call" | custom-call | flops 1 | bytes 1 | tf_op jit(solution)/shard_map/input_part/pallas_call | solution.py:151
  240.6 3.0 collective-permute-start.40
  248.1 8.1 %collective-permute-done.40 = bf16[128,1024]{1,0:T(8,128)(2,1)S(1)} collective-permute-done((bf16[128,1024]{1,0:T(8,128)(2,1)S(1)}, bf16[128,1024]{1,0:T(8,128)(2,1)S(1)}, u32[]{:S(2)}, u32[]{:S(2)}) %collective-permute-start.40) | collective-permute-done | bytes 262176 | tf_op jit(solution)/shard_map/ppermute | solution.py:15
  257.1 14.8 %collective-permute-done.51 = bf16[1,128,1024]{2,1,0:T(8,128)(2,1)} collective-permute-done((bf16[1,128,1024]{2,1,0:T(8,128)(2,1)}, bf16[1,128,1024]{2,1,0:T(8,128)(2,1)}, u32[]{:S(2)}, u32[]{:S(2)}) %collective-permute-start.51) | collective-permute-done | bytes 262176 | tf_op jit(solution)/shard_map/ppermute | solution.py:15
  273.0 11.7 %input_part.6 = f32[128,1024]{1,0:T(8,128)S(1)} custom-call(bf16[32,8192]{1,0:T(8,128)(2,1)S(1)} %constant_dynamic-update-slice_fusion.16.refs_0_.refs_8_, bf16[32,8192]{1,0:T(8,128)(2,1)} %collective-permute-done.43.refs_1_.refs_9_, bf16[32,8192]{1,0:T(8,128)(2,1)} %collective-permute-done.47.refs_2_.refs_10_, ...), custom_call_target="tpu_custom_call" | custom-call | flops 1 | bytes 1 | tf_op jit(solution)/shard_map/input_part/pallas_call | solution.py:151
  286.6 5.2 %fusion.13 = f32[256,2048]{1,0:T(8,128)} fusion(bf16[1,4096,1024]{2,1,0:T(8,128)(2,1)} %param.11, bf16[256,1024]{1,0:T(8,128)(2,1)} %bitcast.185, s32[256]{0:T(256)S(1)} %get-tuple-element.437), kind=kOutput, calls=%fused_computation.14 | convolution fusion | flops 1208287232 | bytes 6816768 | tf_op jit(solution)/shard_map/dot_general | solution.py:23
  291.7 3.8 fusion.9
  300.2 11.5 %input_part.7 = f32[128,1024]{1,0:T(8,128)S(1)} custom-call(bf16[32,8192]{1,0:T(8,128)(2,1)S(1)} %constant_dynamic-update-slice_fusion.20.refs_0_.refs_12_, bf16[32,8192]{1,0:T(8,128)(2,1)} %collective-permute-done.45.refs_1_.refs_13_, bf16[32,8192]{1,0:T(8,128)(2,1)S(1)} %collective-permute-done.49.refs_2_.refs_14_, ...), custom_call_target="tpu_custom_call" | custom-call | flops 1 | bytes 1 | tf_op jit(solution)/shard_map/input_part/pallas_call | solution.py:151
  313.7 13.1 %collective-permute-done.58 = bf16[1,128,1024]{2,1,0:T(8,128)(2,1)S(1)} collective-permute-done((bf16[1,128,1024]{2,1,0:T(8,128)(2,1)S(1)}, bf16[1,128,1024]{2,1,0:T(8,128)(2,1)S(1)}, u32[]{:S(2)}, u32[]{:S(2)}) %collective-permute-start.58) | collective-permute-done | bytes 262176 | tf_op jit(solution)/shard_map/ppermute | solution.py:15
  327.7 5.1 %fusion.7 = f32[256,2048]{1,0:T(8,128)} fusion(bf16[1,4096,1024]{2,1,0:T(8,128)(2,1)} %param.11, bf16[256,1024]{1,0:T(8,128)(2,1)} %bitcast.186, s32[256]{0:T(256)S(1)} %get-tuple-element.440), kind=kOutput, calls=%fused_computation.8 | convolution fusion | flops 1208287232 | bytes 6816768 | tf_op jit(solution)/shard_map/dot_general | solution.py:23
  334.7 3.5 fusion.11
  348.1 18.5 %down_gradient.1 = (bf16[8192,1024]{1,0:T(8,128)(2,1)}, f32[8,128]{1,0:T(8,128)}) custom-call(bf16[512,1024]{1,0:T(8,128)(2,1)S(1)} %pad_maximum_fusion.3.grad_ref, bf16[32,8192]{1,0:T(8,128)(2,1)} %constant_dynamic-update-slice_fusion.6.refs_0_, bf16[32,8192]{1,0:T(8,128)(2,1)} %collective-permute-done.16.refs_1_, ...), custom_call_target="tpu_custom_call" | custom-call | flops 1 | bytes 1 | tf_op jit(solution)/shard_map/down_gradient/pallas_call | solution.py:206
  372.9 16.1 %up_gradient.1 = (bf16[1024,8192]{1,0:T(8,128)(2,1)}, f32[8,128]{1,0:T(8,128)}) custom-call(bf16[1024,512]{1,0:T(8,128)(2,1)S(1)} %copy.12.turned_ref, bf16[32,8192]{1,0:T(8,128)(2,1)S(1)} %constant_dynamic-update-slice_fusion.4.refs_0_, bf16[32,8192]{1,0:T(8,128)(2,1)S(1)} %copy-done.6, bf16[32,8192]{1,0:T(8,128)(2,1)S(1)} %copy-done.10, ...), custom_call_target="tpu_custom_call" | custom-call | flops 1 | bytes 1 | tf_op jit(solution)/shard_map/up_gradient/pallas_call | solution.py:179
  394.4 4.8 %collective-permute-done.60 = bf16[64,2048]{1,0:T(8,128)(2,1)S(1)} collective-permute-done((bf16[64,2048]{1,0:T(8,128)(2,1)S(1)}, bf16[64,2048]{1,0:T(8,128)(2,1)S(1)}, u32[]{:S(2)}, u32[]{:S(2)}) %collective-permute-start.60) | collective-permute-done | bytes 262176 | tf_op jit(solution)/shard_map/ppermute | solution.py:15
  402.6 10.2 %convert_bitcast_fusion = bf16[1,4096,1024]{2,1,0:T(8,128)(2,1)} fusion(bf16[512,1024]{1,0:T(8,128)(2,1)S(1)} %pad_maximum_fusion.4, bf16[128,4096]{1,0:T(8,128)(2,1)} %collective-permute-done.73, bf16[128,4096]{1,0:T(8,128)(2,1)} %constant_dynamic-update-slice_fusion.10, bf16[128,4096]{1,0:T(8,128)(2,1)} %collective-permute-done.72, ...), kind=kOutput, calls=%fused_computation | convolution fusion | flops 4315938816 | bytes 13631488 | tf_op jit(solution)/shard_map/dot_general | solution.py:23
  (311 shorter events, 114.8 us)
Async XLA Ops:
  22.8 23.9 %collective-permute-start.1 = (bf16[32,8192]{1,0:T(8,128)(2,1)S(1)}, bf16[32,8192]{1,0:T(8,128)(2,1)S(1)}, u32[]{:S(2)}, u32[]{:S(2)}) collective-permute-start(bf16[32,8192]{1,0:T(8,128)(2,1)S(1)} %get-tuple-element.408), channel_id=1, source_target_pairs={{0,2},{1,3},{2,0},{3,1},{4,6},{5,7},{6,4},{7,5},{8,10},{9,11},{10,... | collective-permute-start | bytes 1572872 | tf_op jit(solution)/shard_map/ppermute | solution.py:15
  25.7 20.9 %collective-permute-start.2 = (bf16[32,8192]{1,0:T(8,128)(2,1)S(1)}, bf16[32,8192]{1,0:T(8,128)(2,1)S(1)}, u32[]{:S(2)}, u32[]{:S(2)}) collective-permute-start(bf16[32,8192]{1,0:T(8,128)(2,1)S(1)} %get-tuple-element.407), channel_id=1, source_target_pairs={{0,4},{1,5},{2,6},{3,7},{4,0},{5,1},{6,2},{7,3},{8,12},{9,13},{10,... | collective-permute-start | bytes 1572872 | tf_op jit(solution)/shard_map/ppermute | solution.py:15
  42.8 37.7 %collective-permute-start.5 = (bf16[1,2,128,1024]{3,2,1,0:T(8,128)(2,1)S(1)}, bf16[1,2,128,1024]{3,2,1,0:T(8,128)(2,1)S(1)}, u32[]{:S(2)}, u32[]{:S(2)}) collective-permute-start(bf16[1,2,128,1024]{3,2,1,0:T(8,128)(2,1)S(1)} %maximum_bitcast_fusion), channel_id=1, source_target_pairs={{0,8},{1,9},{2,10},{3,11},{4,12},{5,13},{6,14},{7,15},{8,0},{9,1},... | collective-permute-start | bytes 1572872 | tf_op jit(solution)/shard_map/ppermute | solution.py:15
  46.3 70.4 %collective-permute-start.9 = (bf16[1,2,128,1024]{3,2,1,0:T(8,128)(2,1)}, bf16[1,2,128,1024]{3,2,1,0:T(8,128)(2,1)}, u32[]{:S(2)}, u32[]{:S(2)}) collective-permute-start(bf16[1,2,128,1024]{3,2,1,0:T(8,128)(2,1)} %maximum_bitcast_fusion.1), channel_id=1, source_target_pairs={{0,8},{1,9},{2,10},{3,11},{4,12},{5,13},{6,14},{7,15},{8,0},{9,1},... | collective-permute-start | bytes 1572872 | tf_op jit(solution)/shard_map/ppermute | solution.py:15
  46.8 49.3 %collective-permute-start.3 = (bf16[16,8192]{1,0:T(8,128)(2,1)S(1)}, bf16[16,8192]{1,0:T(8,128)(2,1)S(1)}, u32[]{:S(2)}, u32[]{:S(2)}) collective-permute-start(bf16[16,8192]{1,0:T(8,128)(2,1)S(1)} %get-tuple-element.406), channel_id=1, source_target_pairs={{0,4},{1,5},{2,6},{3,7},{4,0},{5,1},{6,2},{7,3},{8,12},{9,13},{10,... | collective-permute-start | bytes 786440 | tf_op jit(solution)/shard_map/ppermute | solution.py:15
  47.3 48.9 %collective-permute-start.4 = (bf16[16,8192]{1,0:T(8,128)(2,1)S(1)}, bf16[16,8192]{1,0:T(8,128)(2,1)S(1)}, u32[]{:S(2)}, u32[]{:S(2)}) collective-permute-start(bf16[16,8192]{1,0:T(8,128)(2,1)S(1)} %get-tuple-element.405), channel_id=1, source_target_pairs={{0,2},{1,3},{2,0},{3,1},{4,6},{5,7},{6,4},{7,5},{8,10},{9,11},{10,... | collective-permute-start | bytes 786440 | tf_op jit(solution)/shard_map/ppermute | solution.py:15
  48.7 51.7 %collective-permute-start.13 = (bf16[32,8192]{1,0:T(8,128)(2,1)}, bf16[32,8192]{1,0:T(8,128)(2,1)S(1)}, u32[]{:S(2)}, u32[]{:S(2)}) collective-permute-start(bf16[32,8192]{1,0:T(8,128)(2,1)} %get-tuple-element.404), channel_id=1, source_target_pairs={{0,2},{1,3},{2,0},{3,1},{4,6},{5,7},{6,4},{7,5},{8,10},{9,11},{10,... | collective-permute-start | bytes 1572872 | tf_op jit(solution)/shard_map/ppermute | solution.py:15
  80.5 22.4 %collective-permute-start.14 = (bf16[32,8192]{1,0:T(8,128)(2,1)}, bf16[32,8192]{1,0:T(8,128)(2,1)S(1)}, u32[]{:S(2)}, u32[]{:S(2)}) collective-permute-start(bf16[32,8192]{1,0:T(8,128)(2,1)} %get-tuple-element.403), channel_id=1, source_target_pairs={{0,4},{1,5},{2,6},{3,7},{4,0},{5,1},{6,2},{7,3},{8,12},{9,13},{10,... | collective-permute-start | bytes 1572872 | tf_op jit(solution)/shard_map/ppermute | solution.py:15
  100.4 33.2 %collective-permute-start.7 = (bf16[16,8192]{1,0:T(8,128)(2,1)}, bf16[16,8192]{1,0:T(8,128)(2,1)}, u32[]{:S(2)}, u32[]{:S(2)}) collective-permute-start(bf16[16,8192]{1,0:T(8,128)(2,1)} %get-tuple-element.237), channel_id=1, source_target_pairs={{0,4},{1,5},{2,6},{3,7},{4,0},{5,1},{6,2},{7,3},{8,12},{9,13},{10,... | collective-permute-start | bytes 786440 | tf_op jit(solution)/shard_map/ppermute | solution.py:15
  102.9 32.4 %collective-permute-start.8 = (bf16[16,8192]{1,0:T(8,128)(2,1)S(1)}, bf16[16,8192]{1,0:T(8,128)(2,1)}, u32[]{:S(2)}, u32[]{:S(2)}) collective-permute-start(bf16[16,8192]{1,0:T(8,128)(2,1)S(1)} %get-tuple-element.239), channel_id=1, source_target_pairs={{0,2},{1,3},{2,0},{3,1},{4,6},{5,7},{6,4},{7,5},{8,10},{9,11},{10,... | collective-permute-start | bytes 786440 | tf_op jit(solution)/shard_map/ppermute | solution.py:15
  106.5 33.1 %collective-permute-start.20 = (bf16[32,8192]{1,0:T(8,128)(2,1)}, bf16[32,8192]{1,0:T(8,128)(2,1)}, u32[]{:S(2)}, u32[]{:S(2)}) collective-permute-start(bf16[32,8192]{1,0:T(8,128)(2,1)} %get-tuple-element.400), channel_id=1, source_target_pairs={{0,2},{1,3},{2,0},{3,1},{4,6},{5,7},{6,4},{7,5},{8,10},{9,11},{10,... | collective-permute-start | bytes 1572872 | tf_op jit(solution)/shard_map/ppermute | solution.py:15
  114.8 25.4 %collective-permute-start.21 = (bf16[32,8192]{1,0:T(8,128)(2,1)}, bf16[32,8192]{1,0:T(8,128)(2,1)}, u32[]{:S(2)}, u32[]{:S(2)}) collective-permute-start(bf16[32,8192]{1,0:T(8,128)(2,1)} %get-tuple-element.399), channel_id=1, source_target_pairs={{0,4},{1,5},{2,6},{3,7},{4,0},{5,1},{6,2},{7,3},{8,12},{9,13},{10,... | collective-permute-start | bytes 1572872 | tf_op jit(solution)/shard_map/ppermute | solution.py:15
  116.7 27.1 %collective-permute-start.17 = (bf16[64,4096]{1,0:T(8,128)(2,1)S(1)}, bf16[64,4096]{1,0:T(8,128)(2,1)}, u32[]{:S(2)}, u32[]{:S(2)}) collective-permute-start(bf16[64,4096]{1,0:T(8,128)(2,1)S(1)} %constant_dynamic-update-slice_fusion), channel_id=1, source_target_pairs={{0,4},{1,5},{2,6},{3,7},{4,0},{5,1},{6,2},{7,3},{8,12},{9,13},{10,... | collective-permute-start | bytes 1572872 | tf_op jit(solution)/shard_map/ppermute | solution.py:15
  139.6 20.2 %collective-permute-start.15 = (bf16[32,8192]{1,0:T(8,128)(2,1)S(1)}, bf16[32,8192]{1,0:T(8,128)(2,1)S(1)}, u32[]{:S(2)}, u32[]{:S(2)}) collective-permute-start(bf16[32,8192]{1,0:T(8,128)(2,1)S(1)} %constant_dynamic-update-slice_fusion.4.refs_0_), channel_id=1, source_target_pairs={{0,2},{1,3},{2,0},{3,1},{4,6},{5,7},{6,4},{7,5},{8,10},{9,11},{10,... | collective-permute-start | bytes 1572872 | tf_op jit(solution)/shard_map/ppermute | solution.py:15
  140.2 19.6 %collective-permute-start.16 = (bf16[32,8192]{1,0:T(8,128)(2,1)}, bf16[32,8192]{1,0:T(8,128)(2,1)}, u32[]{:S(2)}, u32[]{:S(2)}) collective-permute-start(bf16[32,8192]{1,0:T(8,128)(2,1)} %constant_dynamic-update-slice_fusion.6.refs_0_), channel_id=1, source_target_pairs={{0,4},{1,5},{2,6},{3,7},{4,0},{5,1},{6,2},{7,3},{8,12},{9,13},{10,... | collective-permute-start | bytes 1572872 | tf_op jit(solution)/shard_map/ppermute | solution.py:15
  143.7 19.7 %collective-permute-start.27 = (bf16[16,8192]{1,0:T(8,128)(2,1)S(1)}, bf16[16,8192]{1,0:T(8,128)(2,1)S(1)}, u32[]{:S(2)}, u32[]{:S(2)}) collective-permute-start(bf16[16,8192]{1,0:T(8,128)(2,1)S(1)} %get-tuple-element.397), channel_id=1, source_target_pairs={{0,2},{1,3},{2,0},{3,1},{4,6},{5,7},{6,4},{7,5},{8,10},{9,11},{10,... | collective-permute-start | bytes 786440 | tf_op jit(solution)/shard_map/ppermute | solution.py:15
  176.0 29.0 %collective-permute-start.30 = (bf16[32,8192]{1,0:T(8,128)(2,1)S(1)}, bf16[32,8192]{1,0:T(8,128)(2,1)S(1)}, u32[]{:S(2)}, u32[]{:S(2)}) collective-permute-start(bf16[32,8192]{1,0:T(8,128)(2,1)S(1)} %constant_dynamic-update-slice_fusion.12.refs_0_.refs_4_), channel_id=1, source_target_pairs={{0,2},{1,3},{2,0},{3,1},{4,6},{5,7},{6,4},{7,5},{8,10},{9,11},{10,... | collective-permute-start | bytes 1572872 | tf_op jit(solution)/shard_map/ppermute | solution.py:15
  212.5 28.1 %collective-permute-start.43 = (bf16[32,8192]{1,0:T(8,128)(2,1)S(1)}, bf16[32,8192]{1,0:T(8,128)(2,1)}, u32[]{:S(2)}, u32[]{:S(2)}) collective-permute-start(bf16[32,8192]{1,0:T(8,128)(2,1)S(1)} %constant_dynamic-update-slice_fusion.16.refs_0_.refs_8_), channel_id=1, source_target_pairs={{0,2},{1,3},{2,0},{3,1},{4,6},{5,7},{6,4},{7,5},{8,10},{9,11},{10,... | collective-permute-start | bytes 1572872 | tf_op jit(solution)/shard_map/ppermute | solution.py:15
  214.3 29.3 %collective-permute-start.44 = (bf16[32,8192]{1,0:T(8,128)(2,1)}, bf16[32,8192]{1,0:T(8,128)(2,1)}, u32[]{:S(2)}, u32[]{:S(2)}) collective-permute-start(bf16[32,8192]{1,0:T(8,128)(2,1)} %constant_dynamic-update-slice_fusion.18.refs_8_), channel_id=1, source_target_pairs={{0,4},{1,5},{2,6},{3,7},{4,0},{5,1},{6,2},{7,3},{8,12},{9,13},{10,... | collective-permute-start | bytes 1572872 | tf_op jit(solution)/shard_map/ppermute | solution.py:15
  216.1 27.7 %collective-permute-start.41 = (bf16[16,8192]{1,0:T(8,128)(2,1)S(1)}, bf16[16,8192]{1,0:T(8,128)(2,1)S(1)}, u32[]{:S(2)}, u32[]{:S(2)}) collective-permute-start(bf16[16,8192]{1,0:T(8,128)(2,1)S(1)} %get-tuple-element.296), channel_id=1, source_target_pairs={{0,4},{1,5},{2,6},{3,7},{4,0},{5,1},{6,2},{7,3},{8,12},{9,13},{10,... | collective-permute-start | bytes 786440 | tf_op jit(solution)/shard_map/ppermute | solution.py:15
  217.0 26.8 %collective-permute-start.42 = (bf16[16,8192]{1,0:T(8,128)(2,1)S(1)}, bf16[16,8192]{1,0:T(8,128)(2,1)S(1)}, u32[]{:S(2)}, u32[]{:S(2)}) collective-permute-start(bf16[16,8192]{1,0:T(8,128)(2,1)S(1)} %get-tuple-element.298), channel_id=1, source_target_pairs={{0,2},{1,3},{2,0},{3,1},{4,6},{5,7},{6,4},{7,5},{8,10},{9,11},{10,... | collective-permute-start | bytes 786440 | tf_op jit(solution)/shard_map/ppermute | solution.py:15
  229.1 43.8 %collective-permute-start.47 = (bf16[32,8192]{1,0:T(8,128)(2,1)S(1)}, bf16[32,8192]{1,0:T(8,128)(2,1)}, u32[]{:S(2)}, u32[]{:S(2)}) collective-permute-start(bf16[32,8192]{1,0:T(8,128)(2,1)S(1)} %constant_dynamic-update-slice_fusion.16.refs_0_.refs_8_), channel_id=1, source_target_pairs={{0,1},{1,0},{2,3},{3,2},{4,5},{5,4},{6,7},{7,6},{8,9},{9,8},{10,11... | collective-permute-start | bytes 1572872 | tf_op jit(solution)/shard_map/ppermute | solution.py:15
  243.6 29.4 %collective-permute-start.48 = (bf16[32,8192]{1,0:T(8,128)(2,1)}, bf16[32,8192]{1,0:T(8,128)(2,1)}, u32[]{:S(2)}, u32[]{:S(2)}) collective-permute-start(bf16[32,8192]{1,0:T(8,128)(2,1)} %collective-permute-done.43.refs_1_.refs_9_), channel_id=1, source_target_pairs={{0,1},{1,0},{2,3},{3,2},{4,5},{5,4},{6,7},{7,6},{8,9},{9,8},{10,11... | collective-permute-start | bytes 1572872 | tf_op jit(solution)/shard_map/ppermute | solution.py:15
  243.8 41.6 %collective-permute-start.45 = (bf16[32,8192]{1,0:T(8,128)(2,1)S(1)}, bf16[32,8192]{1,0:T(8,128)(2,1)}, u32[]{:S(2)}, u32[]{:S(2)}) collective-permute-start(bf16[32,8192]{1,0:T(8,128)(2,1)S(1)} %constant_dynamic-update-slice_fusion.20.refs_0_.refs_12_), channel_id=1, source_target_pairs={{0,2},{1,3},{2,0},{3,1},{4,6},{5,7},{6,4},{7,5},{8,10},{9,11},{10,... | collective-permute-start | bytes 1572872 | tf_op jit(solution)/shard_map/ppermute | solution.py:15
  246.9 38.6 %collective-permute-start.46 = (bf16[32,8192]{1,0:T(8,128)(2,1)}, bf16[32,8192]{1,0:T(8,128)(2,1)}, u32[]{:S(2)}, u32[]{:S(2)}) collective-permute-start(bf16[32,8192]{1,0:T(8,128)(2,1)} %constant_dynamic-update-slice_fusion.22.refs_12_), channel_id=1, source_target_pairs={{0,4},{1,5},{2,6},{3,7},{4,0},{5,1},{6,2},{7,3},{8,12},{9,13},{10,... | collective-permute-start | bytes 1572872 | tf_op jit(solution)/shard_map/ppermute | solution.py:15
  312.6 21.6 %collective-permute-start.64 = (bf16[32,8192]{1,0:T(8,128)(2,1)}, bf16[32,8192]{1,0:T(8,128)(2,1)}, u32[]{:S(2)}, u32[]{:S(2)}) collective-permute-start(bf16[32,8192]{1,0:T(8,128)(2,1)} %constant_dynamic-update-slice_fusion.6.refs_0_), channel_id=1, source_target_pairs={{0,1},{1,0},{2,3},{3,2},{4,5},{5,4},{6,7},{7,6},{8,9},{9,8},{10,11... | collective-permute-start | bytes 1572872 | tf_op jit(solution)/shard_map/ppermute | solution.py:15
  312.7 27.7 %collective-permute-start.65 = (bf16[32,8192]{1,0:T(8,128)(2,1)}, bf16[32,8192]{1,0:T(8,128)(2,1)}, u32[]{:S(2)}, u32[]{:S(2)}) collective-permute-start(bf16[32,8192]{1,0:T(8,128)(2,1)} %collective-permute-done.16.refs_1_), channel_id=1, source_target_pairs={{0,1},{1,0},{2,3},{3,2},{4,5},{5,4},{6,7},{7,6},{8,9},{9,8},{10,11... | collective-permute-start | bytes 1572872 | tf_op jit(solution)/shard_map/ppermute | solution.py:15
  313.2 27.8 %collective-permute-start.72 = (bf16[128,4096]{1,0:T(8,128)(2,1)}, bf16[128,4096]{1,0:T(8,128)(2,1)}, u32[]{:S(2)}, u32[]{:S(2)}) collective-permute-start(bf16[128,4096]{1,0:T(8,128)(2,1)} %constant_dynamic-update-slice_fusion.8), channel_id=1, source_target_pairs={{0,1},{1,0},{2,3},{3,2},{4,5},{5,4},{6,7},{7,6},{8,9},{9,8},{10,11... | collective-permute-start | bytes 3145736 | tf_op jit(solution)/shard_map/ppermute | solution.py:15
  313.3 27.9 %collective-permute-start.73 = (bf16[128,4096]{1,0:T(8,128)(2,1)}, bf16[128,4096]{1,0:T(8,128)(2,1)}, u32[]{:S(2)}, u32[]{:S(2)}) collective-permute-start(bf16[128,4096]{1,0:T(8,128)(2,1)} %constant_dynamic-update-slice_fusion.10), channel_id=1, source_target_pairs={{0,1},{1,0},{2,3},{3,2},{4,5},{5,4},{6,7},{7,6},{8,9},{9,8},{10,11... | collective-permute-start | bytes 3145736 | tf_op jit(solution)/shard_map/ppermute | solution.py:15
  342.6 46.5 %collective-permute-start.59 = (bf16[128,4096]{1,0:T(8,128)(2,1)}, bf16[128,4096]{1,0:T(8,128)(2,1)}, u32[]{:S(2)}, u32[]{:S(2)}) collective-permute-start(bf16[128,4096]{1,0:T(8,128)(2,1)} %pad_maximum_fusion.1), channel_id=1, source_target_pairs={{0,1},{1,0},{2,3},{3,2},{4,5},{5,4},{6,7},{7,6},{8,9},{9,8},{10,11... | collective-permute-start | bytes 3145736 | tf_op jit(solution)/shard_map/ppermute | solution.py:15
  345.4 23.6 %collective-permute-start.54 = (bf16[64,2048]{1,0:T(8,128)(2,1)}, bf16[64,2048]{1,0:T(8,128)(2,1)S(1)}, u32[]{:S(2)}, u32[]{:S(2)}) collective-permute-start(bf16[64,2048]{1,0:T(8,128)(2,1)} %get-tuple-element.420), channel_id=1, source_target_pairs={{0,2},{1,3},{2,0},{3,1},{4,6},{5,7},{6,4},{7,5},{8,10},{9,11},{10,... | collective-permute-start | bytes 786440 | tf_op jit(solution)/shard_map/ppermute | solution.py:15
  346.8 22.1 %collective-permute-start.55 = (bf16[64,2048]{1,0:T(8,128)(2,1)}, bf16[64,2048]{1,0:T(8,128)(2,1)S(1)}, u32[]{:S(2)}, u32[]{:S(2)}) collective-permute-start(bf16[64,2048]{1,0:T(8,128)(2,1)} %get-tuple-element.419), channel_id=1, source_target_pairs={{0,4},{1,5},{2,6},{3,7},{4,0},{5,1},{6,2},{7,3},{8,12},{9,13},{10,... | collective-permute-start | bytes 786440 | tf_op jit(solution)/shard_map/ppermute | solution.py:15
  (94 other events, 1119.0 us)

commit v3 on v1

v3 whole, which is shorter than its diff:
```python
import jax
import jax.numpy as jnp
from jax import lax
from jax.experimental import pallas as pl
from jax.experimental.pallas import tpu as pltpu
from jax.sharding import PartitionSpec as P

CORE, NEAR, FAR = 1, 2, 4
SHARES = 8
GROUP = 16


def swap(value, mask):
    count = lax.axis_size("gx")
    return lax.ppermute(value, "gx", [(at, at ^ mask) for at in range(count)])


def gelu_tanh(value):
    return jax.nn.gelu(value, approximate=True)


def contract(left, right, left_dim, right_dim):
    return lax.dot_general(
        left, right, (((left_dim,), (right_dim,)), ((), ())), preferred_element_type=jnp.float32
    )


def gather(value, masks):
    for mask in masks:
        value = jnp.concatenate([value, swap(value, mask)], axis=0)
    return value


def scatter(value, masks):
    for mask in masks:
        half = value.shape[0] // 2
        sent = value[half:].astype(jnp.bfloat16)
        value = value[:half].astype(jnp.float32) + swap(sent, mask).astype(jnp.float32)
    return value


NEAR_FAR = (CORE, NEAR, FAR)
FAR_NEAR = (CORE, FAR, NEAR)


def offset_of(place, order):
    total = jnp.zeros_like(place)
    for at, mask in enumerate(order):
        total = total + mask * ((place >> (2 - at)) & 1)
    return total


def place_of(offset, order):
    total = jnp.zeros_like(offset)
    for at, mask in enumerate(order):
        total = total + jnp.where((offset & mask) != 0, 1 << (2 - at), 0)
    return total


def picked(source, value):
    columns = lax.broadcasted_iota(jnp.int32, (source.shape[0], value.shape[0]), 1)
    chooser = (source[:, None] == columns).astype(jnp.bfloat16)
    return contract(chooser, value, 1, 0).astype(jnp.bfloat16)


def estimate():
    return pl.CostEstimate(flops=1, bytes_accessed=1, transcendentals=0)


def params():
    return pltpu.CompilerParams(
        dimension_semantics=("arbitrary",), vmem_limit_bytes=44 * 1024 * 1024
    )


def tile_of(size, most):
    return most if size % most == 0 else size


def whole_block(part):
    return pl.BlockSpec(part.shape, lambda at: (0,) * part.ndim)


def run(kernel, operands, in_specs, out_specs, out_shape, grid, name, marks, aliases=None):
    count = len(operands)

    def body_of(*refs):
        kernel(*refs[:count], *refs[count + len(marks) :])

    return pl.pallas_call(
        body_of,
        grid=grid,
        in_specs=list(in_specs) + [pl.BlockSpec(memory_space=pl.ANY)] * len(marks),
        out_specs=out_specs,
        out_shape=out_shape,
        input_output_aliases=aliases or {},
        compiler_params=params(),
        cost_estimate=estimate(),
        name=name,
    )(*operands, *marks)


def hidden_parts(rows_in, rows_grad, up_block, down_block, first, width, *, marks):
    count, depth = rows_in.shape
    tile = tile_of(width, 512)
    skip = first // tile
    half = count // 2

    def kernel(in_ref, grad_ref, up_ref, down_ref, keep_ref, send_ref):
        pre = jnp.dot(in_ref[...], up_ref[...], preferred_element_type=jnp.float32)
        keep_ref[0] = pre[:half]
        send_ref[0] = pre[half:].astype(jnp.bfloat16)
        hidden = contract(grad_ref[...], down_ref[...], 1, 1)
        keep_ref[1] = hidden[:half]
        send_ref[1] = hidden[half:].astype(jnp.bfloat16)

    return run(
        kernel,
        (rows_in, rows_grad, up_block, down_block),
        [
            whole_block(rows_in),
            whole_block(rows_grad),
            pl.BlockSpec((depth, tile), lambda at: (0, at + skip)),
            pl.BlockSpec((tile, depth), lambda at: (at + skip, 0)),
        ],
        [pl.BlockSpec((2, half, tile), lambda at: (0, 0, at))] * 2,
        (
            jax.ShapeDtypeStruct((2, half, width), jnp.float32),
            jax.ShapeDtypeStruct((2, half, width), jnp.bfloat16),
        ),
        (width // tile,),
        "hidden_parts",
        marks,
    )


def joined(pieces):
    if pieces[0].shape[0] % 16:
        return [jnp.concatenate(pieces, axis=0)]
    return pieces


def input_part(pieces, up_block, first, start=None, *, marks):
    pieces = joined(pieces)
    count = sum(piece.shape[0] for piece in pieces)
    depth = up_block.shape[0]
    width = pieces[0].shape[1]
    tile = tile_of(width, 512)
    skip = first // tile
    begin = [] if start is None else [start]

    def kernel(*refs):
        up_ref, out_ref = refs[len(pieces)], refs[-1]
        rows = jnp.concatenate([ref[...] for ref in refs[: len(pieces)]], axis=0)
        part = contract(rows, up_ref[...], 1, 1)

        @pl.when(pl.program_id(0) == 0)
        def _():
            out_ref[...] = part + refs[-2][...] if begin else part

        @pl.when(pl.program_id(0) != 0)
        def _():
            out_ref[...] += part

    result = jax.ShapeDtypeStruct((count, depth), jnp.float32)
    return run(
        kernel,
        (*pieces, up_block, *begin),
        [pl.BlockSpec((piece.shape[0], tile), lambda at: (0, at)) for piece in pieces]
        + [pl.BlockSpec((depth, tile), lambda at: (0, at + skip))]
        + [whole_block(part) for part in begin],
        whole_block(result),
        result,
        (width // tile,),
        "input_part",
        marks,
    )


def up_gradient(turned, pieces, first, full, before=None, *, marks):
    pieces = joined(pieces)
    depth = turned.shape[0]
    width = pieces[0].shape[1]
    tile = tile_of(width, 512)
    skip = first // tile
    begin = [] if before is None else [before]

    def kernel(turned_ref, *refs):
        rows = jnp.concatenate([ref[...] for ref in refs[: len(pieces)]], axis=0)
        refs[-1][...] = jnp.zeros_like(refs[-1])
        refs[-2][...] = jnp.dot(
            turned_ref[...], rows, preferred_element_type=jnp.float32
        ).astype(jnp.bfloat16)

    mark = jax.ShapeDtypeStruct((8, 128), jnp.float32)
    return run(
        kernel,
        (turned, *pieces, *begin),
        [whole_block(turned)]
        + [pl.BlockSpec((piece.shape[0], tile), lambda at: (0, at)) for piece in pieces]
        + [pl.BlockSpec(memory_space=pl.ANY)] * len(begin),
        (pl.BlockSpec((depth, tile), lambda at: (0, at + skip)), whole_block(mark)),
        (jax.ShapeDtypeStruct((depth, full), jnp.bfloat16), mark),
        (width // tile,),
        "up_gradient",
        marks,
        {1 + len(pieces): 0} if begin else {},
    )


def down_gradient(pieces, rows_grad, first, full, before=None, *, marks):
    pieces = joined(pieces)
    depth = rows_grad.shape[1]
    width = pieces[0].shape[1]
    tile = tile_of(width, 512)
    skip = first // tile
    begin = [] if before is None else [before]

    def kernel(grad_ref, *refs):
        rows = jnp.concatenate([ref[...] for ref in refs[: len(pieces)]], axis=0)
        refs[-1][...] = jnp.zeros_like(refs[-1])
        refs[-2][...] = contract(rows, grad_ref[...], 0, 0).astype(jnp.bfloat16)

    mark = jax.ShapeDtypeStruct((8, 128), jnp.float32)
    return run(
        kernel,
        (rows_grad, *pieces, *begin),
        [whole_block(rows_grad)]
        + [pl.BlockSpec((piece.shape[0], tile), lambda at: (0, at)) for piece in pieces]
        + [pl.BlockSpec(memory_space=pl.ANY)] * len(begin),
        (pl.BlockSpec((tile, depth), lambda at: (at + skip, 0)), whole_block(mark)),
        (jax.ShapeDtypeStruct((full, depth), jnp.bfloat16), mark),
        (width // tile,),
        "down_gradient",
        marks,
        {1 + len(pieces): 0} if begin else {},
    )


def context_parts(rows_by_order, proj_block, *, marks):
    _, count, depth = rows_by_order.shape
    width = proj_block.shape[0]
    tile = tile_of(width // 2, 1024)
    each = width // 2 // tile
    half = count // 2

    def kernel(rows_ref, proj_ref, keep_ref, send_ref):
        part = contract(rows_ref[0], proj_ref[...], 1, 1)
        keep_ref[...] = part[:half]
        send_ref[...] = part[half:].astype(jnp.bfloat16)

    return run(
        kernel,
        (rows_by_order, proj_block),
        [
            pl.BlockSpec((1, count, depth), lambda at: (at // each, 0, 0)),
            pl.BlockSpec((tile, depth), lambda at: (at, 0)),
        ],
        [pl.BlockSpec((half, tile), lambda at: (0, at))] * 2,
        (
            jax.ShapeDtypeStruct((half, width), jnp.float32),
            jax.ShapeDtypeStruct((half, width), jnp.bfloat16),
        ),
        (width // tile,),
        "context_parts",
        marks,
    )


def body(input_tiles, grad_tiles, context_tiles, up_tiles, down_tiles, output_tiles):
    grid_index = lax.axis_index("gx")
    total_bits = lax.axis_size("gx").bit_length() - 1
    q_masks = [1 << bit for bit in range(3, total_bits)]
    own_p = grid_index & (SHARES - 1)
    own_q = grid_index >> 3
    inputs = input_tiles[0]
    grads = grad_tiles[0]
    context = context_tiles[0]
    up_block = up_tiles[0]
    down_block = down_tiles[0]
    proj_block = output_tiles[0]
    rows = inputs.shape[0]
    half_rows = rows // 2
    share_rows = rows // SHARES
    block_rows = context.shape[0]
    half_block = block_rows // 2
    q_count = 1 << len(q_masks)
    width = up_block.shape[1]
    part_width = width // 2

    def row_source(order):
        at = jnp.arange(rows, dtype=jnp.int32)
        share = own_p ^ offset_of(at // share_rows, order)
        return share * share_rows + at % share_rows

    def half_source(half):
        at = jnp.arange(half_rows, dtype=jnp.int32)
        local = (at // GROUP) * 2 * GROUP + half * GROUP + at % GROUP
        place = place_of(own_p ^ (local // share_rows), NEAR_FAR)
        return place * share_rows + local % share_rows

    def token_source(half, order):
        at = jnp.arange(SHARES * half_block, dtype=jnp.int32)
        block = own_p ^ offset_of(at // half_block, order)
        at = at % half_block
        token = block * block_rows + (at // GROUP) * 2 * GROUP + half * GROUP + at % GROUP
        local = token % rows
        inside = (local // (2 * GROUP)) * GROUP + local % GROUP
        return ((token // rows) ^ own_q) * half_rows + inside

    def q_gather(value):
        value = value[None]
        for mask in q_masks:
            value = jnp.concatenate([value, swap(value, mask)], axis=0)
        return value

    source_nf = row_source(NEAR_FAR)
    own_rows = picked(source_nf, inputs), picked(row_source(FAR_NEAR), grads)
    count_gx = lax.axis_size("gx")
    pair = jnp.stack(own_rows)
    if q_count == 2:
        groups = [[at, at + SHARES] for at in range(SHARES)]
        pairs = lax.all_gather(pair, "gx", axis_index_groups=groups)
    else:
        pairs = q_gather(pair)
    groups = [[at + low for at in range(SHARES)] for low in range(0, count_gx, SHARES)]
    context_all = lax.all_gather(context, "gx", axis_index_groups=groups, tiled=True)
    chunks = {"own": own_rows}
    grads_nf = picked(source_nf, grads)

    state, saved = {}, {}
    act_rows, dpre_rows = {}, {}
    late, alive = [pair], []

    def held(values):
        part = late[0]
        part = part.reshape(-1, part.shape[-1])[:8, :128]
        values, after = lax.optimization_barrier((values, part))
        alive.append(after)
        return values

    def marks():
        used = list(alive)
        alive.clear()
        return used

    def fetch_other():
        pair = held(pairs)
        pair = jnp.where(own_q == 0, pair[1:], pair[:1]) if q_count == 2 else pair[1:]
        chunks["other"] = tuple(
            pair[:, which].reshape((q_count - 1) * rows, -1) for which in range(2)
        )
        late[0] = pair

    def sums(name):
        chunk_in, chunk_grad = held(chunks[name[0]])
        keep, send = hidden_parts(
            chunk_in, chunk_grad, up_block, down_block, name[1] * part_width, part_width,
            marks=marks(),
        )
        state[name] = keep, swap(send, CORE)
        late[0] = send

    def summed(parts, which, at):
        keep, recv, *more = parts
        total = keep[which, at] + recv[which, at].astype(jnp.float32)
        for part in more:
            total = total + part[which][at].astype(jnp.float32)
        return total

    def halved(parts, which):
        count = parts[-1][which].shape[0] // 2
        return summed(parts, which, slice(count, 2 * count)).astype(jnp.bfloat16)

    def sums_core(name):
        parts = held(state[name])
        send = halved(parts, 0), halved(parts, 1)
        state[name] = *parts, (swap(send[0], NEAR), swap(send[1], FAR))
        late[0] = send[0]

    def sums_one(name):
        parts = held(state[name])
        send = halved(parts, 0), halved(parts, 1)
        state[name] = *parts, (swap(send[0], FAR), swap(send[1], NEAR))
        late[0] = send[0]

    def gelu(name):
        parts = held(state[name])
        at = slice(0, parts[-1][0].shape[0])
        act, gelu_back = jax.vjp(gelu_tanh, summed(parts, 0, at))
        dpre = gelu_back(summed(parts, 1, at))[0].astype(jnp.bfloat16)
        act = act.astype(jnp.bfloat16)
        state[name] = dpre, act, swap(dpre, FAR), swap(act, NEAR)
        late[0] = dpre

    def spread_one(name):
        dpre, act, dpre_recv, act_recv = held(state[name])
        dpre = jnp.concatenate([dpre, dpre_recv], axis=0)
        act = jnp.concatenate([act, act_recv], axis=0)
        state[name] = dpre, act, swap(dpre, NEAR), swap(act, FAR)
        late[0] = dpre

    def spread_two(name):
        dpre, act, dpre_recv, act_recv = held(state[name])
        dpre_rows[name] = [dpre, dpre_recv, swap(dpre, CORE), swap(dpre_recv, CORE)]
        act_rows[name] = [act, act_recv]
        late[0] = dpre_recv

    def act_core(name):
        act_rows[name] = held(act_rows[name])
        act_rows[name] = act_rows[name] + [swap(part, CORE) for part in act_rows[name]]

    parts = {}

    def back(name):
        dpre_rows[name] = held(dpre_rows[name])
        part = input_part(
            dpre_rows[name], up_block, name[1] * part_width, parts.get(name[0]), marks=marks()
        )
        parts[name[0]] = part
        late[0] = part

    def q_sums():
        if q_count == 2:
            sent = held(parts["other"]).astype(jnp.bfloat16)
            parts["recv"] = swap(sent, q_masks[0])
            late[0] = sent

    halves, d_context_halves = {}, {}

    def finish_rows():
        if q_count == 2:
            own, recv = held((parts["own"], parts["recv"]))
            share = own + recv.astype(jnp.float32)
        else:
            other = parts["other"].reshape(q_count - 1, rows, -1)
            share = scatter(
                jnp.concatenate([parts["own"][None], other], axis=0), q_masks[::-1]
            )[0]
        d_input = (grads_nf.astype(jnp.float32) + share).astype(jnp.bfloat16)
        saved["d_input"] = d_input
        for half in range(2):
            halves[half] = q_gather(picked(half_source(half), d_input))
        late[0] = d_input

    def context_sums(half):
        gathered = held(halves[half]).reshape(q_count * half_rows, -1)
        by_order = [picked(token_source(half, order), gathered) for order in (NEAR_FAR, FAR_NEAR)]
        saved["d_input", half] = gathered
        keep, send = context_parts(jnp.stack(by_order), proj_block, marks=marks())
        halves[half] = keep, swap(send, CORE)
        late[0] = send

    def context_summed(parts, which, at):
        keep, recv, *more = parts
        columns = keep.shape[1] // 2
        here = slice(which * columns, (which + 1) * columns)
        total = keep[at, here] + recv[at, here].astype(jnp.float32)
        for part in more:
            total = total + part[which][at].astype(jnp.float32)
        return total

    def context_halved(parts, which, count):
        return context_summed(parts, which, slice(count, 2 * count)).astype(jnp.bfloat16)

    def context_core(half):
        parts = held(halves[half])
        count = parts[1].shape[0] // 2
        sent = context_halved(parts, 0, count), context_halved(parts, 1, count)
        halves[half] = *parts, (swap(sent[0], NEAR), swap(sent[1], FAR))
        late[0] = sent[0]

    def context_one(half):
        parts = held(halves[half])
        count = parts[1].shape[0] // 4
        sent = context_halved(parts, 0, count), context_halved(parts, 1, count)
        halves[half] = *parts, (swap(sent[0], FAR), swap(sent[1], NEAR))
        late[0] = sent[0]

    def context_two(half):
        parts = held(halves[half])
        at = slice(0, parts[1].shape[0] // 4)
        first, second = context_summed(parts, 0, at), context_summed(parts, 1, at)
        d_context_halves[half] = jnp.concatenate([first, second], axis=1).astype(jnp.bfloat16)
        late[0] = d_context_halves[half]

    mine_a, mine_b, other_a, other_b = ("own", 0), ("own", 1), ("other", 0), ("other", 1)
    sums(mine_a)
    sums_core(mine_a)
    sums(mine_b)
    sums_one(mine_a)
    gelu(mine_a)
    sums_core(mine_b)
    spread_one(mine_a)
    sums_one(mine_b)
    fetch_other()
    sums(other_a)
    spread_two(mine_a)
    sums_core(other_a)
    sums(other_b)
    sums_one(other_a)
    gelu(other_a)
    sums_core(other_b)
    back(mine_a)
    act_core(mine_a)
    spread_one(other_a)
    sums_one(other_b)
    gelu(other_b)
    in_all = jnp.concatenate([chunks[name][0] for name in ("own", "other")], axis=0)
    turned = in_all.T
    grad_all = jnp.concatenate([chunks[name][1] for name in ("own", "other")], axis=0)
    spread_two(other_a)
    spread_one(other_b)
    gelu(mine_b)
    back(other_a)
    spread_two(other_b)
    spread_one(mine_b)
    act_core(other_a)
    pieces = held([piece for name in (mine_a, other_a) for piece in dpre_rows[name]])
    d_up, late[0] = up_gradient(turned, pieces, 0, width, marks=marks())
    back(other_b)
    q_sums()
    spread_two(mine_b)
    act_core(other_b)
    pieces = held([piece for name in (mine_a, other_a) for piece in act_rows[name]])
    d_down, late[0] = down_gradient(pieces, grad_all, 0, width, marks=marks())
    back(mine_b)
    finish_rows()
    act_core(mine_b)
    pieces = held([piece for name in (mine_b, other_b) for piece in dpre_rows[name]])
    d_up, late[0] = up_gradient(turned, pieces, part_width, width, d_up, marks=marks())
    context_sums(0)
    context_core(0)
    context_sums(1)
    context_core(1)
    pieces = held([piece for name in (mine_b, other_b) for piece in act_rows[name]])
    d_down, late[0] = down_gradient(pieces, grad_all, part_width, width, d_down, marks=marks())
    context_one(0)
    context_one(1)
    tokens = jnp.arange(q_count * rows, dtype=jnp.int32)
    local = tokens % rows
    source = ((tokens // rows) ^ own_q) * half_rows + (local // (2 * GROUP)) * GROUP
    source = source + local % GROUP + ((local // GROUP) % 2) * q_count * half_rows
    both = held(jnp.concatenate([saved["d_input", 0], saved["d_input", 1]], axis=0))
    d_input_all = picked(source, both)
    d_output = contract(context_all, d_input_all, 0, 0).astype(jnp.bfloat16)
    context_two(0)
    context_two(1)

    columns = lax.broadcasted_iota(jnp.int32, (rows, rows), 1)
    chooser = (source_nf[:, None] == columns).astype(jnp.bfloat16)
    d_input = contract(chooser, saved["d_input"], 0, 0).astype(jnp.bfloat16)

    split = [
        d_context_halves[half].reshape(block_rows // (2 * GROUP), 1, GROUP, -1)
        for half in range(2)
    ]
    d_context = jnp.concatenate(split, axis=1).reshape(block_rows, -1)
    return (d_input[None], d_context[None], d_up[None], d_down[None], d_output[None])


def solution(mesh):
    return jax.shard_map(
        body,
        mesh=mesh,
        in_specs=(
            P("gx", "groups", None),
            P("gx", "groups", None),
            P("gx", "groups", None),
            P("gx", None, None),
            P("gx", None, None),
            P("gx", None, None),
        ),
        out_specs=(
            P("gx", "groups", None),
            P("gx", "groups", None),
            P("gx", "groups", None),
            P("gx", "groups", None),
            P("gx", "groups", None),
        ),
        check_vma=False,
    )
```

time: 529 us -> 398 us (0.75)
  matrix products: 201 us -> 15 us
  Pallas kernels: 0 us -> 126 us
  waiting for transfers between devices: 175 us -> 126 us
  local copies, waits for them, and re-layouts: 57.3 us -> 41.4 us
  between operations: 1.98 us -> 16.5 us
  starting transfers between devices: 56 us -> 46.3 us
  other arithmetic: 27.9 us -> 21.6 us
    dot_general x25 -> x11, matrix products: 201 us -> 15 us  [contract(): lax.dot_general(left, right, (((left_dim,), (right_dim,)), ((), ())), pre...]
    pallas_call x0 -> x14, Pallas kernels: none -> 126 us  [run(): pl.pallas_call(body_of, grid=grid, in_specs=list(in_specs) + [pl.BlockSpe...]
    ppermute x72 -> x65, waiting for transfers between devices: 175 us -> 121 us  [swap(): return lax.ppermute(value, 'gx', [(at, at ^ mask) for at in range(count)])]
    slice x37 -> x36, local copies, waits for them, and re-layouts: 18.9 us -> 2.73 us  [held(): part = part.reshape(-1, part.shape[-1])[:8, :128]]
    convert_element_type x0 -> x18, other arithmetic: none -> 15.6 us  [the longest x8 7.74 us: halved(): return summed(parts, which, slice(count, 2 * count)).astype(jnp.bfloat16)]
    concatenate x20 -> x2, other arithmetic: 10.3 us -> 0.14 us  [the longest x1 0.07 us: body(): jnp.concatenate([chunks[name][1] for name in ('own', 'other')], axis=0)]
    add x29 -> x7, other arithmetic: 9.95 us -> 0.15 us  [the longest x2 0.07 us: token_source(): return (token // rows ^ own_q) * half_rows + inside]
    ppermute x72 -> x65, starting transfers between devices: 56 us -> 46.2 us  [swap(): return lax.ppermute(value, 'gx', [(at, at ^ mask) for at in range(count)])]
  transfers between devices with their start and end apart: 72 -> 67, of which waited for: 32 -> 23; matrix products, arithmetic and copies ran while one was open for 51% -> 15% of each run, Pallas kernels for 0% -> 27%
where the time goes in v3:
time: 398 us; the launch traced here: 393 us
  Pallas kernels  126 us (32%)
  waiting for transfers between devices  126 us (32%)
  starting transfers between devices  46.3 us (12%)
  local copies, waits for them, and re-layouts  41.4 us (10%)
  other arithmetic  21.6 us (5%)
  between operations  16.5 us (4%)
  matrix products  15 us (4%)
    pallas_call x14, Pallas kernels, run(): pl.pallas_call(body_of, grid=grid, in_specs=list(in_specs) + [pl.BlockSpe...  126 us
    ppermute x65, waiting for transfers between devices, swap(): return lax.ppermute(value, 'gx', [(at, at ^ mask) for at in range(count)])  121 us
    ppermute x65, starting transfers between devices, swap(): return lax.ppermute(value, 'gx', [(at, at ^ mask) for at in range(count)])  46.2 us
    unnamed x95, local copies, waits for them, and re-layouts  30.5 us
    dot_general x11, matrix products, contract(): lax.dot_general(left, right, (((left_dim,), (right_dim,)), ((), ())), pre...  15 us
  transfers between devices with their start and end apart: 67, of which 23 were waited for; matrix products, arithmetic and copies ran while one was open for 15% of the time, Pallas kernels for 27%

profile of v3, /device:TPU:0, one launch (start us, length us, event | category | flops | bytes accessed | tf_op | source)
XLA Modules:
  0.0 393.4 jit_solution(10004696543195112345)
XLA Ops:
  10.0 10.8 %hidden_parts.4 = (f32[2,128,4096]{2,1,0:T(8,128)S(1)}, bf16[2,128,4096]{2,1,0:T(8,128)(2,1)S(1)}) custom-call(bf16[256,1024]{1,0:T(8,128)(2,1)S(1)} %convolution_convert_fusion.7.refs_0_, bf16[256,1024]{1,0:T(8,128)(2,1)S(1)} %convolution_convert_fusion.6.refs_1_, bf16[1024,8192]{1,0:T(8,128)(2,1)} %bitcast.173, bf16[8192,1024]{1,0:T(8,128)(2,1)} %bitcast.181, ...), custom_call_target="tpu_custom_call" | custom-call | flops 1 | bytes 1 | tf_op jit(solution)/shard_map/hidden_parts/pallas_call | solution.py:90
  21.4 3.8 collective-permute-done
  25.4 3.0 collective-permute-start.2
  30.0 11.4 %hidden_parts.5 = (f32[2,128,4096]{2,1,0:T(8,128)S(1)}, bf16[2,128,4096]{2,1,0:T(8,128)(2,1)}) custom-call(bf16[256,1024]{1,0:T(8,128)(2,1)S(1)} %convolution_convert_fusion.7.refs_0_, bf16[256,1024]{1,0:T(8,128)(2,1)S(1)} %convolution_convert_fusion.6.refs_1_, bf16[1024,8192]{1,0:T(8,128)(2,1)} %bitcast.174, bf16[8192,1024]{1,0:T(8,128)(2,1)} %bitcast.182, ...), custom_call_target="tpu_custom_call" | custom-call | flops 1 | bytes 1 | tf_op jit(solution)/shard_map/hidden_parts/pallas_call | solution.py:90
  45.0 8.0 %collective-permute-done.4 = bf16[32,4096]{1,0:T(8,128)(2,1)S(1)} collective-permute-done((bf16[32,4096]{1,0:T(8,128)(2,1)S(1)}, bf16[32,4096]{1,0:T(8,128)(2,1)S(1)}, u32[]{:S(2)}, u32[]{:S(2)}) %collective-permute-start.4) | collective-permute-done | bytes 262176 | tf_op jit(solution)/shard_map/ppermute | solution.py:15
  55.5 3.0 fusion.40
  62.6 31.7 %collective-permute-done.8 = bf16[32,4096]{1,0:T(8,128)(2,1)} collective-permute-done((bf16[32,4096]{1,0:T(8,128)(2,1)S(1)}, bf16[32,4096]{1,0:T(8,128)(2,1)}, u32[]{:S(2)}, u32[]{:S(2)}) %collective-permute-start.8) | collective-permute-done | bytes 262176 | tf_op jit(solution)/shard_map/ppermute | solution.py:15
  97.5 5.7 %all-gather.5.cloned.1.call-done = bf16[4,256,1024]{2,1,0:T(8,128)(2,1)} async-done(((bf16[2,256,1024]{2,1,0:T(8,128)(2,1)}), bf16[4,256,1024]{2,1,0:T(8,128)(2,1)}) %all-gather.5.cloned.1.call-update) | async-done | bytes 2097168 | tf_op jit(solution)/shard_map/all_gather | solution.py:323
  105.0 10.6 %hidden_parts.6 = (f32[2,128,4096]{2,1,0:T(8,128)S(1)}, bf16[2,128,4096]{2,1,0:T(8,128)(2,1)S(1)}) custom-call(bf16[256,1024]{1,0:T(8,128)(2,1)S(1)} %get-tuple-element.290.refs_0_, bf16[256,1024]{1,0:T(8,128)(2,1)S(1)} %get-tuple-element.291.refs_1_, bf16[1024,8192]{1,0:T(8,128)(2,1)} %bitcast.175, bf16[8192,1024]{1,0:T(8,128)(2,1)} %bitcast.183, ...), custom_call_target="tpu_custom_call" | custom-call | flops 1 | bytes 1 | tf_op jit(solution)/shard_map/hidden_parts/pallas_call | solution.py:90
  119.7 11.4 %collective-permute-done.13.refs_1_.refs_2_ = bf16[64,4096]{1,0:T(8,128)(2,1)S(1)} collective-permute-done((bf16[64,4096]{1,0:T(8,128)(2,1)S(1)}, bf16[64,4096]{1,0:T(8,128)(2,1)S(1)}, u32[]{:S(2)}, u32[]{:S(2)}) %collective-permute-start.13) | collective-permute-done | bytes 524320 | tf_op jit(solution)/shard_map/ppermute | solution.py:15
  136.2 10.5 %hidden_parts.7 = (f32[2,128,4096]{2,1,0:T(8,128)S(1)}, bf16[2,128,4096]{2,1,0:T(8,128)(2,1)S(1)}) custom-call(bf16[256,1024]{1,0:T(8,128)(2,1)S(1)} %get-tuple-element.290.refs_0_, bf16[256,1024]{1,0:T(8,128)(2,1)S(1)} %get-tuple-element.291.refs_1_, bf16[1024,8192]{1,0:T(8,128)(2,1)} %bitcast.176, bf16[8192,1024]{1,0:T(8,128)(2,1)} %bitcast.184, ...), custom_call_target="tpu_custom_call" | custom-call | flops 1 | bytes 1 | tf_op jit(solution)/shard_map/hidden_parts/pallas_call | solution.py:90
  152.7 4.0 %collective-permute-done.18 = bf16[32,4096]{1,0:T(8,128)(2,1)S(1)} collective-permute-done((bf16[32,4096]{1,0:T(8,128)(2,1)S(1)}, bf16[32,4096]{1,0:T(8,128)(2,1)S(1)}, u32[]{:S(2)}, u32[]{:S(2)}) %collective-permute-start.18) | collective-permute-done | bytes 262176 | tf_op jit(solution)/shard_map/ppermute | solution.py:15
  164.3 8.2 %input_part.4.refs_5_ = f32[256,1024]{1,0:T(8,128)S(1)} custom-call(bf16[64,4096]{1,0:T(8,128)(2,1)S(1)} %constant_dynamic-update-slice_fusion.refs_0_.refs_1_, bf16[64,4096]{1,0:T(8,128)(2,1)S(1)} %collective-permute-done.13.refs_1_.refs_2_, bf16[64,4096]{1,0:T(8,128)(2,1)S(1)} %collective-permute-done.24.refs_2_.refs_3_, ...), custom_call_target="tpu_custom_call" | custom-call | flops 1 | bytes 1 | tf_op jit(solution)/shard_map/input_part/pallas_call | solution.py:90
  174.2 6.5 %collective-permute-done.20 = bf16[64,4096]{1,0:T(8,128)(2,1)S(1)} collective-permute-done((bf16[64,4096]{1,0:T(8,128)(2,1)S(1)}, bf16[64,4096]{1,0:T(8,128)(2,1)S(1)}, u32[]{:S(2)}, u32[]{:S(2)}) %collective-permute-start.20) | collective-permute-done | bytes 524320 | tf_op jit(solution)/shard_map/ppermute | solution.py:15
  184.6 4.8 %collective-permute-done.26 = bf16[32,4096]{1,0:T(8,128)(2,1)S(1)} collective-permute-done((bf16[32,4096]{1,0:T(8,128)(2,1)S(1)}, bf16[32,4096]{1,0:T(8,128)(2,1)S(1)}, u32[]{:S(2)}, u32[]{:S(2)}) %collective-permute-start.26) | collective-permute-done | bytes 262176 | tf_op jit(solution)/shard_map/ppermute | solution.py:15
  189.4 5.4 %collective-permute-done.27 = bf16[32,4096]{1,0:T(8,128)(2,1)S(1)} collective-permute-done((bf16[32,4096]{1,0:T(8,128)(2,1)S(1)}, bf16[32,4096]{1,0:T(8,128)(2,1)S(1)}, u32[]{:S(2)}, u32[]{:S(2)}) %collective-permute-start.27) | collective-permute-done | bytes 262176 | tf_op jit(solution)/shard_map/ppermute | solution.py:15
  200.2 3.6 collective-permute-done.28
  219.0 8.4 %input_part.5.refs_5_ = f32[256,1024]{1,0:T(8,128)S(1)} custom-call(bf16[64,4096]{1,0:T(8,128)(2,1)S(1)} %copy-done.12, bf16[64,4096]{1,0:T(8,128)(2,1)} %collective-permute-done.30.refs_1_.refs_6_, bf16[64,4096]{1,0:T(8,128)(2,1)S(1)} %copy-done.23, bf16[64,4096]{1,0:T(8,128)(2,1)} %collective-permute-done.37.refs_3_.refs_8_, bf16[1024,8192]{1,0:T(8,128)(2,1)} %bitcast.178, ...), custom_call_target="tpu_custom_call" | custom-call | flops 1 | bytes 1 | tf_op jit(solution)/shard_map/input_part/pallas_call | solution.py:90
  246.8 9.1 %up_gradient.2 = (bf16[1024,8192]{1,0:T(8,128)(2,1)}, f32[8,128]{1,0:T(8,128)S(1)}) custom-call(bf16[1024,512]{1,0:T(8,128)(2,1)S(1)} %copy.17.refs_0_, bf16[64,4096]{1,0:T(8,128)(2,1)S(1)} %copy-done.10, bf16[64,4096]{1,0:T(8,128)(2,1)S(1)} %copy-done.15, bf16[64,4096]{1,0:T(8,128)(2,1)S(1)} %copy-done.19, bf16[64,4096]{1,0:T(8,128)(2,1)S(1)} %copy-done.17, ...), custom_call_target="tpu_custom_call" | custom-call | flops 1 | bytes 1 | tf_op jit(solution)/shard_map/up_gradient/pallas_call | solution.py:90
  256.5 8.4 %input_part.6 = f32[256,1024]{1,0:T(8,128)S(1)} custom-call(bf16[64,4096]{1,0:T(8,128)(2,1)S(1)} %copy-done.8, bf16[64,4096]{1,0:T(8,128)(2,1)} %collective-permute-done.34.refs_1_.refs_6_, bf16[64,4096]{1,0:T(8,128)(2,1)S(1)} %copy-done.21, bf16[64,4096]{1,0:T(8,128)(2,1)} %collective-permute-done.41.refs_3_.refs_8_, bf16[1024,8192]{1,0:T(8,128)(2,1)} %bitcast.179, ...), custom_call_target="tpu_custom_call" | custom-call | flops 1 | bytes 1 | tf_op jit(solution)/shard_map/input_part/pallas_call | solution.py:90
  268.0 9.7 %down_gradient.2 = (bf16[8192,1024]{1,0:T(8,128)(2,1)}, f32[8,128]{1,0:T(8,128)S(1)}) custom-call(bf16[512,1024]{1,0:T(8,128)(2,1)S(1)} %pad_maximum_fusion.1.refs_0_, bf16[64,4096]{1,0:T(8,128)(2,1)} %constant_dynamic-update-slice_fusion.2.refs_1_, bf16[64,4096]{1,0:T(8,128)(2,1)} %collective-permute-done.14.refs_2_, ...), custom_call_target="tpu_custom_call" | custom-call | flops 1 | bytes 1 | tf_op jit(solution)/shard_map/down_gradient/pallas_call | solution.py:90
  277.7 8.3 %input_part.7 = f32[256,1024]{1,0:T(8,128)S(1)} custom-call(bf16[64,4096]{1,0:T(8,128)(2,1)} %constant_dynamic-update-slice_fusion.12.refs_0_.refs_1_, bf16[64,4096]{1,0:T(8,128)(2,1)} %collective-permute-done.38.refs_1_.refs_2_, bf16[64,4096]{1,0:T(8,128)(2,1)S(1)} %collective-permute-done.42.refs_2_.refs_3_, ...), custom_call_target="tpu_custom_call" | custom-call | flops 1 | bytes 1 | tf_op jit(solution)/shard_map/input_part/pallas_call | solution.py:90
  286.1 5.5 %collective-permute-done.48 = bf16[256,1024]{1,0:T(8,128)(2,1)S(1)} collective-permute-done((bf16[256,1024]{1,0:T(8,128)(2,1)S(1)}, bf16[256,1024]{1,0:T(8,128)(2,1)S(1)}, u32[]{:S(2)}, u32[]{:S(2)}) %collective-permute-start.48) | collective-permute-done | bytes 524320 | tf_op jit(solution)/shard_map/ppermute | solution.py:15
  292.3 9.8 %up_gradient.3 = (bf16[1024,8192]{1,0:T(8,128)(2,1)}, f32[8,128]{1,0:T(8,128)S(1)}) custom-call(bf16[1024,512]{1,0:T(8,128)(2,1)S(1)} %copy.17.refs_0_, bf16[64,4096]{1,0:T(8,128)(2,1)} %constant_dynamic-update-slice_fusion.12.refs_0_.refs_1_, bf16[64,4096]{1,0:T(8,128)(2,1)} %collective-permute-done.38.refs_1_.refs_2_, ...), custom_call_target="tpu_custom_call", output_to_operand_aliasing={{0}: (9, {})} | custom-call | flops 1 | bytes 1 | tf_op jit(solution)/shard_map/up_gradient/pallas_call | solution.py:90
  302.0 3.9 collective-permute-done.49
  306.8 5.7 %context_parts.2 = (f32[128,4096]{1,0:T(8,128)S(1)}, bf16[128,4096]{1,0:T(8,128)(2,1)S(1)}) custom-call(bf16[2,256,1024]{2,1,0:T(8,128)(2,1)S(1)} %pad_maximum_fusion.2.refs_0_, bf16[4096,1024]{1,0:T(8,128)(2,1)} %bitcast.185, f32[8,128]{1,0:T(8,128)S(1)} %get-tuple-element.429.refs_2_), custom_call_target="tpu_custom_call" | custom-call | flops 1 | bytes 1 | tf_op jit(solution)/shard_map/context_parts/pallas_call | solution.py:90
  313.0 14.1 %collective-permute-done.55 = bf16[1,128,1024]{2,1,0:T(8,128)(2,1)S(1)} collective-permute-done((bf16[1,128,1024]{2,1,0:T(8,128)(2,1)S(1)}, bf16[1,128,1024]{2,1,0:T(8,128)(2,1)S(1)}, u32[]{:S(2)}, u32[]{:S(2)}) %collective-permute-start.55) | collective-permute-done | bytes 262176 | tf_op jit(solution)/shard_map/ppermute | solution.py:15
  328.1 5.7 %context_parts.3 = (f32[128,4096]{1,0:T(8,128)S(1)}, bf16[128,4096]{1,0:T(8,128)(2,1)S(1)}) custom-call(bf16[2,256,1024]{2,1,0:T(8,128)(2,1)S(1)} %pad_maximum_fusion.3.refs_0_, bf16[4096,1024]{1,0:T(8,128)(2,1)} %bitcast.186, bf16[8,128]{1,0:T(8,128)(2,1)S(1)} %slice.518.refs_2_, bf16[8,128]{1,0:T(8,128)(2,1)S(1)} %slice.581.refs_3_), custom_call_target="tpu_custom_call" | custom-call | flops 1 | bytes 1 | tf_op jit(solution)/shard_map/context_parts/pallas_call | solution.py:90
  337.9 5.6 %collective-permute-done.51 = bf16[64,2048]{1,0:T(8,128)(2,1)S(1)} collective-permute-done((bf16[64,2048]{1,0:T(8,128)(2,1)S(1)}, bf16[64,2048]{1,0:T(8,128)(2,1)S(1)}, u32[]{:S(2)}, u32[]{:S(2)}) %collective-permute-start.51) | collective-permute-done | bytes 262176 | tf_op jit(solution)/shard_map/ppermute | solution.py:15
  349.4 9.7 %down_gradient.3 = (bf16[8192,1024]{1,0:T(8,128)(2,1)}, f32[8,128]{1,0:T(8,128)}) custom-call(bf16[512,1024]{1,0:T(8,128)(2,1)S(1)} %pad_maximum_fusion.1.refs_0_, bf16[64,4096]{1,0:T(8,128)(2,1)} %constant_dynamic-update-slice_fusion.14.refs_1_, bf16[64,4096]{1,0:T(8,128)(2,1)} %collective-permute-done.39.refs_2_, ...), custom_call_target="tpu_custom_call", output_to_operand_aliasing={{0}: (9, {})} | custom-call | flops 1 | bytes 1 | tf_op jit(solution)/shard_map/down_gradient/pallas_call | solution.py:90
  360.7 9.8 %convert_bitcast_fusion = bf16[1,4096,1024]{1,2,0:T(8,128)(2,1)} fusion(bf16[1,512,4096]{2,1,0:T(8,128)(2,1)} %all-gather.7.cloned.1.call-done, bf16[512,1024]{1,0:T(8,128)(2,1)S(1)} %pad_maximum_fusion.4, s32[512]{0:T(512)S(1)} %fusion.84), kind=kOutput, calls=%fused_computation | convolution fusion | flops 4836818944 | bytes 13633536 | tf_op jit(solution)/shard_map/dot_general | solution.py:23
  371.8 12.0 %copy.20 = bf16[1,4096,1024]{2,1,0:T(8,128)(2,1)} copy(bf16[1,4096,1024]{1,2,0:T(8,128)(2,1)} %convert_bitcast_fusion) | data formatting | bytes 16777216
  (308 shorter events, 108.8 us)
Async XLA Ops:
  8.0 95.2 %all-gather.5.cloned.1.call-start = ((), (), s32[]{:S(2)}) async-start(), calls=%async_computation | async-start | bytes 3145728 | tf_op jit(solution)/shard_map/all_gather | solution.py:323
  25.4 18.6 %collective-permute-start.2 = (bf16[64,4096]{1,0:T(8,128)(2,1)S(1)}, bf16[64,4096]{1,0:T(8,128)(2,1)S(1)}, u32[]{:S(2)}, u32[]{:S(2)}) collective-permute-start(bf16[64,4096]{1,0:T(8,128)(2,1)S(1)} %get-tuple-element.512), channel_id=1, source_target_pairs={{0,2},{1,3},{2,0},{3,1},{4,6},{5,7},{6,4},{7,5},{8,10},{9,11},{10,... | collective-permute-start | bytes 1572872 | tf_op jit(solution)/shard_map/ppermute | solution.py:15
  28.4 15.7 %collective-permute-start.3 = (bf16[64,4096]{1,0:T(8,128)(2,1)S(1)}, bf16[64,4096]{1,0:T(8,128)(2,1)S(1)}, u32[]{:S(2)}, u32[]{:S(2)}) collective-permute-start(bf16[64,4096]{1,0:T(8,128)(2,1)S(1)} %get-tuple-element.511), channel_id=1, source_target_pairs={{0,4},{1,5},{2,6},{3,7},{4,0},{5,1},{6,2},{7,3},{8,12},{9,13},{10,... | collective-permute-start | bytes 1572872 | tf_op jit(solution)/shard_map/ppermute | solution.py:15
  44.9 315.8 %all-gather.7.cloned.1.call-start = ((), (), s32[]{:S(2)}) async-start(), calls=%async_computation.1 | async-start | bytes 4718592 | tf_op jit(solution)/shard_map/all_gather | solution.py:327
  58.5 35.8 %collective-permute-start.6 = (bf16[64,4096]{1,0:T(8,128)(2,1)S(1)}, bf16[64,4096]{1,0:T(8,128)(2,1)S(1)}, u32[]{:S(2)}, u32[]{:S(2)}) collective-permute-start(bf16[64,4096]{1,0:T(8,128)(2,1)S(1)} %get-tuple-element.508), channel_id=1, source_target_pairs={{0,2},{1,3},{2,0},{3,1},{4,6},{5,7},{6,4},{7,5},{8,10},{9,11},{10,... | collective-permute-start | bytes 1572872 | tf_op jit(solution)/shard_map/ppermute | solution.py:15
  58.9 36.1 %collective-permute-start.7 = (bf16[64,4096]{1,0:T(8,128)(2,1)}, bf16[64,4096]{1,0:T(8,128)(2,1)}, u32[]{:S(2)}, u32[]{:S(2)}) collective-permute-start(bf16[64,4096]{1,0:T(8,128)(2,1)} %get-tuple-element.507), channel_id=1, source_target_pairs={{0,4},{1,5},{2,6},{3,7},{4,0},{5,1},{6,2},{7,3},{8,12},{9,13},{10,... | collective-permute-start | bytes 1572872 | tf_op jit(solution)/shard_map/ppermute | solution.py:15
  60.6 33.7 %collective-permute-start.8 = (bf16[32,4096]{1,0:T(8,128)(2,1)S(1)}, bf16[32,4096]{1,0:T(8,128)(2,1)}, u32[]{:S(2)}, u32[]{:S(2)}) collective-permute-start(bf16[32,4096]{1,0:T(8,128)(2,1)S(1)} %get-tuple-element.267), channel_id=1, source_target_pairs={{0,4},{1,5},{2,6},{3,7},{4,0},{5,1},{6,2},{7,3},{8,12},{9,13},{10,... | collective-permute-start | bytes 786440 | tf_op jit(solution)/shard_map/ppermute | solution.py:15
  61.0 33.3 %collective-permute-start.9 = (bf16[32,4096]{1,0:T(8,128)(2,1)S(1)}, bf16[32,4096]{1,0:T(8,128)(2,1)S(1)}, u32[]{:S(2)}, u32[]{:S(2)}) collective-permute-start(bf16[32,4096]{1,0:T(8,128)(2,1)S(1)} %get-tuple-element.285), channel_id=1, source_target_pairs={{0,2},{1,3},{2,0},{3,1},{4,6},{5,7},{6,4},{7,5},{8,10},{9,11},{10,... | collective-permute-start | bytes 786440 | tf_op jit(solution)/shard_map/ppermute | solution.py:15
  115.6 18.4 %collective-permute-start.12 = (bf16[2,128,4096]{2,1,0:T(8,128)(2,1)S(1)}, bf16[2,128,4096]{2,1,0:T(8,128)(2,1)S(1)}, u32[]{:S(2)}, u32[]{:S(2)}) collective-permute-start(bf16[2,128,4096]{2,1,0:T(8,128)(2,1)S(1)} %get-tuple-element.283), channel_id=1, source_target_pairs={{0,1},{1,0},{2,3},{3,2},{4,5},{5,4},{6,7},{7,6},{8,9},{9,8},{10,11... | collective-permute-start | bytes 6291464 | tf_op jit(solution)/shard_map/ppermute | solution.py:15
  116.7 14.4 %collective-permute-start.13 = (bf16[64,4096]{1,0:T(8,128)(2,1)S(1)}, bf16[64,4096]{1,0:T(8,128)(2,1)S(1)}, u32[]{:S(2)}, u32[]{:S(2)}) collective-permute-start(bf16[64,4096]{1,0:T(8,128)(2,1)S(1)} %constant_dynamic-update-slice_fusion.refs_0_.refs_1_), channel_id=1, source_target_pairs={{0,2},{1,3},{2,0},{3,1},{4,6},{5,7},{6,4},{7,5},{8,10},{9,11},{10,... | collective-permute-start | bytes 1572872 | tf_op jit(solution)/shard_map/ppermute | solution.py:15
  119.7 14.4 %collective-permute-start.14 = (bf16[64,4096]{1,0:T(8,128)(2,1)}, bf16[64,4096]{1,0:T(8,128)(2,1)}, u32[]{:S(2)}, u32[]{:S(2)}) collective-permute-start(bf16[64,4096]{1,0:T(8,128)(2,1)} %constant_dynamic-update-slice_fusion.2.refs_1_), channel_id=1, source_target_pairs={{0,4},{1,5},{2,6},{3,7},{4,0},{5,1},{6,2},{7,3},{8,12},{9,13},{10,... | collective-permute-start | bytes 1572872 | tf_op jit(solution)/shard_map/ppermute | solution.py:15
  146.6 15.1 %collective-permute-start.15 = (bf16[2,128,4096]{2,1,0:T(8,128)(2,1)S(1)}, bf16[2,128,4096]{2,1,0:T(8,128)(2,1)S(1)}, u32[]{:S(2)}, u32[]{:S(2)}) collective-permute-start(bf16[2,128,4096]{2,1,0:T(8,128)(2,1)S(1)} %get-tuple-element.296), channel_id=1, source_target_pairs={{0,1},{1,0},{2,3},{3,2},{4,5},{5,4},{6,7},{7,6},{8,9},{9,8},{10,11... | collective-permute-start | bytes 6291464 | tf_op jit(solution)/shard_map/ppermute | solution.py:15
  162.0 18.7 %collective-permute-start.20 = (bf16[64,4096]{1,0:T(8,128)(2,1)S(1)}, bf16[64,4096]{1,0:T(8,128)(2,1)S(1)}, u32[]{:S(2)}, u32[]{:S(2)}) collective-permute-start(bf16[64,4096]{1,0:T(8,128)(2,1)S(1)} %get-tuple-element.500), channel_id=1, source_target_pairs={{0,2},{1,3},{2,0},{3,1},{4,6},{5,7},{6,4},{7,5},{8,10},{9,11},{10,... | collective-permute-start | bytes 1572872 | tf_op jit(solution)/shard_map/ppermute | solution.py:15
  162.6 18.1 %collective-permute-start.21 = (bf16[64,4096]{1,0:T(8,128)(2,1)S(1)}, bf16[64,4096]{1,0:T(8,128)(2,1)S(1)}, u32[]{:S(2)}, u32[]{:S(2)}) collective-permute-start(bf16[64,4096]{1,0:T(8,128)(2,1)S(1)} %get-tuple-element.499), channel_id=1, source_target_pairs={{0,4},{1,5},{2,6},{3,7},{4,0},{5,1},{6,2},{7,3},{8,12},{9,13},{10,... | collective-permute-start | bytes 1572872 | tf_op jit(solution)/shard_map/ppermute | solution.py:15
  172.7 26.3 %collective-permute-start.30 = (bf16[64,4096]{1,0:T(8,128)(2,1)S(1)}, bf16[64,4096]{1,0:T(8,128)(2,1)}, u32[]{:S(2)}, u32[]{:S(2)}) collective-permute-start(bf16[64,4096]{1,0:T(8,128)(2,1)S(1)} %constant_dynamic-update-slice_fusion.4.refs_0_.refs_5_), channel_id=1, source_target_pairs={{0,2},{1,3},{2,0},{3,1},{4,6},{5,7},{6,4},{7,5},{8,10},{9,11},{10,... | collective-permute-start | bytes 1572872 | tf_op jit(solution)/shard_map/ppermute | solution.py:15
  184.2 15.4 %collective-permute-start.31 = (bf16[64,4096]{1,0:T(8,128)(2,1)S(1)}, bf16[64,4096]{1,0:T(8,128)(2,1)S(1)}, u32[]{:S(2)}, u32[]{:S(2)}) collective-permute-start(bf16[64,4096]{1,0:T(8,128)(2,1)S(1)} %constant_dynamic-update-slice_fusion.6.refs_5_), channel_id=1, source_target_pairs={{0,4},{1,5},{2,6},{3,7},{4,0},{5,1},{6,2},{7,3},{8,12},{9,13},{10,... | collective-permute-start | bytes 1572872 | tf_op jit(solution)/shard_map/ppermute | solution.py:15
  200.2 16.7 %collective-permute-start.37 = (bf16[64,4096]{1,0:T(8,128)(2,1)}, bf16[64,4096]{1,0:T(8,128)(2,1)}, u32[]{:S(2)}, u32[]{:S(2)}) collective-permute-start(bf16[64,4096]{1,0:T(8,128)(2,1)} %collective-permute-done.30.refs_1_.refs_6_), channel_id=1, source_target_pairs={{0,1},{1,0},{2,3},{3,2},{4,5},{5,4},{6,7},{7,6},{8,9},{9,8},{10,11... | collective-permute-start | bytes 1572872 | tf_op jit(solution)/shard_map/ppermute | solution.py:15
  208.5 18.9 %collective-permute-start.34 = (bf16[64,4096]{1,0:T(8,128)(2,1)S(1)}, bf16[64,4096]{1,0:T(8,128)(2,1)}, u32[]{:S(2)}, u32[]{:S(2)}) collective-permute-start(bf16[64,4096]{1,0:T(8,128)(2,1)S(1)} %constant_dynamic-update-slice_fusion.8.refs_0_.refs_5_), channel_id=1, source_target_pairs={{0,2},{1,3},{2,0},{3,1},{4,6},{5,7},{6,4},{7,5},{8,10},{9,11},{10,... | collective-permute-start | bytes 1572872 | tf_op jit(solution)/shard_map/ppermute | solution.py:15
  210.8 16.7 %collective-permute-start.35 = (bf16[64,4096]{1,0:T(8,128)(2,1)}, bf16[64,4096]{1,0:T(8,128)(2,1)}, u32[]{:S(2)}, u32[]{:S(2)}) collective-permute-start(bf16[64,4096]{1,0:T(8,128)(2,1)} %constant_dynamic-update-slice_fusion.10.refs_5_), channel_id=1, source_target_pairs={{0,4},{1,5},{2,6},{3,7},{4,0},{5,1},{6,2},{7,3},{8,12},{9,13},{10,... | collective-permute-start | bytes 1572872 | tf_op jit(solution)/shard_map/ppermute | solution.py:15
  214.2 13.9 %collective-permute-start.32 = (bf16[32,4096]{1,0:T(8,128)(2,1)S(1)}, bf16[32,4096]{1,0:T(8,128)(2,1)}, u32[]{:S(2)}, u32[]{:S(2)}) collective-permute-start(bf16[32,4096]{1,0:T(8,128)(2,1)S(1)} %get-tuple-element.359), channel_id=1, source_target_pairs={{0,4},{1,5},{2,6},{3,7},{4,0},{5,1},{6,2},{7,3},{8,12},{9,13},{10,... | collective-permute-start | bytes 786440 | tf_op jit(solution)/shard_map/ppermute | solution.py:15
  228.1 27.8 %collective-permute-start.41 = (bf16[64,4096]{1,0:T(8,128)(2,1)}, bf16[64,4096]{1,0:T(8,128)(2,1)}, u32[]{:S(2)}, u32[]{:S(2)}) collective-permute-start(bf16[64,4096]{1,0:T(8,128)(2,1)} %collective-permute-done.34.refs_1_.refs_6_), channel_id=1, source_target_pairs={{0,1},{1,0},{2,3},{3,2},{4,5},{5,4},{6,7},{7,6},{8,9},{9,8},{10,11... | collective-permute-start | bytes 1572872 | tf_op jit(solution)/shard_map/ppermute | solution.py:15
  232.7 23.3 %collective-permute-start.38 = (bf16[64,4096]{1,0:T(8,128)(2,1)}, bf16[64,4096]{1,0:T(8,128)(2,1)}, u32[]{:S(2)}, u32[]{:S(2)}) collective-permute-start(bf16[64,4096]{1,0:T(8,128)(2,1)} %constant_dynamic-update-slice_fusion.12.refs_0_.refs_1_), channel_id=1, source_target_pairs={{0,2},{1,3},{2,0},{3,1},{4,6},{5,7},{6,4},{7,5},{8,10},{9,11},{10,... | collective-permute-start | bytes 1572872 | tf_op jit(solution)/shard_map/ppermute | solution.py:15
  235.8 29.1 %collective-permute-start.39 = (bf16[64,4096]{1,0:T(8,128)(2,1)}, bf16[64,4096]{1,0:T(8,128)(2,1)}, u32[]{:S(2)}, u32[]{:S(2)}) collective-permute-start(bf16[64,4096]{1,0:T(8,128)(2,1)} %constant_dynamic-update-slice_fusion.14.refs_1_), channel_id=1, source_target_pairs={{0,4},{1,5},{2,6},{3,7},{4,0},{5,1},{6,2},{7,3},{8,12},{9,13},{10,... | collective-permute-start | bytes 1572872 | tf_op jit(solution)/shard_map/ppermute | solution.py:15
  236.6 28.5 %collective-permute-start.44 = (bf16[64,4096]{1,0:T(8,128)(2,1)}, bf16[64,4096]{1,0:T(8,128)(2,1)}, u32[]{:S(2)}, u32[]{:S(2)}) collective-permute-start(bf16[64,4096]{1,0:T(8,128)(2,1)} %constant_dynamic-update-slice_fusion.2.refs_1_), channel_id=1, source_target_pairs={{0,1},{1,0},{2,3},{3,2},{4,5},{5,4},{6,7},{7,6},{8,9},{9,8},{10,11... | collective-permute-start | bytes 1572872 | tf_op jit(solution)/shard_map/ppermute | solution.py:15
  237.4 28.1 %collective-permute-start.45 = (bf16[64,4096]{1,0:T(8,128)(2,1)}, bf16[64,4096]{1,0:T(8,128)(2,1)}, u32[]{:S(2)}, u32[]{:S(2)}) collective-permute-start(bf16[64,4096]{1,0:T(8,128)(2,1)} %collective-permute-done.14.refs_2_), channel_id=1, source_target_pairs={{0,1},{1,0},{2,3},{3,2},{4,5},{5,4},{6,7},{7,6},{8,9},{9,8},{10,11... | collective-permute-start | bytes 1572872 | tf_op jit(solution)/shard_map/ppermute | solution.py:15
  265.5 26.1 %collective-permute-start.48 = (bf16[256,1024]{1,0:T(8,128)(2,1)S(1)}, bf16[256,1024]{1,0:T(8,128)(2,1)S(1)}, u32[]{:S(2)}, u32[]{:S(2)}) collective-permute-start(bf16[256,1024]{1,0:T(8,128)(2,1)S(1)} %convert_element_type.522), channel_id=1, source_target_pairs={{0,8},{1,9},{2,10},{3,11},{4,12},{5,13},{6,14},{7,15},{8,0},{9,1},... | collective-permute-start | bytes 1572872 | tf_op jit(solution)/shard_map/ppermute | solution.py:15
  312.5 14.7 %collective-permute-start.50 = (bf16[128,4096]{1,0:T(8,128)(2,1)S(1)}, bf16[128,4096]{1,0:T(8,128)(2,1)S(1)}, u32[]{:S(2)}, u32[]{:S(2)}) collective-permute-start(bf16[128,4096]{1,0:T(8,128)(2,1)S(1)} %get-tuple-element.431), channel_id=1, source_target_pairs={{0,1},{1,0},{2,3},{3,2},{4,5},{5,4},{6,7},{7,6},{8,9},{9,8},{10,11... | collective-permute-start | bytes 3145736 | tf_op jit(solution)/shard_map/ppermute | solution.py:15
  312.9 14.2 %collective-permute-start.55 = (bf16[1,128,1024]{2,1,0:T(8,128)(2,1)S(1)}, bf16[1,128,1024]{2,1,0:T(8,128)(2,1)S(1)}, u32[]{:S(2)}, u32[]{:S(2)}) collective-permute-start(bf16[1,128,1024]{2,1,0:T(8,128)(2,1)S(1)} %fusion.8), channel_id=1, source_target_pairs={{0,8},{1,9},{2,10},{3,11},{4,12},{5,13},{6,14},{7,15},{8,0},{9,1},... | collective-permute-start | bytes 786440 | tf_op jit(solution)/shard_map/ppermute | solution.py:15
  345.1 14.0 %collective-permute-start.57 = (bf16[64,2048]{1,0:T(8,128)(2,1)S(1)}, bf16[64,2048]{1,0:T(8,128)(2,1)S(1)}, u32[]{:S(2)}, u32[]{:S(2)}) collective-permute-start(bf16[64,2048]{1,0:T(8,128)(2,1)S(1)} %get-tuple-element.524), channel_id=1, source_target_pairs={{0,2},{1,3},{2,0},{3,1},{4,6},{5,7},{6,4},{7,5},{8,10},{9,11},{10,... | collective-permute-start | bytes 786440 | tf_op jit(solution)/shard_map/ppermute | solution.py:15
  346.1 14.6 %collective-permute-start.53 = (bf16[32,2048]{1,0:T(8,128)(2,1)S(1)}, bf16[32,2048]{1,0:T(8,128)(2,1)S(1)}, u32[]{:S(2)}, u32[]{:S(2)}) collective-permute-start(bf16[32,2048]{1,0:T(8,128)(2,1)S(1)} %get-tuple-element.516), channel_id=1, source_target_pairs={{0,4},{1,5},{2,6},{3,7},{4,0},{5,1},{6,2},{7,3},{8,12},{9,13},{10,... | collective-permute-start | bytes 393224 | tf_op jit(solution)/shard_map/ppermute | solution.py:15
  359.8 24.0 %collective-permute-start.59 = (bf16[32,2048]{1,0:T(8,128)(2,1)S(1)}, bf16[32,2048]{1,0:T(8,128)(2,1)S(1)}, u32[]{:S(2)}, u32[]{:S(2)}) collective-permute-start(bf16[32,2048]{1,0:T(8,128)(2,1)S(1)} %get-tuple-element.522), channel_id=1, source_target_pairs={{0,4},{1,5},{2,6},{3,7},{4,0},{5,1},{6,2},{7,3},{8,12},{9,13},{10,... | collective-permute-start | bytes 393224 | tf_op jit(solution)/shard_map/ppermute | solution.py:15
  360.1 23.7 %collective-permute-start.60 = (bf16[32,2048]{1,0:T(8,128)(2,1)S(1)}, bf16[32,2048]{1,0:T(8,128)(2,1)S(1)}, u32[]{:S(2)}, u32[]{:S(2)}) collective-permute-start(bf16[32,2048]{1,0:T(8,128)(2,1)S(1)} %get-tuple-element.521), channel_id=1, source_target_pairs={{0,2},{1,3},{2,0},{3,1},{4,6},{5,7},{6,4},{7,5},{8,10},{9,11},{10,... | collective-permute-start | bytes 393224 | tf_op jit(solution)/shard_map/ppermute | solution.py:15
  (78 other events, 854.2 us)
Sparse Core Ops, SparseCore 0:
  45.0 58.1 all-gather.4
Sparse Core Ops, SparseCore 1:
  217.0 36.1 all-gather.6

commit v4 on v3

--- a/solution.py
+++ b/solution.py
@@ -316,44 +316,39 @@
 
     source_nf = row_source(NEAR_FAR)
     own_rows = picked(source_nf, inputs), picked(row_source(FAR_NEAR), grads)
-    count_gx = lax.axis_size("gx")
-    pair = jnp.stack(own_rows)
-    if q_count == 2:
-        groups = [[at, at + SHARES] for at in range(SHARES)]
-        pairs = lax.all_gather(pair, "gx", axis_index_groups=groups)
-    else:
-        pairs = q_gather(pair)
-    groups = [[at + low for at in range(SHARES)] for low in range(0, count_gx, SHARES)]
+    pairs = [q_gather(part)[1:] for part in own_rows]
+    groups = [
+        [at + low for at in range(SHARES)] for low in range(0, lax.axis_size("gx"), SHARES)
+    ]
     context_all = lax.all_gather(context, "gx", axis_index_groups=groups, tiled=True)
     chunks = {"own": own_rows}
     grads_nf = picked(source_nf, grads)
 
     state, saved = {}, {}
     act_rows, dpre_rows = {}, {}
-    late, alive = [pair], []
+    late, alive = [own_rows[1]], []
+
+    def corner(part):
+        return part.reshape(-1, part.shape[-1])[:8, :128]
 
     def held(values):
-        part = late[0]
-        part = part.reshape(-1, part.shape[-1])[:8, :128]
-        values, after = lax.optimization_barrier((values, part))
+        values, after = lax.optimization_barrier((values, corner(late[0])))
         alive.append(after)
         return values
 
     def marks():
-        used = list(alive)
+        used = [*alive, corner(late[0])]
         alive.clear()
         return used
 
-    def fetch_other():
-        pair = held(pairs)
-        pair = jnp.where(own_q == 0, pair[1:], pair[:1]) if q_count == 2 else pair[1:]
-        chunks["other"] = tuple(
-            pair[:, which].reshape((q_count - 1) * rows, -1) for which in range(2)
-        )
-        late[0] = pair
+    def fetch(which):
+        pairs[which] = held(pairs[which])
+        late[0] = pairs[which]
+        if which == 1:
+            chunks["other"] = tuple(part.reshape((q_count - 1) * rows, -1) for part in pairs)
 
     def sums(name):
-        chunk_in, chunk_grad = held(chunks[name[0]])
+        chunk_in, chunk_grad = chunks[name[0]]
         keep, send = hidden_parts(
             chunk_in, chunk_grad, up_block, down_block, name[1] * part_width, part_width,
             marks=marks(),
@@ -390,8 +385,12 @@
         act, gelu_back = jax.vjp(gelu_tanh, summed(parts, 0, at))
         dpre = gelu_back(summed(parts, 1, at))[0].astype(jnp.bfloat16)
         act = act.astype(jnp.bfloat16)
+        state[name] = dpre, act
+        late[0] = dpre
+
+    def spread(name):
+        dpre, act = held(state[name])
         state[name] = dpre, act, swap(dpre, FAR), swap(act, NEAR)
-        late[0] = dpre
 
     def spread_one(name):
         dpre, act, dpre_recv, act_recv = held(state[name])
@@ -403,17 +402,17 @@
     def spread_two(name):
         dpre, act, dpre_recv, act_recv = held(state[name])
         dpre_rows[name] = [dpre, dpre_recv, swap(dpre, CORE), swap(dpre_recv, CORE)]
-        act_rows[name] = [act, act_recv]
+        act_rows[name] = act, act_recv
         late[0] = dpre_recv
 
     def act_core(name):
-        act_rows[name] = held(act_rows[name])
-        act_rows[name] = act_rows[name] + [swap(part, CORE) for part in act_rows[name]]
+        act = jnp.concatenate(held(act_rows[name]), axis=0)
+        act_rows[name] = [act, swap(act, CORE)]
+        late[0] = act
 
     parts = {}
 
     def back(name):
-        dpre_rows[name] = held(dpre_rows[name])
         part = input_part(
             dpre_rows[name], up_block, name[1] * part_width, parts.get(name[0]), marks=marks()
         )
@@ -439,9 +438,11 @@
             )[0]
         d_input = (grads_nf.astype(jnp.float32) + share).astype(jnp.bfloat16)
         saved["d_input"] = d_input
+        source = jnp.concatenate([half_source(0), half_source(1)])
+        ordered = picked(source, d_input)
         for half in range(2):
-            halves[half] = q_gather(picked(half_source(half), d_input))
-        late[0] = d_input
+            halves[half] = q_gather(ordered[half * half_rows : (half + 1) * half_rows])
+        late[0] = ordered
 
     def context_sums(half):
         gathered = held(halves[half]).reshape(q_count * half_rows, -1)
@@ -488,52 +489,57 @@
     sums(mine_a)
     sums_core(mine_a)
     sums(mine_b)
+    fetch(0)
     sums_one(mine_a)
     gelu(mine_a)
+    spread(mine_a)
     sums_core(mine_b)
+    fetch(1)
+    sums(other_a)
+    sums_one(mine_b)
     spread_one(mine_a)
-    sums_one(mine_b)
-    fetch_other()
-    sums(other_a)
-    spread_two(mine_a)
+    gelu(mine_b)
     sums_core(other_a)
     sums(other_b)
+    spread_two(mine_a)
     sums_one(other_a)
-    gelu(other_a)
     sums_core(other_b)
     back(mine_a)
-    act_core(mine_a)
-    spread_one(other_a)
+    gelu(other_a)
+    spread(other_a)
     sums_one(other_b)
-    gelu(other_b)
     in_all = jnp.concatenate([chunks[name][0] for name in ("own", "other")], axis=0)
     turned = in_all.T
     grad_all = jnp.concatenate([chunks[name][1] for name in ("own", "other")], axis=0)
+    spread_one(other_a)
+    gelu(other_b)
+    spread(other_b)
     spread_two(other_a)
     spread_one(other_b)
-    gelu(mine_b)
     back(other_a)
+    act_core(mine_a)
+    spread(mine_b)
+    pieces = [piece for name in (mine_a, other_a) for piece in dpre_rows[name]]
+    d_up, late[0] = up_gradient(turned, pieces, 0, width, marks=marks())
     spread_two(other_b)
+    act_core(other_a)
     spread_one(mine_b)
-    act_core(other_a)
-    pieces = held([piece for name in (mine_a, other_a) for piece in dpre_rows[name]])
-    d_up, late[0] = up_gradient(turned, pieces, 0, width, marks=marks())
     back(other_b)
     q_sums()
+    pieces = [piece for name in (mine_a, other_a) for piece in act_rows[name]]
+    d_down, late[0] = down_gradient(pieces, grad_all, 0, width, marks=marks())
     spread_two(mine_b)
     act_core(other_b)
-    pieces = held([piece for name in (mine_a, other_a) for piece in act_rows[name]])
-    d_down, late[0] = down_gradient(pieces, grad_all, 0, width, marks=marks())
     back(mine_b)
+    act_core(mine_b)
     finish_rows()
-    act_core(mine_b)
-    pieces = held([piece for name in (mine_b, other_b) for piece in dpre_rows[name]])
+    pieces = [piece for name in (mine_b, other_b) for piece in dpre_rows[name]]
     d_up, late[0] = up_gradient(turned, pieces, part_width, width, d_up, marks=marks())
     context_sums(0)
+    context_sums(1)
     context_core(0)
-    context_sums(1)
     context_core(1)
-    pieces = held([piece for name in (mine_b, other_b) for piece in act_rows[name]])
+    pieces = [piece for name in (mine_b, other_b) for piece in act_rows[name]]
     d_down, late[0] = down_gradient(pieces, grad_all, part_width, width, d_down, marks=marks())
     context_one(0)
     context_one(1)
@@ -541,9 +547,11 @@
     local = tokens % rows
     source = ((tokens // rows) ^ own_q) * half_rows + (local // (2 * GROUP)) * GROUP
     source = source + local % GROUP + ((local // GROUP) % 2) * q_count * half_rows
-    both = held(jnp.concatenate([saved["d_input", 0], saved["d_input", 1]], axis=0))
+    both = jnp.concatenate([saved["d_input", 0], saved["d_input", 1]], axis=0)
     d_input_all = picked(source, both)
-    d_output = contract(context_all, d_input_all, 0, 0).astype(jnp.bfloat16)
+    d_output, late[0] = down_gradient(
+        [context_all], d_input_all, 0, context_all.shape[1], marks=marks()
+    )
     context_two(0)
     context_two(1)
 

time: 398 us -> 378 us (0.950)
  local copies, waits for them, and re-layouts: 41.4 us -> 23.6 us
  starting transfers between devices: 46.3 us -> 55.7 us
  matrix products: 15 us -> 5.86 us
    unnamed x95 -> x80, local copies, waits for them, and re-layouts: 30.5 us -> 11.6 us
    ppermute x65 -> x63, starting transfers between devices: 46.2 us -> 55.7 us  [swap(): return lax.ppermute(value, 'gx', [(at, at ^ mask) for at in range(count)])]
    dot_general x11 -> x10, matrix products: 15 us -> 5.86 us  [contract(): lax.dot_general(left, right, (((left_dim,), (right_dim,)), ((), ())), pre...]
    all_gather x1 -> x0, waiting for transfers between devices: 5.74 us -> none  [body(): pairs = lax.all_gather(pair, 'gx', axis_index_groups=groups)]
    ppermute x65 -> x63, waiting for transfers between devices: 121 us -> 126 us  [swap(): return lax.ppermute(value, 'gx', [(at, at ^ mask) for at in range(count)])]
    pallas_call x14 -> x15, Pallas kernels: 126 us -> 128 us  [run(): pl.pallas_call(body_of, grid=grid, in_specs=list(in_specs) + [pl.BlockSpe...]
  transfers between devices with their start and end apart: 67 -> 64, of which waited for: 23 -> 24; matrix products, arithmetic and copies ran while one was open for 15% -> 10% of each run, Pallas kernels for 27% -> 28%
where the time goes in v4:
time: 378 us; the launch traced here: 376 us
  Pallas kernels  128 us (34%)
  waiting for transfers between devices  126 us (33%)
  starting transfers between devices  55.7 us (15%)
  local copies, waits for them, and re-layouts  23.6 us (6%)
  other arithmetic  21.5 us (6%)
  between operations  15.1 us (4%)
  matrix products  5.86 us (2%)
    pallas_call x15, Pallas kernels, run(): pl.pallas_call(body_of, grid=grid, in_specs=list(in_specs) + [pl.BlockSpe...  128 us
    ppermute x63, waiting for transfers between devices, swap(): return lax.ppermute(value, 'gx', [(at, at ^ mask) for at in range(count)])  126 us
    ppermute x63, starting transfers between devices, swap(): return lax.ppermute(value, 'gx', [(at, at ^ mask) for at in range(count)])  55.7 us
    unnamed x80, local copies, waits for them, and re-layouts  11.6 us
    convert_element_type x8, other arithmetic, halved(): return summed(parts, which, slice(count, 2 * count)).astype(jnp.bfloat16)  9.73 us
  transfers between devices with their start and end apart: 64, of which 24 were waited for; matrix products, arithmetic and copies ran while one was open for 10% of the time, Pallas kernels for 28%

profile of v4, /device:TPU:0, one launch (start us, length us, event | category | flops | bytes accessed | tf_op | source)
XLA Modules:
  0.0 375.6 jit_solution(14540247825304426946)
XLA Ops:
  9.4 10.4 %hidden_parts.4 = (f32[2,128,4096]{2,1,0:T(8,128)S(1)}, bf16[2,128,4096]{2,1,0:T(8,128)(2,1)S(1)}) custom-call(bf16[256,1024]{1,0:T(8,128)(2,1)S(1)} %copy.15.refs_0_, bf16[256,1024]{1,0:T(8,128)(2,1)S(1)} %convolution_convert_fusion.7.refs_1_, bf16[1024,8192]{1,0:T(8,128)(2,1)} %bitcast.165, bf16[8192,1024]{1,0:T(8,128)(2,1)} %bitcast.173, ...), custom_call_target="tpu_custom_call" | custom-call | flops 1 | bytes 1 | tf_op jit(solution)/shard_map/hidden_parts/pallas_call | solution.py:90
  20.3 3.7 collective-permute-start.4
  28.8 10.5 %hidden_parts.5 = (f32[2,128,4096]{2,1,0:T(8,128)S(1)}, bf16[2,128,4096]{2,1,0:T(8,128)(2,1)S(1)}) custom-call(bf16[256,1024]{1,0:T(8,128)(2,1)S(1)} %copy.15.refs_0_, bf16[256,1024]{1,0:T(8,128)(2,1)S(1)} %convolution_convert_fusion.7.refs_1_, bf16[1024,8192]{1,0:T(8,128)(2,1)} %bitcast.166, bf16[8192,1024]{1,0:T(8,128)(2,1)} %bitcast.174, ...), custom_call_target="tpu_custom_call" | custom-call | flops 1 | bytes 1 | tf_op jit(solution)/shard_map/hidden_parts/pallas_call | solution.py:90
  39.4 8.4 %collective-permute-done.4 = bf16[1,256,1024]{1,2,0:T(8,128)(2,1)S(1)} collective-permute-done((bf16[1,256,1024]{1,2,0:T(8,128)(2,1)S(1)}, bf16[1,256,1024]{1,2,0:T(8,128)(2,1)S(1)}, u32[]{:S(2)}, u32[]{:S(2)}) %collective-permute-start.4) | collective-permute-done | bytes 524320 | tf_op jit(solution)/shard_map/ppermute | solution.py:15
  51.7 5.2 %collective-permute-start.9 = (bf16[1,256,1024]{2,1,0:T(8,128)(2,1)S(1)}, bf16[1,256,1024]{2,1,0:T(8,128)(2,1)S(1)}, u32[]{:S(2)}, u32[]{:S(2)}) collective-permute-start(bf16[1,256,1024]{2,1,0:T(8,128)(2,1)S(1)} %bitcast.156), channel_id=1, source_target_pairs={{0,8},{1,9},{2,10},{3,11},{4,12},{5,13},{6,14},{7,15},{8,0},{9,1},... | collective-permute-start | bytes 1572872 | tf_op jit(solution)/shard_map/ppermute | solution.py:15
  57.0 6.6 %collective-permute-done.5 = bf16[32,4096]{1,0:T(8,128)(2,1)S(1)} collective-permute-done((bf16[32,4096]{1,0:T(8,128)(2,1)S(1)}, bf16[32,4096]{1,0:T(8,128)(2,1)S(1)}, u32[]{:S(2)}, u32[]{:S(2)}) %collective-permute-start.5) | collective-permute-done | bytes 262176 | tf_op jit(solution)/shard_map/ppermute | solution.py:15
  70.9 7.9 %collective-permute-done.9 = bf16[1,256,1024]{2,1,0:T(8,128)(2,1)S(1)} collective-permute-done((bf16[1,256,1024]{2,1,0:T(8,128)(2,1)S(1)}, bf16[1,256,1024]{2,1,0:T(8,128)(2,1)S(1)}, u32[]{:S(2)}, u32[]{:S(2)}) %collective-permute-start.9) | collective-permute-done | bytes 524320 | tf_op jit(solution)/shard_map/ppermute | solution.py:15
  78.9 11.1 %hidden_parts.6 = (f32[2,128,4096]{2,1,0:T(8,128)S(1)}, bf16[2,128,4096]{2,1,0:T(8,128)(2,1)S(1)}) custom-call(bf16[256,1024]{1,0:T(8,128)(2,1)S(1)} %copy.16.refs_0_, bf16[256,1024]{1,0:T(8,128)(2,1)S(1)} %bitcast.158, bf16[1024,8192]{1,0:T(8,128)(2,1)} %bitcast.167, bf16[8192,1024]{1,0:T(8,128)(2,1)} %bitcast.175, bf16[8,128]{1,0:T(8,128)(2,1)S(1)} %slice.573.refs_4_, ...), custom_call_target="tpu_custom_call" | custom-call | flops 1 | bytes 1 | tf_op jit(solution)/shard_map/hidden_parts/pallas_call | solution.py:90
  94.4 5.8 %collective-permute-done.10 = bf16[32,4096]{1,0:T(8,128)(2,1)S(1)} collective-permute-done((bf16[32,4096]{1,0:T(8,128)(2,1)S(1)}, bf16[32,4096]{1,0:T(8,128)(2,1)S(1)}, u32[]{:S(2)}, u32[]{:S(2)}) %collective-permute-start.10) | collective-permute-done | bytes 262176 | tf_op jit(solution)/shard_map/ppermute | solution.py:15
  105.0 11.4 %hidden_parts.7 = (f32[2,128,4096]{2,1,0:T(8,128)S(1)}, bf16[2,128,4096]{2,1,0:T(8,128)(2,1)}) custom-call(bf16[256,1024]{1,0:T(8,128)(2,1)S(1)} %copy.16.refs_0_, bf16[256,1024]{1,0:T(8,128)(2,1)S(1)} %bitcast.159, bf16[1024,8192]{1,0:T(8,128)(2,1)} %bitcast.168, bf16[8192,1024]{1,0:T(8,128)(2,1)} %bitcast.176, bf16[8,128]{1,0:T(8,128)(2,1)S(1)} %slice.579.refs_4_, ...), custom_call_target="tpu_custom_call" | custom-call | flops 1 | bytes 1 | tf_op jit(solution)/shard_map/hidden_parts/pallas_call | solution.py:90
  123.9 9.2 %collective-permute-done.14.refs_1_.refs_2_ = bf16[64,4096]{1,0:T(8,128)(2,1)S(1)} collective-permute-done((bf16[64,4096]{1,0:T(8,128)(2,1)S(1)}, bf16[64,4096]{1,0:T(8,128)(2,1)S(1)}, u32[]{:S(2)}, u32[]{:S(2)}) %collective-permute-start.14) | collective-permute-done | bytes 524320 | tf_op jit(solution)/shard_map/ppermute | solution.py:15
  133.2 4.3 %collective-permute-done.15 = bf16[64,4096]{1,0:T(8,128)(2,1)} collective-permute-done((bf16[64,4096]{1,0:T(8,128)(2,1)}, bf16[64,4096]{1,0:T(8,128)(2,1)}, u32[]{:S(2)}, u32[]{:S(2)}) %collective-permute-start.15) | collective-permute-done | bytes 524320 | tf_op jit(solution)/shard_map/ppermute | solution.py:15
  138.0 16.6 %collective-permute-done.17 = bf16[64,4096]{1,0:T(8,128)(2,1)S(1)} collective-permute-done((bf16[64,4096]{1,0:T(8,128)(2,1)}, bf16[64,4096]{1,0:T(8,128)(2,1)S(1)}, u32[]{:S(2)}, u32[]{:S(2)}) %collective-permute-start.17) | collective-permute-done | bytes 524320 | tf_op jit(solution)/shard_map/ppermute | solution.py:15
  154.5 4.7 %collective-permute-done.18 = bf16[64,4096]{1,0:T(8,128)(2,1)} collective-permute-done((bf16[64,4096]{1,0:T(8,128)(2,1)}, bf16[64,4096]{1,0:T(8,128)(2,1)}, u32[]{:S(2)}, u32[]{:S(2)}) %collective-permute-start.18) | collective-permute-done | bytes 524320 | tf_op jit(solution)/shard_map/ppermute | solution.py:15
  168.7 8.5 %input_part.4.refs_5_ = f32[256,1024]{1,0:T(8,128)S(1)} custom-call(bf16[64,4096]{1,0:T(8,128)(2,1)S(1)} %constant_dynamic-update-slice_fusion.refs_0_.refs_1_, bf16[64,4096]{1,0:T(8,128)(2,1)S(1)} %copy-done.8, bf16[64,4096]{1,0:T(8,128)(2,1)S(1)} %collective-permute-done.21.refs_2_.refs_3_, bf16[64,4096]{1,0:T(8,128)(2,1)S(1)} %collective-permute-done.22.refs_3_.refs_4_, ...), custom_call_target="tpu_custom_call" | custom-call | flops 1 | bytes 1 | tf_op jit(solution)/shard_map/input_part/pallas_call | solution.py:90
  181.5 10.7 %collective-permute-done.27 = bf16[64,4096]{1,0:T(8,128)(2,1)S(1)} collective-permute-done((bf16[64,4096]{1,0:T(8,128)(2,1)S(1)}, bf16[64,4096]{1,0:T(8,128)(2,1)S(1)}, u32[]{:S(2)}, u32[]{:S(2)}) %collective-permute-start.27) | collective-permute-done | bytes 524320 | tf_op jit(solution)/shard_map/ppermute | solution.py:15
  193.6 3.2 collective-permute-done.24
  202.4 11.3 %collective-permute-done.31 = bf16[32,4096]{1,0:T(8,128)(2,1)S(1)} collective-permute-done((bf16[32,4096]{1,0:T(8,128)(2,1)S(1)}, bf16[32,4096]{1,0:T(8,128)(2,1)S(1)}, u32[]{:S(2)}, u32[]{:S(2)}) %collective-permute-start.31) | collective-permute-done | bytes 262176 | tf_op jit(solution)/shard_map/ppermute | solution.py:15
  217.7 4.8 %collective-permute-done.34 = bf16[32,4096]{1,0:T(8,128)(2,1)} collective-permute-done((bf16[32,4096]{1,0:T(8,128)(2,1)S(1)}, bf16[32,4096]{1,0:T(8,128)(2,1)}, u32[]{:S(2)}, u32[]{:S(2)}) %collective-permute-start.34) | collective-permute-done | bytes 262176 | tf_op jit(solution)/shard_map/ppermute | solution.py:15
  228.3 8.3 %input_part.5.refs_5_ = f32[256,1024]{1,0:T(8,128)S(1)} custom-call(bf16[64,4096]{1,0:T(8,128)(2,1)} %constant_dynamic-update-slice_fusion.4.refs_0_.refs_5_, bf16[64,4096]{1,0:T(8,128)(2,1)} %collective-permute-done.28.refs_1_.refs_6_, bf16[64,4096]{1,0:T(8,128)(2,1)S(1)} %collective-permute-done.32.refs_2_.refs_7_, ...), custom_call_target="tpu_custom_call" | custom-call | flops 1 | bytes 1 | tf_op jit(solution)/shard_map/input_part/pallas_call | solution.py:90
  237.3 8.9 %up_gradient.2 = (bf16[1024,8192]{1,0:T(8,128)(2,1)}, f32[8,128]{1,0:T(8,128)S(1)}) custom-call(bf16[1024,512]{1,0:T(8,128)(2,1)S(1)} %maximum_bitcast_fusion.refs_0_, bf16[64,4096]{1,0:T(8,128)(2,1)S(1)} %constant_dynamic-update-slice_fusion.refs_0_.refs_1_, bf16[64,4096]{1,0:T(8,128)(2,1)S(1)} %copy-done.9, bf16[64,4096]{1,0:T(8,128)(2,1)S(1)} %copy-done.13, ...), custom_call_target="tpu_custom_call" | custom-call | flops 1 | bytes 1 | tf_op jit(solution)/shard_map/up_gradient/pallas_call | solution.py:90
  254.0 3.9 %collective-permute-done.36 = bf16[32,4096]{1,0:T(8,128)(2,1)S(1)} collective-permute-done((bf16[32,4096]{1,0:T(8,128)(2,1)S(1)}, bf16[32,4096]{1,0:T(8,128)(2,1)S(1)}, u32[]{:S(2)}, u32[]{:S(2)}) %collective-permute-start.36) | collective-permute-done | bytes 262176 | tf_op jit(solution)/shard_map/ppermute | solution.py:15
  262.3 8.2 %input_part.6 = f32[256,1024]{1,0:T(8,128)S(1)} custom-call(bf16[64,4096]{1,0:T(8,128)(2,1)S(1)} %constant_dynamic-update-slice_fusion.8.refs_0_.refs_5_, bf16[64,4096]{1,0:T(8,128)(2,1)S(1)} %collective-permute-done.38.refs_1_.refs_6_, bf16[64,4096]{1,0:T(8,128)(2,1)S(1)} %collective-permute-done.44.refs_2_.refs_7_, ...), custom_call_target="tpu_custom_call" | custom-call | flops 1 | bytes 1 | tf_op jit(solution)/shard_map/input_part/pallas_call | solution.py:90
  271.1 7.8 %down_gradient.3 = (bf16[8192,1024]{1,0:T(8,128)(2,1)}, f32[8,128]{1,0:T(8,128)S(1)}) custom-call(bf16[512,1024]{1,0:T(8,128)(2,1)S(1)} %pad_maximum_fusion.refs_0_, bf16[128,4096]{1,0:T(8,128)(2,1)S(1)} %constant_dynamic-update-slice_fusion.16.refs_1_, bf16[128,4096]{1,0:T(8,128)(2,1)S(1)} %collective-permute-done.42.refs_2_, ...), custom_call_target="tpu_custom_call" | custom-call | flops 1 | bytes 1 | tf_op jit(solution)/shard_map/down_gradient/pallas_call | solution.py:90
  281.6 8.3 %input_part.7 = f32[256,1024]{1,0:T(8,128)S(1)} custom-call(bf16[64,4096]{1,0:T(8,128)(2,1)S(1)} %constant_dynamic-update-slice_fusion.12.refs_0_.refs_1_, bf16[64,4096]{1,0:T(8,128)(2,1)S(1)} %collective-permute-done.40.refs_1_.refs_2_, bf16[64,4096]{1,0:T(8,128)(2,1)S(1)} %collective-permute-done.46.refs_2_.refs_3_, ...), custom_call_target="tpu_custom_call" | custom-call | flops 1 | bytes 1 | tf_op jit(solution)/shard_map/input_part/pallas_call | solution.py:90
  289.9 5.5 %collective-permute-done.48 = bf16[256,1024]{1,0:T(8,128)(2,1)S(1)} collective-permute-done((bf16[256,1024]{1,0:T(8,128)(2,1)S(1)}, bf16[256,1024]{1,0:T(8,128)(2,1)S(1)}, u32[]{:S(2)}, u32[]{:S(2)}) %collective-permute-start.48) | collective-permute-done | bytes 524320 | tf_op jit(solution)/shard_map/ppermute | solution.py:15
  299.1 7.7 %up_gradient.3 = (bf16[1024,8192]{1,0:T(8,128)(2,1)}, f32[8,128]{1,0:T(8,128)S(1)}) custom-call(bf16[1024,512]{1,0:T(8,128)(2,1)S(1)} %maximum_bitcast_fusion.refs_0_, bf16[64,4096]{1,0:T(8,128)(2,1)S(1)} %constant_dynamic-update-slice_fusion.12.refs_0_.refs_1_, ...), custom_call_target="tpu_custom_call", output_to_operand_aliasing={{0}: (9, {})} | custom-call | flops 1 | bytes 1 | tf_op jit(solution)/shard_map/up_gradient/pallas_call | solution.py:90
  306.8 12.7 %collective-permute-done.49 = bf16[1,128,1024]{2,1,0:T(8,128)(2,1)S(1)} collective-permute-done((bf16[1,128,1024]{2,1,0:T(8,128)(2,1)S(1)}, bf16[1,128,1024]{2,1,0:T(8,128)(2,1)S(1)}, u32[]{:S(2)}, u32[]{:S(2)}) %collective-permute-start.49) | collective-permute-done | bytes 262176 | tf_op jit(solution)/shard_map/ppermute | solution.py:15
  320.3 5.7 %context_parts.2 = (f32[128,4096]{1,0:T(8,128)S(1)}, bf16[128,4096]{1,0:T(8,128)(2,1)S(1)}) custom-call(bf16[2,256,1024]{2,1,0:T(8,128)(2,1)S(1)} %pad_maximum_fusion.1.refs_0_, bf16[4096,1024]{1,0:T(8,128)(2,1)} %bitcast.177, f32[8,128]{1,0:T(8,128)S(1)} %get-tuple-element.335.refs_2_.refs_3_, f32[8,128]{1,0:T(8,128)S(1)} %get-tuple-element.335.refs_2_.refs_3_), custom_call_target="tpu_custom_call" | custom-call | flops 1 | bytes 1 | tf_op jit(solution)/shard_map/context_parts/pallas_call | solution.py:90
  327.0 5.7 %context_parts.3 = (f32[128,4096]{1,0:T(8,128)S(1)}, bf16[128,4096]{1,0:T(8,128)(2,1)S(1)}) custom-call(bf16[2,256,1024]{2,1,0:T(8,128)(2,1)S(1)} %pad_maximum_fusion.2.refs_0_, bf16[4096,1024]{1,0:T(8,128)(2,1)} %bitcast.178, bf16[8,128]{1,0:T(8,128)(2,1)S(1)} %slice.532.refs_2_.refs_3_, bf16[8,128]{1,0:T(8,128)(2,1)S(1)} %slice.532.refs_2_.refs_3_), custom_call_target="tpu_custom_call" | custom-call | flops 1 | bytes 1 | tf_op jit(solution)/shard_map/context_parts/pallas_call | solution.py:90
  339.8 7.8 %down_gradient.4 = (bf16[8192,1024]{1,0:T(8,128)(2,1)}, f32[8,128]{1,0:T(8,128)S(1)}) custom-call(bf16[512,1024]{1,0:T(8,128)(2,1)S(1)} %pad_maximum_fusion.refs_0_, bf16[128,4096]{1,0:T(8,128)(2,1)S(1)} %constant_dynamic-update-slice_fusion.20.refs_1_, bf16[128,4096]{1,0:T(8,128)(2,1)S(1)} %collective-permute-done.54.refs_2_, ...), custom_call_target="tpu_custom_call", output_to_operand_aliasing={{0}: (5, {})} | custom-call | flops 1 | bytes 1 | tf_op jit(solution)/shard_map/down_gradient/pallas_call | solution.py:90
  357.4 7.9 %down_gradient.5 = (bf16[4096,1024]{1,0:T(8,128)(2,1)}, f32[8,128]{1,0:T(8,128)}) custom-call(bf16[512,1024]{1,0:T(8,128)(2,1)S(1)} %convolution_convert_fusion.refs_0_, bf16[512,4096]{1,0:T(8,128)(2,1)S(1)} %bitcast.161, f32[8,128]{1,0:T(8,128)S(1)} %get-tuple-element.374.refs_2_, bf16[8,128]{1,0:T(8,128)(2,1)S(1)} %slice.599.refs_3_, ...), custom_call_target="tpu_custom_call" | custom-call | flops 1 | bytes 1 | tf_op jit(solution)/shard_map/down_gradient/pallas_call | solution.py:90
  (295 shorter events, 107.6 us)
Async XLA Ops:
  7.2 348.0 %all-gather.3.cloned.1.call-start = ((), (), s32[]{:S(2)}) async-start(), calls=%async_computation | async-start | bytes 4718592 | tf_op jit(solution)/shard_map/all_gather | solution.py:323
  20.3 27.5 %collective-permute-start.4 = (bf16[1,256,1024]{1,2,0:T(8,128)(2,1)S(1)}, bf16[1,256,1024]{1,2,0:T(8,128)(2,1)S(1)}, u32[]{:S(2)}, u32[]{:S(2)}) collective-permute-start(bf16[1,256,1024]{1,2,0:T(8,128)(2,1)S(1)} %bitcast.187), channel_id=1, source_target_pairs={{0,8},{1,9},{2,10},{3,11},{4,12},{5,13},{6,14},{7,15},{8,0},{9,1},... | collective-permute-start | bytes 1572872 | tf_op jit(solution)/shard_map/ppermute | solution.py:15
  24.3 23.5 %collective-permute-start.2 = (bf16[64,4096]{1,0:T(8,128)(2,1)S(1)}, bf16[64,4096]{1,0:T(8,128)(2,1)S(1)}, u32[]{:S(2)}, u32[]{:S(2)}) collective-permute-start(bf16[64,4096]{1,0:T(8,128)(2,1)S(1)} %get-tuple-element.400), channel_id=1, source_target_pairs={{0,2},{1,3},{2,0},{3,1},{4,6},{5,7},{6,4},{7,5},{8,10},{9,11},{10,... | collective-permute-start | bytes 1572872 | tf_op jit(solution)/shard_map/ppermute | solution.py:15
  27.3 23.7 %collective-permute-start.3 = (bf16[64,4096]{1,0:T(8,128)(2,1)S(1)}, bf16[64,4096]{1,0:T(8,128)(2,1)S(1)}, u32[]{:S(2)}, u32[]{:S(2)}) collective-permute-start(bf16[64,4096]{1,0:T(8,128)(2,1)S(1)} %get-tuple-element.399), channel_id=1, source_target_pairs={{0,4},{1,5},{2,6},{3,7},{4,0},{5,1},{6,2},{7,3},{8,12},{9,13},{10,... | collective-permute-start | bytes 1572872 | tf_op jit(solution)/shard_map/ppermute | solution.py:15
  39.3 24.9 %collective-permute-start.1 = (bf16[2,128,4096]{2,1,0:T(8,128)(2,1)S(1)}, bf16[2,128,4096]{2,1,0:T(8,128)(2,1)S(1)}, u32[]{:S(2)}, u32[]{:S(2)}) collective-permute-start(bf16[2,128,4096]{2,1,0:T(8,128)(2,1)S(1)} %get-tuple-element.197), channel_id=1, source_target_pairs={{0,1},{1,0},{2,3},{3,2},{4,5},{5,4},{6,7},{7,6},{8,9},{9,8},{10,11... | collective-permute-start | bytes 6291464 | tf_op jit(solution)/shard_map/ppermute | solution.py:15
  51.7 27.1 %collective-permute-start.9 = (bf16[1,256,1024]{2,1,0:T(8,128)(2,1)S(1)}, bf16[1,256,1024]{2,1,0:T(8,128)(2,1)S(1)}, u32[]{:S(2)}, u32[]{:S(2)}) collective-permute-start(bf16[1,256,1024]{2,1,0:T(8,128)(2,1)S(1)} %bitcast.156), channel_id=1, source_target_pairs={{0,8},{1,9},{2,10},{3,11},{4,12},{5,13},{6,14},{7,15},{8,0},{9,1},... | collective-permute-start | bytes 1572872 | tf_op jit(solution)/shard_map/ppermute | solution.py:15
  65.9 24.2 %collective-permute-start.7 = (bf16[64,4096]{1,0:T(8,128)(2,1)}, bf16[64,4096]{1,0:T(8,128)(2,1)}, u32[]{:S(2)}, u32[]{:S(2)}) collective-permute-start(bf16[64,4096]{1,0:T(8,128)(2,1)} %get-tuple-element.396), channel_id=1, source_target_pairs={{0,2},{1,3},{2,0},{3,1},{4,6},{5,7},{6,4},{7,5},{8,10},{9,11},{10,... | collective-permute-start | bytes 1572872 | tf_op jit(solution)/shard_map/ppermute | solution.py:15
  65.9 24.2 %collective-permute-start.8 = (bf16[64,4096]{1,0:T(8,128)(2,1)}, bf16[64,4096]{1,0:T(8,128)(2,1)}, u32[]{:S(2)}, u32[]{:S(2)}) collective-permute-start(bf16[64,4096]{1,0:T(8,128)(2,1)} %get-tuple-element.395), channel_id=1, source_target_pairs={{0,4},{1,5},{2,6},{3,7},{4,0},{5,1},{6,2},{7,3},{8,12},{9,13},{10,... | collective-permute-start | bytes 1572872 | tf_op jit(solution)/shard_map/ppermute | solution.py:15
  66.2 27.4 %collective-permute-start.12 = (bf16[32,4096]{1,0:T(8,128)(2,1)S(1)}, bf16[32,4096]{1,0:T(8,128)(2,1)S(1)}, u32[]{:S(2)}, u32[]{:S(2)}) collective-permute-start(bf16[32,4096]{1,0:T(8,128)(2,1)S(1)} %get-tuple-element.225), channel_id=1, source_target_pairs={{0,4},{1,5},{2,6},{3,7},{4,0},{5,1},{6,2},{7,3},{8,12},{9,13},{10,... | collective-permute-start | bytes 786440 | tf_op jit(solution)/shard_map/ppermute | solution.py:15
  68.2 25.3 %collective-permute-start.13 = (bf16[32,4096]{1,0:T(8,128)(2,1)S(1)}, bf16[32,4096]{1,0:T(8,128)(2,1)S(1)}, u32[]{:S(2)}, u32[]{:S(2)}) collective-permute-start(bf16[32,4096]{1,0:T(8,128)(2,1)S(1)} %get-tuple-element.233), channel_id=1, source_target_pairs={{0,2},{1,3},{2,0},{3,1},{4,6},{5,7},{6,4},{7,5},{8,10},{9,11},{10,... | collective-permute-start | bytes 786440 | tf_op jit(solution)/shard_map/ppermute | solution.py:15
  118.3 45.0 %collective-permute-start.23 = (bf16[2,128,4096]{2,1,0:T(8,128)(2,1)}, bf16[2,128,4096]{2,1,0:T(8,128)(2,1)}, u32[]{:S(2)}, u32[]{:S(2)}) collective-permute-start(bf16[2,128,4096]{2,1,0:T(8,128)(2,1)} %get-tuple-element.242), channel_id=1, source_target_pairs={{0,1},{1,0},{2,3},{3,2},{4,5},{5,4},{6,7},{7,6},{8,9},{9,8},{10,11... | collective-permute-start | bytes 6291464 | tf_op jit(solution)/shard_map/ppermute | solution.py:15
  120.7 16.7 %collective-permute-start.15 = (bf16[64,4096]{1,0:T(8,128)(2,1)}, bf16[64,4096]{1,0:T(8,128)(2,1)}, u32[]{:S(2)}, u32[]{:S(2)}) collective-permute-start(bf16[64,4096]{1,0:T(8,128)(2,1)} %constant_dynamic-update-slice_fusion.2), channel_id=1, source_target_pairs={{0,4},{1,5},{2,6},{3,7},{4,0},{5,1},{6,2},{7,3},{8,12},{9,13},{10,... | collective-permute-start | bytes 1572872 | tf_op jit(solution)/shard_map/ppermute | solution.py:15
  122.4 32.2 %collective-permute-start.17 = (bf16[64,4096]{1,0:T(8,128)(2,1)}, bf16[64,4096]{1,0:T(8,128)(2,1)S(1)}, u32[]{:S(2)}, u32[]{:S(2)}) collective-permute-start(bf16[64,4096]{1,0:T(8,128)(2,1)} %get-tuple-element.392), channel_id=1, source_target_pairs={{0,2},{1,3},{2,0},{3,1},{4,6},{5,7},{6,4},{7,5},{8,10},{9,11},{10,... | collective-permute-start | bytes 1572872 | tf_op jit(solution)/shard_map/ppermute | solution.py:15
  122.9 36.4 %collective-permute-start.18 = (bf16[64,4096]{1,0:T(8,128)(2,1)}, bf16[64,4096]{1,0:T(8,128)(2,1)}, u32[]{:S(2)}, u32[]{:S(2)}) collective-permute-start(bf16[64,4096]{1,0:T(8,128)(2,1)} %get-tuple-element.391), channel_id=1, source_target_pairs={{0,4},{1,5},{2,6},{3,7},{4,0},{5,1},{6,2},{7,3},{8,12},{9,13},{10,... | collective-permute-start | bytes 1572872 | tf_op jit(solution)/shard_map/ppermute | solution.py:15
  137.4 30.1 %collective-permute-start.22 = (bf16[64,4096]{1,0:T(8,128)(2,1)S(1)}, bf16[64,4096]{1,0:T(8,128)(2,1)S(1)}, u32[]{:S(2)}, u32[]{:S(2)}) collective-permute-start(bf16[64,4096]{1,0:T(8,128)(2,1)S(1)} %collective-permute-done.14.refs_1_.refs_2_), channel_id=1, source_target_pairs={{0,1},{1,0},{2,3},{3,2},{4,5},{5,4},{6,7},{7,6},{8,9},{9,8},{10,11... | collective-permute-start | bytes 1572872 | tf_op jit(solution)/shard_map/ppermute | solution.py:15
  137.5 30.0 %collective-permute-start.21 = (bf16[64,4096]{1,0:T(8,128)(2,1)S(1)}, bf16[64,4096]{1,0:T(8,128)(2,1)S(1)}, u32[]{:S(2)}, u32[]{:S(2)}) collective-permute-start(bf16[64,4096]{1,0:T(8,128)(2,1)S(1)} %constant_dynamic-update-slice_fusion.refs_0_.refs_1_), channel_id=1, source_target_pairs={{0,1},{1,0},{2,3},{3,2},{4,5},{5,4},{6,7},{7,6},{8,9},{9,8},{10,11... | collective-permute-start | bytes 1572872 | tf_op jit(solution)/shard_map/ppermute | solution.py:15
  160.8 16.4 %collective-permute-start.19 = (bf16[32,4096]{1,0:T(8,128)(2,1)S(1)}, bf16[32,4096]{1,0:T(8,128)(2,1)S(1)}, u32[]{:S(2)}, u32[]{:S(2)}) collective-permute-start(bf16[32,4096]{1,0:T(8,128)(2,1)S(1)} %get-tuple-element.390), channel_id=1, source_target_pairs={{0,4},{1,5},{2,6},{3,7},{4,0},{5,1},{6,2},{7,3},{8,12},{9,13},{10,... | collective-permute-start | bytes 786440 | tf_op jit(solution)/shard_map/ppermute | solution.py:15
  165.5 16.1 %collective-permute-start.26 = (bf16[64,4096]{1,0:T(8,128)(2,1)S(1)}, bf16[64,4096]{1,0:T(8,128)(2,1)S(1)}, u32[]{:S(2)}, u32[]{:S(2)}) collective-permute-start(bf16[64,4096]{1,0:T(8,128)(2,1)S(1)} %get-tuple-element.388), channel_id=1, source_target_pairs={{0,2},{1,3},{2,0},{3,1},{4,6},{5,7},{6,4},{7,5},{8,10},{9,11},{10,... | collective-permute-start | bytes 1572872 | tf_op jit(solution)/shard_map/ppermute | solution.py:15
  179.5 17.3 %collective-permute-start.24 = (bf16[32,4096]{1,0:T(8,128)(2,1)S(1)}, bf16[32,4096]{1,0:T(8,128)(2,1)S(1)}, u32[]{:S(2)}, u32[]{:S(2)}) collective-permute-start(bf16[32,4096]{1,0:T(8,128)(2,1)S(1)} %get-tuple-element.268), channel_id=1, source_target_pairs={{0,4},{1,5},{2,6},{3,7},{4,0},{5,1},{6,2},{7,3},{8,12},{9,13},{10,... | collective-permute-start | bytes 786440 | tf_op jit(solution)/shard_map/ppermute | solution.py:15
  181.5 15.3 %collective-permute-start.25 = (bf16[32,4096]{1,0:T(8,128)(2,1)S(1)}, bf16[32,4096]{1,0:T(8,128)(2,1)S(1)}, u32[]{:S(2)}, u32[]{:S(2)}) collective-permute-start(bf16[32,4096]{1,0:T(8,128)(2,1)S(1)} %get-tuple-element.270), channel_id=1, source_target_pairs={{0,2},{1,3},{2,0},{3,1},{4,6},{5,7},{6,4},{7,5},{8,10},{9,11},{10,... | collective-permute-start | bytes 786440 | tf_op jit(solution)/shard_map/ppermute | solution.py:15
  199.0 17.5 %collective-permute-start.28 = (bf16[64,4096]{1,0:T(8,128)(2,1)}, bf16[64,4096]{1,0:T(8,128)(2,1)}, u32[]{:S(2)}, u32[]{:S(2)}) collective-permute-start(bf16[64,4096]{1,0:T(8,128)(2,1)} %constant_dynamic-update-slice_fusion.4.refs_0_.refs_5_), channel_id=1, source_target_pairs={{0,2},{1,3},{2,0},{3,1},{4,6},{5,7},{6,4},{7,5},{8,10},{9,11},{10,... | collective-permute-start | bytes 1572872 | tf_op jit(solution)/shard_map/ppermute | solution.py:15
  224.8 22.6 %collective-permute-start.38 = (bf16[64,4096]{1,0:T(8,128)(2,1)S(1)}, bf16[64,4096]{1,0:T(8,128)(2,1)S(1)}, u32[]{:S(2)}, u32[]{:S(2)}) collective-permute-start(bf16[64,4096]{1,0:T(8,128)(2,1)S(1)} %constant_dynamic-update-slice_fusion.8.refs_0_.refs_5_), channel_id=1, source_target_pairs={{0,2},{1,3},{2,0},{3,1},{4,6},{5,7},{6,4},{7,5},{8,10},{9,11},{10,... | collective-permute-start | bytes 1572872 | tf_op jit(solution)/shard_map/ppermute | solution.py:15
  226.0 21.4 %collective-permute-start.39 = (bf16[64,4096]{1,0:T(8,128)(2,1)S(1)}, bf16[64,4096]{1,0:T(8,128)(2,1)S(1)}, u32[]{:S(2)}, u32[]{:S(2)}) collective-permute-start(bf16[64,4096]{1,0:T(8,128)(2,1)S(1)} %constant_dynamic-update-slice_fusion.10), channel_id=1, source_target_pairs={{0,4},{1,5},{2,6},{3,7},{4,0},{5,1},{6,2},{7,3},{8,12},{9,13},{10,... | collective-permute-start | bytes 1572872 | tf_op jit(solution)/shard_map/ppermute | solution.py:15
  252.3 18.8 %collective-permute-start.42 = (bf16[128,4096]{1,0:T(8,128)(2,1)S(1)}, bf16[128,4096]{1,0:T(8,128)(2,1)S(1)}, u32[]{:S(2)}, u32[]{:S(2)}) collective-permute-start(bf16[128,4096]{1,0:T(8,128)(2,1)S(1)} %constant_dynamic-update-slice_fusion.16.refs_1_), channel_id=1, source_target_pairs={{0,1},{1,0},{2,3},{3,2},{4,5},{5,4},{6,7},{7,6},{8,9},{9,8},{10,11... | collective-permute-start | bytes 3145736 | tf_op jit(solution)/shard_map/ppermute | solution.py:15
  253.6 17.5 %collective-permute-start.43 = (bf16[128,4096]{1,0:T(8,128)(2,1)S(1)}, bf16[128,4096]{1,0:T(8,128)(2,1)S(1)}, u32[]{:S(2)}, u32[]{:S(2)}) collective-permute-start(bf16[128,4096]{1,0:T(8,128)(2,1)S(1)} %constant_dynamic-update-slice_fusion.18.refs_3_), channel_id=1, source_target_pairs={{0,1},{1,0},{2,3},{3,2},{4,5},{5,4},{6,7},{7,6},{8,9},{9,8},{10,11... | collective-permute-start | bytes 3145736 | tf_op jit(solution)/shard_map/ppermute | solution.py:15
  258.2 20.8 %collective-permute-start.40 = (bf16[64,4096]{1,0:T(8,128)(2,1)S(1)}, bf16[64,4096]{1,0:T(8,128)(2,1)S(1)}, u32[]{:S(2)}, u32[]{:S(2)}) collective-permute-start(bf16[64,4096]{1,0:T(8,128)(2,1)S(1)} %constant_dynamic-update-slice_fusion.12.refs_0_.refs_1_), channel_id=1, source_target_pairs={{0,2},{1,3},{2,0},{3,1},{4,6},{5,7},{6,4},{7,5},{8,10},{9,11},{10,... | collective-permute-start | bytes 1572872 | tf_op jit(solution)/shard_map/ppermute | solution.py:15
  260.0 18.9 %collective-permute-start.41 = (bf16[64,4096]{1,0:T(8,128)(2,1)S(1)}, bf16[64,4096]{1,0:T(8,128)(2,1)S(1)}, u32[]{:S(2)}, u32[]{:S(2)}) collective-permute-start(bf16[64,4096]{1,0:T(8,128)(2,1)S(1)} %constant_dynamic-update-slice_fusion.14), channel_id=1, source_target_pairs={{0,4},{1,5},{2,6},{3,7},{4,0},{5,1},{6,2},{7,3},{8,12},{9,13},{10,... | collective-permute-start | bytes 1572872 | tf_op jit(solution)/shard_map/ppermute | solution.py:15
  270.6 24.8 %collective-permute-start.48 = (bf16[256,1024]{1,0:T(8,128)(2,1)S(1)}, bf16[256,1024]{1,0:T(8,128)(2,1)S(1)}, u32[]{:S(2)}, u32[]{:S(2)}) collective-permute-start(bf16[256,1024]{1,0:T(8,128)(2,1)S(1)} %convert_element_type.512), channel_id=1, source_target_pairs={{0,8},{1,9},{2,10},{3,11},{4,12},{5,13},{6,14},{7,15},{8,0},{9,1},... | collective-permute-start | bytes 1572872 | tf_op jit(solution)/shard_map/ppermute | solution.py:15
  279.6 58.3 %collective-permute-start.55 = (bf16[128,4096]{1,0:T(8,128)(2,1)S(1)}, bf16[128,4096]{1,0:T(8,128)(2,1)S(1)}, u32[]{:S(2)}, u32[]{:S(2)}) collective-permute-start(bf16[128,4096]{1,0:T(8,128)(2,1)S(1)} %constant_dynamic-update-slice_fusion.22.refs_3_), channel_id=1, source_target_pairs={{0,1},{1,0},{2,3},{3,2},{4,5},{5,4},{6,7},{7,6},{8,9},{9,8},{10,11... | collective-permute-start | bytes 3145736 | tf_op jit(solution)/shard_map/ppermute | solution.py:15
  296.1 30.1 %collective-permute-start.51 = (bf16[1,128,1024]{2,1,0:T(8,128)(2,1)S(1)}, bf16[1,128,1024]{2,1,0:T(8,128)(2,1)S(1)}, u32[]{:S(2)}, u32[]{:S(2)}) collective-permute-start(bf16[1,128,1024]{2,1,0:T(8,128)(2,1)S(1)} %get-tuple-element.414), channel_id=1, source_target_pairs={{0,8},{1,9},{2,10},{3,11},{4,12},{5,13},{6,14},{7,15},{8,0},{9,1},... | collective-permute-start | bytes 786440 | tf_op jit(solution)/shard_map/ppermute | solution.py:15
  296.1 23.3 %collective-permute-start.49 = (bf16[1,128,1024]{2,1,0:T(8,128)(2,1)S(1)}, bf16[1,128,1024]{2,1,0:T(8,128)(2,1)S(1)}, u32[]{:S(2)}, u32[]{:S(2)}) collective-permute-start(bf16[1,128,1024]{2,1,0:T(8,128)(2,1)S(1)} %get-tuple-element.413), channel_id=1, source_target_pairs={{0,8},{1,9},{2,10},{3,11},{4,12},{5,13},{6,14},{7,15},{8,0},{9,1},... | collective-permute-start | bytes 786440 | tf_op jit(solution)/shard_map/ppermute | solution.py:15
  347.8 17.5 %collective-permute-start.57 = (bf16[32,2048]{1,0:T(8,128)(2,1)S(1)}, bf16[32,2048]{1,0:T(8,128)(2,1)S(1)}, u32[]{:S(2)}, u32[]{:S(2)}) collective-permute-start(bf16[32,2048]{1,0:T(8,128)(2,1)S(1)} %get-tuple-element.404), channel_id=1, source_target_pairs={{0,4},{1,5},{2,6},{3,7},{4,0},{5,1},{6,2},{7,3},{8,12},{9,13},{10,... | collective-permute-start | bytes 393224 | tf_op jit(solution)/shard_map/ppermute | solution.py:15
  (66 other events, 658.6 us)
Sparse Core Ops, SparseCore 0:
  123.4 41.7 all-gather.2

commit v5 on v4

--- a/solution.py
+++ b/solution.py
@@ -63,6 +63,12 @@
     return contract(chooser, value, 1, 0).astype(jnp.bfloat16)
 
 
+def turned_contract(left, right):
+    if left.shape[0] % 128 or right.shape[0] % 128:
+        return contract(left, right, 1, 1)
+    return contract(right, left, 1, 1).T
+
+
 def estimate():
     return pl.CostEstimate(flops=1, bytes_accessed=1, transcendentals=0)
 
@@ -81,7 +87,7 @@
     return pl.BlockSpec(part.shape, lambda at: (0,) * part.ndim)
 
 
-def run(kernel, operands, in_specs, out_specs, out_shape, grid, name, marks, aliases=None):
+def run(kernel, operands, in_specs, out_specs, out_shape, grid, name, marks, aliases=None, scratch=()):
     count = len(operands)
 
     def body_of(*refs):
@@ -94,6 +100,7 @@
         out_specs=out_specs,
         out_shape=out_shape,
         input_output_aliases=aliases or {},
+        scratch_shapes=scratch,
         compiler_params=params(),
         cost_estimate=estimate(),
         name=name,
@@ -110,7 +117,7 @@
         pre = jnp.dot(in_ref[...], up_ref[...], preferred_element_type=jnp.float32)
         keep_ref[0] = pre[:half]
         send_ref[0] = pre[half:].astype(jnp.bfloat16)
-        hidden = contract(grad_ref[...], down_ref[...], 1, 1)
+        hidden = turned_contract(grad_ref[...], down_ref[...])
         keep_ref[1] = hidden[:half]
         send_ref[1] = hidden[half:].astype(jnp.bfloat16)
 
@@ -149,18 +156,27 @@
     skip = first // tile
     begin = [] if start is None else [start]
 
+    last = width // tile - 1
+    turned = count % 128 == 0
+
     def kernel(*refs):
-        up_ref, out_ref = refs[len(pieces)], refs[-1]
+        up_ref, out_ref = refs[len(pieces)], refs[-2]
+        total_ref = refs[-1]
         rows = jnp.concatenate([ref[...] for ref in refs[: len(pieces)]], axis=0)
-        part = contract(rows, up_ref[...], 1, 1)
+        part = contract(up_ref[...], rows, 1, 1) if turned else contract(rows, up_ref[...], 1, 1)
 
         @pl.when(pl.program_id(0) == 0)
         def _():
-            out_ref[...] = part + refs[-2][...] if begin else part
+            total_ref[...] = part
 
         @pl.when(pl.program_id(0) != 0)
         def _():
-            out_ref[...] += part
+            total_ref[...] += part
+
+        @pl.when(pl.program_id(0) == last)
+        def _():
+            total = total_ref[...].T if turned else total_ref[...]
+            out_ref[...] = total + refs[-3][...] if begin else total
 
     result = jax.ShapeDtypeStruct((count, depth), jnp.float32)
     return run(
@@ -174,6 +190,7 @@
         (width // tile,),
         "input_part",
         marks,
+        scratch=[pltpu.VMEM((depth, count) if turned else (count, depth), jnp.float32)],
     )
 
 
@@ -245,7 +262,7 @@
     half = count // 2
 
     def kernel(rows_ref, proj_ref, keep_ref, send_ref):
-        part = contract(rows_ref[0], proj_ref[...], 1, 1)
+        part = turned_contract(rows_ref[0], proj_ref[...])
         keep_ref[...] = part[:half]
         send_ref[...] = part[half:].astype(jnp.bfloat16)
 
@@ -320,7 +337,6 @@
     groups = [
         [at + low for at in range(SHARES)] for low in range(0, lax.axis_size("gx"), SHARES)
     ]
-    context_all = lax.all_gather(context, "gx", axis_index_groups=groups, tiled=True)
     chunks = {"own": own_rows}
     grads_nf = picked(source_nf, grads)
 
@@ -489,12 +505,15 @@
     sums(mine_a)
     sums_core(mine_a)
     sums(mine_b)
+    sums_one(mine_a)
     fetch(0)
-    sums_one(mine_a)
     gelu(mine_a)
     spread(mine_a)
     sums_core(mine_b)
     fetch(1)
+    in_all = jnp.concatenate([chunks[name][0] for name in ("own", "other")], axis=0)
+    turned = in_all.T
+    grad_all = jnp.concatenate([chunks[name][1] for name in ("own", "other")], axis=0)
     sums(other_a)
     sums_one(mine_b)
     spread_one(mine_a)
@@ -503,46 +522,43 @@
     sums(other_b)
     spread_two(mine_a)
     sums_one(other_a)
-    sums_core(other_b)
     back(mine_a)
     gelu(other_a)
     spread(other_a)
+    sums_core(other_b)
+    spread_one(other_a)
     sums_one(other_b)
-    in_all = jnp.concatenate([chunks[name][0] for name in ("own", "other")], axis=0)
-    turned = in_all.T
-    grad_all = jnp.concatenate([chunks[name][1] for name in ("own", "other")], axis=0)
-    spread_one(other_a)
     gelu(other_b)
     spread(other_b)
     spread_two(other_a)
     spread_one(other_b)
     back(other_a)
+    spread(mine_b)
     act_core(mine_a)
-    spread(mine_b)
+    spread_two(other_b)
+    spread_one(mine_b)
+    context_all = lax.all_gather(held(context), "gx", axis_index_groups=groups, tiled=True)
+    back(other_b)
+    q_sums()
+    act_core(other_a)
+    spread_two(mine_b)
     pieces = [piece for name in (mine_a, other_a) for piece in dpre_rows[name]]
     d_up, late[0] = up_gradient(turned, pieces, 0, width, marks=marks())
-    spread_two(other_b)
-    act_core(other_a)
-    spread_one(mine_b)
-    back(other_b)
-    q_sums()
     pieces = [piece for name in (mine_a, other_a) for piece in act_rows[name]]
     d_down, late[0] = down_gradient(pieces, grad_all, 0, width, marks=marks())
-    spread_two(mine_b)
     act_core(other_b)
     back(mine_b)
+    finish_rows()
     act_core(mine_b)
-    finish_rows()
     pieces = [piece for name in (mine_b, other_b) for piece in dpre_rows[name]]
     d_up, late[0] = up_gradient(turned, pieces, part_width, width, d_up, marks=marks())
+    pieces = [piece for name in (mine_b, other_b) for piece in act_rows[name]]
+    d_down, late[0] = down_gradient(pieces, grad_all, part_width, width, d_down, marks=marks())
+    context_all = held(context_all)
     context_sums(0)
     context_sums(1)
     context_core(0)
     context_core(1)
-    pieces = [piece for name in (mine_b, other_b) for piece in act_rows[name]]
-    d_down, late[0] = down_gradient(pieces, grad_all, part_width, width, d_down, marks=marks())
-    context_one(0)
-    context_one(1)
     tokens = jnp.arange(q_count * rows, dtype=jnp.int32)
     local = tokens % rows
     source = ((tokens // rows) ^ own_q) * half_rows + (local // (2 * GROUP)) * GROUP
@@ -552,6 +568,8 @@
     d_output, late[0] = down_gradient(
         [context_all], d_input_all, 0, context_all.shape[1], marks=marks()
     )
+    context_one(0)
+    context_one(1)
     context_two(0)
     context_two(1)
 

time: 378 us -> 347 us (0.918)
  waiting for transfers between devices: 126 us -> 89.6 us
  Pallas kernels: 128 us -> 135 us
  other arithmetic: 21.5 us -> 15.3 us
    ppermute x63, waiting for transfers between devices: 126 us -> 89.5 us  [swap(): return lax.ppermute(value, 'gx', [(at, at ^ mask) for at in range(count)])]
    pallas_call x15, Pallas kernels: 128 us -> 135 us  [run(): pl.pallas_call(body_of, grid=grid, in_specs=list(in_specs) + [pl.BlockSpe...]
    unnamed x80 -> x130, local copies, waits for them, and re-layouts: 11.6 us -> 14.7 us
  transfers between devices with their start and end apart: 64 -> 64, of which waited for: 24 -> 25; matrix products, arithmetic and copies ran while one was open for 10% -> 9% of each run, Pallas kernels for 28% -> 36%
where the time goes in v5:
time: 347 us; the launch traced here: 344 us
  Pallas kernels  135 us (39%)
  waiting for transfers between devices  89.6 us (26%)
  starting transfers between devices  59.2 us (17%)
  local copies, waits for them, and re-layouts  23.5 us (7%)
  between operations  15.5 us (4%)
  other arithmetic  15.3 us (4%)
  matrix products  5.86 us (2%)
    pallas_call x15, Pallas kernels, run(): pl.pallas_call(body_of, grid=grid, in_specs=list(in_specs) + [pl.BlockSpe...  135 us
    ppermute x63, waiting for transfers between devices, swap(): return lax.ppermute(value, 'gx', [(at, at ^ mask) for at in range(count)])  89.5 us
    ppermute x63, starting transfers between devices, swap(): return lax.ppermute(value, 'gx', [(at, at ^ mask) for at in range(count)])  59.1 us
    unnamed x130, local copies, waits for them, and re-layouts  14.7 us
    convert_element_type x8, other arithmetic, halved(): return summed(parts, which, slice(count, 2 * count)).astype(jnp.bfloat16)  7.13 us
  transfers between devices with their start and end apart: 64, of which 25 were waited for; matrix products, arithmetic and copies ran while one was open for 9% of the time, Pallas kernels for 36%

profile of v5, /device:TPU:0, one launch (start us, length us, event | category | flops | bytes accessed | tf_op | source)
XLA Modules:
  0.0 344.2 jit_solution(4790072398469160624)
XLA Ops:
  9.4 10.8 %hidden_parts.4 = (f32[2,128,4096]{2,1,0:T(8,128)S(1)}, bf16[2,128,4096]{2,1,0:T(8,128)(2,1)S(1)}) custom-call(bf16[256,1024]{1,0:T(8,128)(2,1)S(1)} %copy.15.refs_0_, bf16[256,1024]{1,0:T(8,128)(2,1)S(1)} %convolution_convert_fusion.7.refs_1_, bf16[1024,8192]{1,0:T(8,128)(2,1)} %bitcast.165, bf16[8192,1024]{1,0:T(8,128)(2,1)} %bitcast.173, ...), custom_call_target="tpu_custom_call" | custom-call | flops 1 | bytes 1 | tf_op jit(solution)/shard_map/hidden_parts/pallas_call | solution.py:96
  20.7 3.8 %collective-permute-done = bf16[2,128,4096]{2,1,0:T(8,128)(2,1)S(1)} collective-permute-done((bf16[2,128,4096]{2,1,0:T(8,128)(2,1)S(1)}, bf16[2,128,4096]{2,1,0:T(8,128)(2,1)S(1)}, u32[]{:S(2)}, u32[]{:S(2)}) %collective-permute-start) | collective-permute-done | bytes 2097184 | tf_op jit(solution)/shard_map/ppermute | solution.py:15
  24.6 3.0 collective-permute-start.2
  31.8 10.8 %hidden_parts.5 = (f32[2,128,4096]{2,1,0:T(8,128)S(1)}, bf16[2,128,4096]{2,1,0:T(8,128)(2,1)S(1)}) custom-call(bf16[256,1024]{1,0:T(8,128)(2,1)S(1)} %copy.15.refs_0_, bf16[256,1024]{1,0:T(8,128)(2,1)S(1)} %convolution_convert_fusion.7.refs_1_, bf16[1024,8192]{1,0:T(8,128)(2,1)} %bitcast.166, bf16[8192,1024]{1,0:T(8,128)(2,1)} %bitcast.174, ...), custom_call_target="tpu_custom_call" | custom-call | flops 1 | bytes 1 | tf_op jit(solution)/shard_map/hidden_parts/pallas_call | solution.py:96
  42.7 9.7 %collective-permute-done.3 = bf16[64,4096]{1,0:T(8,128)(2,1)S(1)} collective-permute-done((bf16[64,4096]{1,0:T(8,128)(2,1)S(1)}, bf16[64,4096]{1,0:T(8,128)(2,1)S(1)}, u32[]{:S(2)}, u32[]{:S(2)}) %collective-permute-start.3) | collective-permute-done | bytes 524320 | tf_op jit(solution)/shard_map/ppermute | solution.py:15
  53.1 3.1 collective-permute-start.9
  56.2 8.8 %collective-permute-done.4 = bf16[32,4096]{1,0:T(8,128)(2,1)S(1)} collective-permute-done((bf16[32,4096]{1,0:T(8,128)(2,1)S(1)}, bf16[32,4096]{1,0:T(8,128)(2,1)S(1)}, u32[]{:S(2)}, u32[]{:S(2)}) %collective-permute-start.4) | collective-permute-done | bytes 262176 | tf_op jit(solution)/shard_map/ppermute | solution.py:15
  72.3 5.9 %collective-permute-done.9 = bf16[1,256,1024]{2,1,0:T(8,128)(2,1)S(1)} collective-permute-done((bf16[1,256,1024]{2,1,0:T(8,128)(2,1)S(1)}, bf16[1,256,1024]{2,1,0:T(8,128)(2,1)S(1)}, u32[]{:S(2)}, u32[]{:S(2)}) %collective-permute-start.9) | collective-permute-done | bytes 524320 | tf_op jit(solution)/shard_map/ppermute | solution.py:15
  78.2 11.0 %hidden_parts.6 = (f32[2,128,4096]{2,1,0:T(8,128)S(1)}, bf16[2,128,4096]{2,1,0:T(8,128)(2,1)S(1)}) custom-call(bf16[256,1024]{1,0:T(8,128)(2,1)S(1)} %copy.16.refs_0_, bf16[256,1024]{1,0:T(8,128)(2,1)S(1)} %bitcast.158, bf16[1024,8192]{1,0:T(8,128)(2,1)} %bitcast.167, bf16[8192,1024]{1,0:T(8,128)(2,1)} %bitcast.175, bf16[8,128]{1,0:T(8,128)(2,1)S(1)} %slice.568.refs_4_, ...), custom_call_target="tpu_custom_call" | custom-call | flops 1 | bytes 1 | tf_op jit(solution)/shard_map/hidden_parts/pallas_call | solution.py:96
  95.2 4.7 %collective-permute-done.10 = bf16[32,4096]{1,0:T(8,128)(2,1)S(1)} collective-permute-done((bf16[32,4096]{1,0:T(8,128)(2,1)S(1)}, bf16[32,4096]{1,0:T(8,128)(2,1)S(1)}, u32[]{:S(2)}, u32[]{:S(2)}) %collective-permute-start.10) | collective-permute-done | bytes 262176 | tf_op jit(solution)/shard_map/ppermute | solution.py:15
  107.0 10.9 %hidden_parts.7 = (f32[2,128,4096]{2,1,0:T(8,128)S(1)}, bf16[2,128,4096]{2,1,0:T(8,128)(2,1)S(1)}) custom-call(bf16[256,1024]{1,0:T(8,128)(2,1)S(1)} %copy.16.refs_0_, bf16[256,1024]{1,0:T(8,128)(2,1)S(1)} %bitcast.159, bf16[1024,8192]{1,0:T(8,128)(2,1)} %bitcast.168, bf16[8192,1024]{1,0:T(8,128)(2,1)} %bitcast.176, bf16[8,128]{1,0:T(8,128)(2,1)S(1)} %slice.574.refs_4_, ...), custom_call_target="tpu_custom_call" | custom-call | flops 1 | bytes 1 | tf_op jit(solution)/shard_map/hidden_parts/pallas_call | solution.py:96
  119.4 2.7 collective-permute-done.15
  125.5 8.8 %input_part.4.refs_5_ = f32[256,1024]{1,0:T(8,128)S(1)} custom-call(bf16[64,4096]{1,0:T(8,128)(2,1)S(1)} %constant_dynamic-update-slice_fusion.refs_0_.refs_1_, bf16[64,4096]{1,0:T(8,128)(2,1)S(1)} %collective-permute-done.17.refs_1_.refs_2_, bf16[64,4096]{1,0:T(8,128)(2,1)S(1)} %collective-permute-done.21.refs_2_.refs_3_, ...), custom_call_target="tpu_custom_call" | custom-call | flops 1 | bytes 1 | tf_op jit(solution)/shard_map/input_part/pallas_call | solution.py:96
  140.6 3.6 %collective-permute-done.23 = bf16[32,4096]{1,0:T(8,128)(2,1)S(1)} collective-permute-done((bf16[32,4096]{1,0:T(8,128)(2,1)S(1)}, bf16[32,4096]{1,0:T(8,128)(2,1)S(1)}, u32[]{:S(2)}, u32[]{:S(2)}) %collective-permute-start.23) | collective-permute-done | bytes 262176 | tf_op jit(solution)/shard_map/ppermute | solution.py:15
  146.4 7.1 %collective-permute-done.28 = bf16[64,4096]{1,0:T(8,128)(2,1)S(1)} collective-permute-done((bf16[64,4096]{1,0:T(8,128)(2,1)S(1)}, bf16[64,4096]{1,0:T(8,128)(2,1)S(1)}, u32[]{:S(2)}, u32[]{:S(2)}) %collective-permute-start.28) | collective-permute-done | bytes 524320 | tf_op jit(solution)/shard_map/ppermute | solution.py:15
  159.0 11.1 %collective-permute-done.30 = bf16[32,4096]{1,0:T(8,128)(2,1)S(1)} collective-permute-done((bf16[32,4096]{1,0:T(8,128)(2,1)S(1)}, bf16[32,4096]{1,0:T(8,128)(2,1)S(1)}, u32[]{:S(2)}, u32[]{:S(2)}) %collective-permute-start.30) | collective-permute-done | bytes 262176 | tf_op jit(solution)/shard_map/ppermute | solution.py:15
  173.6 4.6 %collective-permute-done.34 = bf16[32,4096]{1,0:T(8,128)(2,1)S(1)} collective-permute-done((bf16[32,4096]{1,0:T(8,128)(2,1)S(1)}, bf16[32,4096]{1,0:T(8,128)(2,1)S(1)}, u32[]{:S(2)}, u32[]{:S(2)}) %collective-permute-start.34) | collective-permute-done | bytes 262176 | tf_op jit(solution)/shard_map/ppermute | solution.py:15
  181.2 8.9 %input_part.5.refs_5_ = f32[256,1024]{1,0:T(8,128)S(1)} custom-call(bf16[64,4096]{1,0:T(8,128)(2,1)S(1)} %constant_dynamic-update-slice_fusion.4.refs_0_.refs_5_, bf16[64,4096]{1,0:T(8,128)(2,1)S(1)} %collective-permute-done.26.refs_1_.refs_6_, bf16[64,4096]{1,0:T(8,128)(2,1)S(1)} %collective-permute-done.32.refs_2_.refs_7_, ...), custom_call_target="tpu_custom_call" | custom-call | flops 1 | bytes 1 | tf_op jit(solution)/shard_map/input_part/pallas_call | solution.py:96
  204.2 9.0 %input_part.6 = f32[256,1024]{1,0:T(8,128)S(1)} custom-call(bf16[64,4096]{1,0:T(8,128)(2,1)S(1)} %constant_dynamic-update-slice_fusion.8.refs_0_.refs_5_, bf16[64,4096]{1,0:T(8,128)(2,1)} %collective-permute-done.38.refs_1_.refs_6_, bf16[64,4096]{1,0:T(8,128)(2,1)S(1)} %collective-permute-done.42.refs_2_.refs_7_, ...), custom_call_target="tpu_custom_call" | custom-call | flops 1 | bytes 1 | tf_op jit(solution)/shard_map/input_part/pallas_call | solution.py:96
  214.5 3.0 collective-permute-start.48
  218.9 4.7 %collective-permute-done.40.refs_1_.refs_2_ = bf16[64,4096]{1,0:T(8,128)(2,1)S(1)} collective-permute-done((bf16[64,4096]{1,0:T(8,128)(2,1)S(1)}, bf16[64,4096]{1,0:T(8,128)(2,1)S(1)}, u32[]{:S(2)}, u32[]{:S(2)}) %collective-permute-start.40) | collective-permute-done | bytes 524320 | tf_op jit(solution)/shard_map/ppermute | solution.py:15
  226.7 7.7 %up_gradient.2 = (bf16[1024,8192]{1,0:T(8,128)(2,1)}, f32[8,128]{1,0:T(8,128)S(1)}) custom-call(bf16[1024,512]{1,0:T(8,128)(2,1)S(1)} %maximum_bitcast_fusion.refs_0_, bf16[64,4096]{1,0:T(8,128)(2,1)S(1)} %copy-done.15, bf16[64,4096]{1,0:T(8,128)(2,1)S(1)} %copy-done.17, bf16[64,4096]{1,0:T(8,128)(2,1)S(1)} %copy-done.25, bf16[64,4096]{1,0:T(8,128)(2,1)S(1)} %copy-done.23, ...), custom_call_target="tpu_custom_call" | custom-call | flops 1 | bytes 1 | tf_op jit(solution)/shard_map/up_gradient/pallas_call | solution.py:96
  234.4 10.0 %down_gradient.3 = (bf16[8192,1024]{1,0:T(8,128)(2,1)}, f32[8,128]{1,0:T(8,128)S(1)}) custom-call(bf16[512,1024]{1,0:T(8,128)(2,1)S(1)} %pad_maximum_fusion.refs_0_, bf16[128,4096]{1,0:T(8,128)(2,1)} %constant_dynamic-update-slice_fusion.16.refs_1_, bf16[128,4096]{1,0:T(8,128)(2,1)} %collective-permute-done.46.refs_2_, ...), custom_call_target="tpu_custom_call" | custom-call | flops 1 | bytes 1 | tf_op jit(solution)/shard_map/down_gradient/pallas_call | solution.py:96
  244.4 8.8 %input_part.7 = f32[256,1024]{1,0:T(8,128)S(1)} custom-call(bf16[64,4096]{1,0:T(8,128)(2,1)S(1)} %constant_dynamic-update-slice_fusion.12.refs_0_.refs_1_, bf16[64,4096]{1,0:T(8,128)(2,1)S(1)} %collective-permute-done.40.refs_1_.refs_2_, bf16[64,4096]{1,0:T(8,128)(2,1)S(1)} %collective-permute-done.44.refs_2_.refs_3_, ...), custom_call_target="tpu_custom_call" | custom-call | flops 1 | bytes 1 | tf_op jit(solution)/shard_map/input_part/pallas_call | solution.py:96
  259.0 3.4 collective-permute-start.49
  269.3 8.6 %up_gradient.3 = (bf16[1024,8192]{1,0:T(8,128)(2,1)}, f32[8,128]{1,0:T(8,128)S(1)}) custom-call(bf16[1024,512]{1,0:T(8,128)(2,1)S(1)} %maximum_bitcast_fusion.refs_0_, bf16[64,4096]{1,0:T(8,128)(2,1)S(1)} %copy-done.11, bf16[64,4096]{1,0:T(8,128)(2,1)S(1)} %copy-done.21, bf16[64,4096]{1,0:T(8,128)(2,1)S(1)} %copy-done.35, ...), custom_call_target="tpu_custom_call", output_to_operand_aliasing={{0}: (9, {})} | custom-call | flops 1 | bytes 1 | tf_op jit(solution)/shard_map/up_gradient/pallas_call | solution.py:96
  281.1 10.3 %down_gradient.4 = (bf16[8192,1024]{1,0:T(8,128)(2,1)}, f32[8,128]{1,0:T(8,128)S(1)}) custom-call(bf16[512,1024]{1,0:T(8,128)(2,1)S(1)} %pad_maximum_fusion.refs_0_, bf16[128,4096]{1,0:T(8,128)(2,1)} %constant_dynamic-update-slice_fusion.20.refs_1_, bf16[128,4096]{1,0:T(8,128)(2,1)} %collective-permute-done.50.refs_2_, ...), custom_call_target="tpu_custom_call", output_to_operand_aliasing={{0}: (5, {})} | custom-call | flops 1 | bytes 1 | tf_op jit(solution)/shard_map/down_gradient/pallas_call | solution.py:96
  292.3 6.0 %context_parts.2 = (f32[128,4096]{1,0:T(8,128)S(1)}, bf16[128,4096]{1,0:T(8,128)(2,1)S(1)}) custom-call(bf16[2,256,1024]{2,1,0:T(8,128)(2,1)S(1)} %pad_maximum_fusion.1.refs_0_, bf16[4096,1024]{1,0:T(8,128)(2,1)} %bitcast.177, f32[8,128]{1,0:T(8,128)S(1)} %get-tuple-element.344.refs_2_.refs_3_.refs_4_, ...), custom_call_target="tpu_custom_call" | custom-call | flops 1 | bytes 1 | tf_op jit(solution)/shard_map/context_parts/pallas_call | solution.py:96
  300.1 6.0 %context_parts.3 = (f32[128,4096]{1,0:T(8,128)S(1)}, bf16[128,4096]{1,0:T(8,128)(2,1)S(1)}) custom-call(bf16[2,256,1024]{2,1,0:T(8,128)(2,1)S(1)} %pad_maximum_fusion.2.refs_0_, bf16[4096,1024]{1,0:T(8,128)(2,1)} %bitcast.178, bf16[8,128]{1,0:T(8,128)(2,1)S(1)} %slice.529.refs_2_.refs_3_, bf16[8,128]{1,0:T(8,128)(2,1)S(1)} %slice.529.refs_2_.refs_3_), custom_call_target="tpu_custom_call" | custom-call | flops 1 | bytes 1 | tf_op jit(solution)/shard_map/context_parts/pallas_call | solution.py:96
  308.1 3.5 %collective-permute-start.54 = (bf16[64,2048]{1,0:T(8,128)(2,1)S(1)}, bf16[64,2048]{1,0:T(8,128)(2,1)S(1)}, u32[]{:S(2)}, u32[]{:S(2)}) collective-permute-start(bf16[64,2048]{1,0:T(8,128)(2,1)S(1)} %get-tuple-element.410), channel_id=1, source_target_pairs={{0,2},{1,3},{2,0},{3,1},{4,6},{5,7},{6,4},{7,5},{8,10},{9,11},{10,... | collective-permute-start | bytes 786440 | tf_op jit(solution)/shard_map/ppermute | solution.py:15
  314.7 4.0 %collective-permute-done.54 = bf16[64,2048]{1,0:T(8,128)(2,1)S(1)} collective-permute-done((bf16[64,2048]{1,0:T(8,128)(2,1)S(1)}, bf16[64,2048]{1,0:T(8,128)(2,1)S(1)}, u32[]{:S(2)}, u32[]{:S(2)}) %collective-permute-start.54) | collective-permute-done | bytes 262176 | tf_op jit(solution)/shard_map/ppermute | solution.py:15
  328.4 7.8 %down_gradient.5 = (bf16[4096,1024]{1,0:T(8,128)(2,1)}, f32[8,128]{1,0:T(8,128)}) custom-call(bf16[512,1024]{1,0:T(8,128)(2,1)S(1)} %convolution_convert_fusion.refs_0_, bf16[512,4096]{1,0:T(8,128)(2,1)S(1)} %copy-done.7, bf16[8,128]{1,0:T(8,128)(2,1)S(1)} %slice.530.refs_2_, bf16[8,128]{1,0:T(8,128)(2,1)S(1)} %slice.592.refs_3_, ...), custom_call_target="tpu_custom_call" | custom-call | flops 1 | bytes 1 | tf_op jit(solution)/shard_map/down_gradient/pallas_call | solution.py:96
  (343 shorter events, 106.5 us)
Async XLA Ops:
  7.2 285.1 %all-gather.2.cloned.1.call-start = ((), (), s32[]{:S(2)}) async-start(), calls=%async_computation | async-start | bytes 4718592 | tf_op jit(solution)/shard_map/all_gather | solution.py:540
  24.6 18.0 %collective-permute-start.2 = (bf16[64,4096]{1,0:T(8,128)(2,1)S(1)}, bf16[64,4096]{1,0:T(8,128)(2,1)S(1)}, u32[]{:S(2)}, u32[]{:S(2)}) collective-permute-start(bf16[64,4096]{1,0:T(8,128)(2,1)S(1)} %get-tuple-element.404), channel_id=1, source_target_pairs={{0,2},{1,3},{2,0},{3,1},{4,6},{5,7},{6,4},{7,5},{8,10},{9,11},{10,... | collective-permute-start | bytes 1572872 | tf_op jit(solution)/shard_map/ppermute | solution.py:15
  27.6 24.8 %collective-permute-start.3 = (bf16[64,4096]{1,0:T(8,128)(2,1)S(1)}, bf16[64,4096]{1,0:T(8,128)(2,1)S(1)}, u32[]{:S(2)}, u32[]{:S(2)}) collective-permute-start(bf16[64,4096]{1,0:T(8,128)(2,1)S(1)} %get-tuple-element.403), channel_id=1, source_target_pairs={{0,4},{1,5},{2,6},{3,7},{4,0},{5,1},{6,2},{7,3},{8,12},{9,13},{10,... | collective-permute-start | bytes 1572872 | tf_op jit(solution)/shard_map/ppermute | solution.py:15
  29.2 27.0 %collective-permute-start.6 = (bf16[1,256,1024]{1,2,0:T(8,128)(2,1)S(1)}, bf16[1,256,1024]{1,2,0:T(8,128)(2,1)S(1)}, u32[]{:S(2)}, u32[]{:S(2)}) collective-permute-start(bf16[1,256,1024]{1,2,0:T(8,128)(2,1)S(1)} %bitcast.187), channel_id=1, source_target_pairs={{0,8},{1,9},{2,10},{3,11},{4,12},{5,13},{6,14},{7,15},{8,0},{9,1},... | collective-permute-start | bytes 1572872 | tf_op jit(solution)/shard_map/ppermute | solution.py:15
  42.6 23.0 %collective-permute-start.1 = (bf16[2,128,4096]{2,1,0:T(8,128)(2,1)S(1)}, bf16[2,128,4096]{2,1,0:T(8,128)(2,1)S(1)}, u32[]{:S(2)}, u32[]{:S(2)}) collective-permute-start(bf16[2,128,4096]{2,1,0:T(8,128)(2,1)S(1)} %get-tuple-element.199), channel_id=1, source_target_pairs={{0,1},{1,0},{2,3},{3,2},{4,5},{5,4},{6,7},{7,6},{8,9},{9,8},{10,11... | collective-permute-start | bytes 6291464 | tf_op jit(solution)/shard_map/ppermute | solution.py:15
  53.1 25.1 %collective-permute-start.9 = (bf16[1,256,1024]{2,1,0:T(8,128)(2,1)S(1)}, bf16[1,256,1024]{2,1,0:T(8,128)(2,1)S(1)}, u32[]{:S(2)}, u32[]{:S(2)}) collective-permute-start(bf16[1,256,1024]{2,1,0:T(8,128)(2,1)S(1)} %bitcast.156), channel_id=1, source_target_pairs={{0,8},{1,9},{2,10},{3,11},{4,12},{5,13},{6,14},{7,15},{8,0},{9,1},... | collective-permute-start | bytes 1572872 | tf_op jit(solution)/shard_map/ppermute | solution.py:15
  67.3 22.1 %collective-permute-start.7 = (bf16[64,4096]{1,0:T(8,128)(2,1)}, bf16[64,4096]{1,0:T(8,128)(2,1)}, u32[]{:S(2)}, u32[]{:S(2)}) collective-permute-start(bf16[64,4096]{1,0:T(8,128)(2,1)} %get-tuple-element.400), channel_id=1, source_target_pairs={{0,2},{1,3},{2,0},{3,1},{4,6},{5,7},{6,4},{7,5},{8,10},{9,11},{10,... | collective-permute-start | bytes 1572872 | tf_op jit(solution)/shard_map/ppermute | solution.py:15
  67.3 22.1 %collective-permute-start.8 = (bf16[64,4096]{1,0:T(8,128)(2,1)}, bf16[64,4096]{1,0:T(8,128)(2,1)}, u32[]{:S(2)}, u32[]{:S(2)}) collective-permute-start(bf16[64,4096]{1,0:T(8,128)(2,1)} %get-tuple-element.399), channel_id=1, source_target_pairs={{0,4},{1,5},{2,6},{3,7},{4,0},{5,1},{6,2},{7,3},{8,12},{9,13},{10,... | collective-permute-start | bytes 1572872 | tf_op jit(solution)/shard_map/ppermute | solution.py:15
  67.5 24.3 %collective-permute-start.12 = (bf16[32,4096]{1,0:T(8,128)(2,1)S(1)}, bf16[32,4096]{1,0:T(8,128)(2,1)S(1)}, u32[]{:S(2)}, u32[]{:S(2)}) collective-permute-start(bf16[32,4096]{1,0:T(8,128)(2,1)S(1)} %get-tuple-element.227), channel_id=1, source_target_pairs={{0,4},{1,5},{2,6},{3,7},{4,0},{5,1},{6,2},{7,3},{8,12},{9,13},{10,... | collective-permute-start | bytes 786440 | tf_op jit(solution)/shard_map/ppermute | solution.py:15
  69.6 22.2 %collective-permute-start.13 = (bf16[32,4096]{1,0:T(8,128)(2,1)S(1)}, bf16[32,4096]{1,0:T(8,128)(2,1)S(1)}, u32[]{:S(2)}, u32[]{:S(2)}) collective-permute-start(bf16[32,4096]{1,0:T(8,128)(2,1)S(1)} %get-tuple-element.238), channel_id=1, source_target_pairs={{0,2},{1,3},{2,0},{3,1},{4,6},{5,7},{6,4},{7,5},{8,10},{9,11},{10,... | collective-permute-start | bytes 786440 | tf_op jit(solution)/shard_map/ppermute | solution.py:15
  94.5 23.5 %collective-permute-start.18 = (bf16[64,4096]{1,0:T(8,128)(2,1)S(1)}, bf16[64,4096]{1,0:T(8,128)(2,1)S(1)}, u32[]{:S(2)}, u32[]{:S(2)}) collective-permute-start(bf16[64,4096]{1,0:T(8,128)(2,1)S(1)} %constant_dynamic-update-slice_fusion.2), channel_id=1, source_target_pairs={{0,4},{1,5},{2,6},{3,7},{4,0},{5,1},{6,2},{7,3},{8,12},{9,13},{10,... | collective-permute-start | bytes 1572872 | tf_op jit(solution)/shard_map/ppermute | solution.py:15
  94.6 24.1 %collective-permute-start.17 = (bf16[64,4096]{1,0:T(8,128)(2,1)S(1)}, bf16[64,4096]{1,0:T(8,128)(2,1)S(1)}, u32[]{:S(2)}, u32[]{:S(2)}) collective-permute-start(bf16[64,4096]{1,0:T(8,128)(2,1)S(1)} %constant_dynamic-update-slice_fusion.refs_0_.refs_1_), channel_id=1, source_target_pairs={{0,2},{1,3},{2,0},{3,1},{4,6},{5,7},{6,4},{7,5},{8,10},{9,11},{10,... | collective-permute-start | bytes 1572872 | tf_op jit(solution)/shard_map/ppermute | solution.py:15
  105.0 17.1 %collective-permute-start.15 = (bf16[64,4096]{1,0:T(8,128)(2,1)S(1)}, bf16[64,4096]{1,0:T(8,128)(2,1)S(1)}, u32[]{:S(2)}, u32[]{:S(2)}) collective-permute-start(bf16[64,4096]{1,0:T(8,128)(2,1)S(1)} %get-tuple-element.396), channel_id=1, source_target_pairs={{0,2},{1,3},{2,0},{3,1},{4,6},{5,7},{6,4},{7,5},{8,10},{9,11},{10,... | collective-permute-start | bytes 1572872 | tf_op jit(solution)/shard_map/ppermute | solution.py:15
  107.0 15.1 %collective-permute-start.16 = (bf16[64,4096]{1,0:T(8,128)(2,1)}, bf16[64,4096]{1,0:T(8,128)(2,1)S(1)}, u32[]{:S(2)}, u32[]{:S(2)}) collective-permute-start(bf16[64,4096]{1,0:T(8,128)(2,1)} %get-tuple-element.395), channel_id=1, source_target_pairs={{0,4},{1,5},{2,6},{3,7},{4,0},{5,1},{6,2},{7,3},{8,12},{9,13},{10,... | collective-permute-start | bytes 1572872 | tf_op jit(solution)/shard_map/ppermute | solution.py:15
  118.8 17.2 %collective-permute-start.25 = (bf16[2,128,4096]{2,1,0:T(8,128)(2,1)S(1)}, bf16[2,128,4096]{2,1,0:T(8,128)(2,1)}, u32[]{:S(2)}, u32[]{:S(2)}) collective-permute-start(bf16[2,128,4096]{2,1,0:T(8,128)(2,1)S(1)} %get-tuple-element.244), channel_id=1, source_target_pairs={{0,1},{1,0},{2,3},{3,2},{4,5},{5,4},{6,7},{7,6},{8,9},{9,8},{10,11... | collective-permute-start | bytes 6291464 | tf_op jit(solution)/shard_map/ppermute | solution.py:15
  137.4 16.1 %collective-permute-start.28 = (bf16[64,4096]{1,0:T(8,128)(2,1)S(1)}, bf16[64,4096]{1,0:T(8,128)(2,1)S(1)}, u32[]{:S(2)}, u32[]{:S(2)}) collective-permute-start(bf16[64,4096]{1,0:T(8,128)(2,1)S(1)} %get-tuple-element.392), channel_id=1, source_target_pairs={{0,2},{1,3},{2,0},{3,1},{4,6},{5,7},{6,4},{7,5},{8,10},{9,11},{10,... | collective-permute-start | bytes 1572872 | tf_op jit(solution)/shard_map/ppermute | solution.py:15
  138.9 16.6 %collective-permute-start.29 = (bf16[64,4096]{1,0:T(8,128)(2,1)S(1)}, bf16[64,4096]{1,0:T(8,128)(2,1)S(1)}, u32[]{:S(2)}, u32[]{:S(2)}) collective-permute-start(bf16[64,4096]{1,0:T(8,128)(2,1)S(1)} %get-tuple-element.391), channel_id=1, source_target_pairs={{0,4},{1,5},{2,6},{3,7},{4,0},{5,1},{6,2},{7,3},{8,12},{9,13},{10,... | collective-permute-start | bytes 1572872 | tf_op jit(solution)/shard_map/ppermute | solution.py:15
  144.6 28.4 %collective-permute-start.27 = (bf16[64,4096]{1,0:T(8,128)(2,1)S(1)}, bf16[64,4096]{1,0:T(8,128)(2,1)S(1)}, u32[]{:S(2)}, u32[]{:S(2)}) collective-permute-start(bf16[64,4096]{1,0:T(8,128)(2,1)S(1)} %constant_dynamic-update-slice_fusion.6), channel_id=1, source_target_pairs={{0,4},{1,5},{2,6},{3,7},{4,0},{5,1},{6,2},{7,3},{8,12},{9,13},{10,... | collective-permute-start | bytes 1572872 | tf_op jit(solution)/shard_map/ppermute | solution.py:15
  157.5 15.5 %collective-permute-start.26 = (bf16[64,4096]{1,0:T(8,128)(2,1)S(1)}, bf16[64,4096]{1,0:T(8,128)(2,1)S(1)}, u32[]{:S(2)}, u32[]{:S(2)}) collective-permute-start(bf16[64,4096]{1,0:T(8,128)(2,1)S(1)} %constant_dynamic-update-slice_fusion.4.refs_0_.refs_5_), channel_id=1, source_target_pairs={{0,2},{1,3},{2,0},{3,1},{4,6},{5,7},{6,4},{7,5},{8,10},{9,11},{10,... | collective-permute-start | bytes 1572872 | tf_op jit(solution)/shard_map/ppermute | solution.py:15
  178.8 15.0 %collective-permute-start.39 = (bf16[64,4096]{1,0:T(8,128)(2,1)S(1)}, bf16[64,4096]{1,0:T(8,128)(2,1)S(1)}, u32[]{:S(2)}, u32[]{:S(2)}) collective-permute-start(bf16[64,4096]{1,0:T(8,128)(2,1)S(1)} %constant_dynamic-update-slice_fusion.10), channel_id=1, source_target_pairs={{0,4},{1,5},{2,6},{3,7},{4,0},{5,1},{6,2},{7,3},{8,12},{9,13},{10,... | collective-permute-start | bytes 1572872 | tf_op jit(solution)/shard_map/ppermute | solution.py:15
  193.8 40.5 %collective-permute-start.46 = (bf16[128,4096]{1,0:T(8,128)(2,1)}, bf16[128,4096]{1,0:T(8,128)(2,1)}, u32[]{:S(2)}, u32[]{:S(2)}) collective-permute-start(bf16[128,4096]{1,0:T(8,128)(2,1)} %constant_dynamic-update-slice_fusion.16.refs_1_), channel_id=1, source_target_pairs={{0,1},{1,0},{2,3},{3,2},{4,5},{5,4},{6,7},{7,6},{8,9},{9,8},{10,11... | collective-permute-start | bytes 3145736 | tf_op jit(solution)/shard_map/ppermute | solution.py:15
  200.1 18.7 %collective-permute-start.41 = (bf16[64,4096]{1,0:T(8,128)(2,1)S(1)}, bf16[64,4096]{1,0:T(8,128)(2,1)S(1)}, u32[]{:S(2)}, u32[]{:S(2)}) collective-permute-start(bf16[64,4096]{1,0:T(8,128)(2,1)S(1)} %constant_dynamic-update-slice_fusion.14), channel_id=1, source_target_pairs={{0,4},{1,5},{2,6},{3,7},{4,0},{5,1},{6,2},{7,3},{8,12},{9,13},{10,... | collective-permute-start | bytes 1572872 | tf_op jit(solution)/shard_map/ppermute | solution.py:15
  202.7 20.9 %collective-permute-start.40 = (bf16[64,4096]{1,0:T(8,128)(2,1)S(1)}, bf16[64,4096]{1,0:T(8,128)(2,1)S(1)}, u32[]{:S(2)}, u32[]{:S(2)}) collective-permute-start(bf16[64,4096]{1,0:T(8,128)(2,1)S(1)} %constant_dynamic-update-slice_fusion.12.refs_0_.refs_1_), channel_id=1, source_target_pairs={{0,2},{1,3},{2,0},{3,1},{4,6},{5,7},{6,4},{7,5},{8,10},{9,11},{10,... | collective-permute-start | bytes 1572872 | tf_op jit(solution)/shard_map/ppermute | solution.py:15
  214.2 20.1 %collective-permute-start.47 = (bf16[128,4096]{1,0:T(8,128)(2,1)S(1)}, bf16[128,4096]{1,0:T(8,128)(2,1)S(1)}, u32[]{:S(2)}, u32[]{:S(2)}) collective-permute-start(bf16[128,4096]{1,0:T(8,128)(2,1)S(1)} %constant_dynamic-update-slice_fusion.18.refs_3_), channel_id=1, source_target_pairs={{0,1},{1,0},{2,3},{3,2},{4,5},{5,4},{6,7},{7,6},{8,9},{9,8},{10,11... | collective-permute-start | bytes 3145736 | tf_op jit(solution)/shard_map/ppermute | solution.py:15
  214.5 38.7 %collective-permute-start.48 = (bf16[256,1024]{1,0:T(8,128)(2,1)S(1)}, bf16[256,1024]{1,0:T(8,128)(2,1)S(1)}, u32[]{:S(2)}, u32[]{:S(2)}) collective-permute-start(bf16[256,1024]{1,0:T(8,128)(2,1)S(1)} %convert_element_type.512), channel_id=1, source_target_pairs={{0,8},{1,9},{2,10},{3,11},{4,12},{5,13},{6,14},{7,15},{8,0},{9,1},... | collective-permute-start | bytes 1572872 | tf_op jit(solution)/shard_map/ppermute | solution.py:15
  223.6 20.7 %collective-permute-start.44 = (bf16[64,4096]{1,0:T(8,128)(2,1)S(1)}, bf16[64,4096]{1,0:T(8,128)(2,1)S(1)}, u32[]{:S(2)}, u32[]{:S(2)}) collective-permute-start(bf16[64,4096]{1,0:T(8,128)(2,1)S(1)} %constant_dynamic-update-slice_fusion.12.refs_0_.refs_1_), channel_id=1, source_target_pairs={{0,1},{1,0},{2,3},{3,2},{4,5},{5,4},{6,7},{7,6},{8,9},{9,8},{10,11... | collective-permute-start | bytes 1572872 | tf_op jit(solution)/shard_map/ppermute | solution.py:15
  223.6 20.7 %collective-permute-start.45 = (bf16[64,4096]{1,0:T(8,128)(2,1)S(1)}, bf16[64,4096]{1,0:T(8,128)(2,1)S(1)}, u32[]{:S(2)}, u32[]{:S(2)}) collective-permute-start(bf16[64,4096]{1,0:T(8,128)(2,1)S(1)} %collective-permute-done.40.refs_1_.refs_2_), channel_id=1, source_target_pairs={{0,1},{1,0},{2,3},{3,2},{4,5},{5,4},{6,7},{7,6},{8,9},{9,8},{10,11... | collective-permute-start | bytes 1572872 | tf_op jit(solution)/shard_map/ppermute | solution.py:15
  256.1 25.0 %collective-permute-start.51 = (bf16[128,4096]{1,0:T(8,128)(2,1)}, bf16[128,4096]{1,0:T(8,128)(2,1)}, u32[]{:S(2)}, u32[]{:S(2)}) collective-permute-start(bf16[128,4096]{1,0:T(8,128)(2,1)} %constant_dynamic-update-slice_fusion.22.refs_3_), channel_id=1, source_target_pairs={{0,1},{1,0},{2,3},{3,2},{4,5},{5,4},{6,7},{7,6},{8,9},{9,8},{10,11... | collective-permute-start | bytes 3145736 | tf_op jit(solution)/shard_map/ppermute | solution.py:15
  257.7 23.4 %collective-permute-start.50 = (bf16[128,4096]{1,0:T(8,128)(2,1)}, bf16[128,4096]{1,0:T(8,128)(2,1)}, u32[]{:S(2)}, u32[]{:S(2)}) collective-permute-start(bf16[128,4096]{1,0:T(8,128)(2,1)} %constant_dynamic-update-slice_fusion.20.refs_1_), channel_id=1, source_target_pairs={{0,1},{1,0},{2,3},{3,2},{4,5},{5,4},{6,7},{7,6},{8,9},{9,8},{10,11... | collective-permute-start | bytes 3145736 | tf_op jit(solution)/shard_map/ppermute | solution.py:15
  259.0 21.1 %collective-permute-start.49 = (bf16[1,128,1024]{2,1,0:T(8,128)(2,1)}, bf16[1,128,1024]{2,1,0:T(8,128)(2,1)}, u32[]{:S(2)}, u32[]{:S(2)}) collective-permute-start(bf16[1,128,1024]{2,1,0:T(8,128)(2,1)} %get-tuple-element.417), channel_id=1, source_target_pairs={{0,8},{1,9},{2,10},{3,11},{4,12},{5,13},{6,14},{7,15},{8,0},{9,1},... | collective-permute-start | bytes 786440 | tf_op jit(solution)/shard_map/ppermute | solution.py:15
  263.1 35.2 %collective-permute-start.53 = (bf16[1,128,1024]{2,1,0:T(8,128)(2,1)S(1)}, bf16[1,128,1024]{2,1,0:T(8,128)(2,1)}, u32[]{:S(2)}, u32[]{:S(2)}) collective-permute-start(bf16[1,128,1024]{2,1,0:T(8,128)(2,1)S(1)} %get-tuple-element.418), channel_id=1, source_target_pairs={{0,8},{1,9},{2,10},{3,11},{4,12},{5,13},{6,14},{7,15},{8,0},{9,1},... | collective-permute-start | bytes 786440 | tf_op jit(solution)/shard_map/ppermute | solution.py:15
  320.9 15.3 %collective-permute-start.56 = (bf16[32,2048]{1,0:T(8,128)(2,1)S(1)}, bf16[32,2048]{1,0:T(8,128)(2,1)S(1)}, u32[]{:S(2)}, u32[]{:S(2)}) collective-permute-start(bf16[32,2048]{1,0:T(8,128)(2,1)S(1)} %get-tuple-element.408), channel_id=1, source_target_pairs={{0,4},{1,5},{2,6},{3,7},{4,0},{5,1},{6,2},{7,3},{8,12},{9,13},{10,... | collective-permute-start | bytes 393224 | tf_op jit(solution)/shard_map/ppermute | solution.py:15
  (91 other events, 987.6 us)
Sparse Core Ops, SparseCore 0:
  198.2 46.0 all-gather.1
